TPU v7x, 32 devices: a whole 2x2x4 slice. The times are simulated.
32 devices in a mesh: groups: 2 (over y), gx: 16 (over z, x, core).
Axes of the slice: x: 2, y: 2, z: 4, core: 2. Of those that a mesh axis runs over, the one named last changes fastest.
Arguments:
- tokens: bfloat16 [64, 7168], P(('groups', 'gx')), parts along dimension 0, may hold values from -6 to 6
- route_ids: int32 [64, 2], P('groups'), parts along dimension 0, may hold values from 0 to 7, all different within a row; in each aligned block of 32 rows (0 to 31, 32 to 63, ...) at most 32 rows name the same one
- route_gates: float32 [64, 2], P('groups'), parts along dimension 0, may hold values from 0.2 to 1
- dense_gate: bfloat16 [7168, 4864], P(None, 'gx'), may hold values from -0.0625 to 0.0625
- dense_up: bfloat16 [7168, 4864], P(None, 'gx'), may hold values from -0.0625 to 0.0625
- dense_down: bfloat16 [4864, 7168], P(None, 'gx'), may hold values from -0.078125 to 0.078125
- expert_gate: bfloat16 [7168, 32768], P(None, 'gx'), may hold values from -0.0625 to 0.0625
- expert_up: bfloat16 [7168, 32768], P(None, 'gx'), may hold values from -0.0625 to 0.0625
- expert_down: bfloat16 [32768, 7168], P('gx'), may hold values from -0.09375 to 0.09375
Outputs:
- layer_out: bfloat16 [64, 7168], P(('groups', 'gx')), parts along dimension 0
There are 2 independent parts, one for each index of `groups`. A program takes and returns all parts, laid end to end along the dimension named above; an argument that names none is the same for every part. Nothing has to cross between parts.
Inputs may be any that keep to these rules, and one draw needn't show every extreme that they name: `route_ids`: the 2 experts of a token differ; each expert is named by at most 32 tokens, a bound that some block reaches.
All inputs are finite; a program needn't handle non-finite values.
Results may differ from a plain program's by a relative error of at most 0.0042.
Values may be sent and summed in bfloat16 or wider, within the bound.
No kernel may reach another device: no remote copies, remote signals or barrier semaphores. Data moves between devices by JAX's collectives and lax.ppermute only.
A program may use at most 192 MiB of HBM per device.

v0:
```python
import jax
import jax.numpy as jnp
from jax import lax
from jax.sharding import PartitionSpec as P

EH = 4096


def swiglu(row_block, w_gate, w_up, w_down):
    gate = jnp.dot(row_block, w_gate, preferred_element_type=jnp.float32)
    upward = jnp.dot(row_block, w_up, preferred_element_type=jnp.float32)
    hidden = (jax.nn.silu(gate) * upward).astype(jnp.bfloat16)
    return jnp.dot(hidden, w_down, preferred_element_type=jnp.float32)


def per_device(
    tokens,
    route_ids,
    route_gates,
    dense_gate,
    dense_up,
    dense_down,
    expert_gate,
    expert_up,
    expert_down,
):
    gathered = lax.all_gather(tokens, "gx", axis=0, tiled=True)
    total_rows = gathered.shape[0]
    model_width = gathered.shape[1]
    own_index = lax.axis_index("gx")
    gate = jnp.dot(gathered, dense_gate, preferred_element_type=jnp.float32)
    upward = jnp.dot(gathered, dense_up, preferred_element_type=jnp.float32)
    dense_hidden = (jax.nn.silu(gate) * upward).astype(jnp.bfloat16)
    dense_part = jnp.dot(
        lax.all_gather(dense_hidden, "gx", axis=1, tiled=True),
        dense_down,
        preferred_element_type=jnp.float32,
    )
    slice_width = expert_gate.shape[1]
    expert = own_index * slice_width // EH
    flat_ids = route_ids.reshape(-1)
    flat_gates = route_gates.reshape(-1)
    matches = flat_ids == expert
    position = jnp.cumsum(matches.astype(jnp.int32)) - 1
    target = jnp.where(matches, position, total_rows)
    source_row = jnp.arange(flat_ids.shape[0], dtype=jnp.int32) // route_ids.shape[1]
    slot_rows = jnp.zeros((total_rows,), jnp.int32).at[target].set(source_row, mode="drop")
    slot_weights = jnp.zeros((total_rows,), jnp.float32).at[target].set(flat_gates, mode="drop")
    picked = gathered[slot_rows]
    slot_out = swiglu(picked, expert_gate, expert_up, expert_down)
    weighted = slot_weights[:, None] * slot_out
    expert_term = jnp.zeros((total_rows, model_width), jnp.float32).at[slot_rows].add(weighted)
    moe_rows = lax.psum_scatter(expert_term, "gx", scatter_dimension=0, tiled=True)
    dense_rows = lax.all_to_all(dense_part, "gx", split_axis=0, concat_axis=1, tiled=True)
    result = tokens.astype(jnp.float32) + dense_rows + moe_rows
    return result.astype(jnp.bfloat16)


def solution(mesh):
    in_specs = (
        P(("groups", "gx"), None),
        P("groups", None),
        P("groups", None),
        P(None, "gx"),
        P(None, "gx"),
        P(None, "gx"),
        P(None, "gx"),
        P(None, "gx"),
        P("gx", None),
    )
    out_specs = P(("groups", "gx"), None)
    return jax.shard_map(
        per_device, mesh=mesh, in_specs=in_specs, out_specs=out_specs, check_vma=False
    )
```

profile of v0, /device:TPU:0, one launch (start us, length us, event | category | flops | bytes accessed | tf_op | source)
XLA Modules:
  0.0 170.1 jit_solution(18126757773993111765)
XLA Ops:
  6.5 0.7 broadcast_compare_fusion
  7.2 0.1 copy.23
  7.3 0.1 eq.22
  7.5 0.1 copy.25
  7.6 0.8 copy.26
  8.3 0.1 reshape.68
  8.4 0.1 copy.24
  8.5 0.1 reduce-window.4
  8.6 0.1 fusion.12
  8.7 0.8 scatter_custom_fusion
  9.6 24.6 %all-gather = bf16[16,2,7168]{2,1,0:T(2,128)(2,1)S(1)} all-gather(bf16[1,2,7168]{2,1,0:T(2,128)(2,1)} %bitcast.23), channel_id=1, replica_groups=mesh['groups'=2,'gx'=16] {'gx'}, dimensions={0}, use_global_device_ids=true | all-gather | bytes 487424 | tf_op jit(solution)/shard_map/all_gather | solution.py:27
  34.1 0.2 reshape.83
  34.3 0.8 scatter_custom_fusion.1
  35.1 0.8 gather_fusion
  35.9 12.0 %fusion.20 = f32[32,2048]{1,0:T(8,128)S(1)} fusion(bf16[32,7168]{1,0:T(8,128)(2,1)S(1)} %gather_fusion, bf16[7168,2048]{1,0:T(8,128)(2,1)} %param.15), kind=kOutput, calls=%fused_computation.36 | convolution fusion | flops 939524096 | bytes 30081024 | tf_op jit(solution)/shard_map/dot_general | solution.py:10
  47.9 0.0 copy-start
  47.9 20.8 %convolution_multiply_fusion = f32[32,7168]{1,0:T(8,128)S(1)} fusion(bf16[2048,7168]{1,0:T(8,128)(2,1)} %param.17, bf16[32,7168]{1,0:T(8,128)(2,1)S(1)} %gather_fusion, bf16[7168,2048]{1,0:T(8,128)(2,1)} %param.16, f32[32]{0:T(128)S(1)} %scatter_custom_fusion.1, f32[32,2048]{1,0:T(8,128)S(1)} %fusion.20), kind=kOutput, calls=%fused_computation.4 | convolution fusion | flops 1879670784 | bytes 60358784 | tf_op jit(solution)/shard_map/dot_general | solution.py:13
  68.8 2.6 %scatter_custom_fusion.2 = f32[32,7168]{1,0:T(8,128)} fusion(s32[32]{0:T(128)S(1)} %compare_select_fusion.1, f32[32,7168]{1,0:T(8,128)S(1)} %convolution_multiply_fusion, f32[]{:T(128)} %constant.45.clone.1), kind=kCustom, calls=%fused_computation.10 | custom fusion | flops 229376 | bytes 917508 | tf_op jit(solution)/shard_map/scatter-add | solution.py:52
  71.4 0.0 all-reduce.3.cloned.1.call-update
  71.4 3.6 %fusion.18 = f32[32,304]{1,0:T(8,128)S(1)} fusion(bf16[32,7168]{1,0:T(8,128)(2,1)S(1)} %reshape.83, bf16[7168,304]{0,1:T(8,128)(2,1)} %param.12), kind=kOutput, calls=%fused_computation.34 | convolution fusion | flops 139460608 | bytes 4855808 | tf_op jit(solution)/shard_map/dot_general | solution.py:31
  75.0 3.6 %fusion.2 = bf16[1,304,32]{1,2,0:T(8,128)(2,1)S(1)} fusion(bf16[32,7168]{1,0:T(8,128)(2,1)S(1)} %reshape.83, bf16[7168,304]{0,1:T(8,128)(2,1)} %param.13, f32[32,304]{1,0:T(8,128)S(1)} %fusion.18), kind=kOutput, calls=%fused_computation.9 | convolution fusion | flops 139518976 | bytes 4875264 | tf_op jit(solution)/shard_map/dot_general | solution.py:32
  78.6 18.9 %all-gather.1 = bf16[16,304,32]{1,2,0:T(8,128)(2,1)S(1)} all-gather(bf16[1,304,32]{1,2,0:T(8,128)(2,1)S(1)} %fusion.2), channel_id=1, replica_groups=mesh['groups'=2,'gx'=16] {'gx'}, dimensions={0}, use_global_device_ids=true | all-gather | bytes 330752 | tf_op jit(solution)/shard_map/all_gather | solution.py:35
  97.5 0.1 copy.21
  97.6 0.4 reshape.85
  98.0 3.5 %fusion.19 = f32[32,448]{1,0:T(8,128)S(1)} fusion(bf16[4864,32]{0,1:T(8,128)(2,1)S(1)} %reshape.85, bf16[4864,448]{0,1:T(8,128)(2,1)} %param.14), kind=kOutput, calls=%fused_computation.35 | convolution fusion | flops 139460608 | bytes 4726784 | tf_op jit(solution)/shard_map/dot_general | solution.py:34
  101.5 0.7 all_to_all.14
  102.2 3.5 %all-to-all-start = ((f32[16,2,448]{2,1,0:T(2,128)}), f32[16,2,448]{2,1,0:T(2,128)S(1)}, u32[]{:S(2)}, u32[]{:S(2)}) async-start(f32[16,2,448]{2,1,0:T(2,128)} %all_to_all.14), calls=%async_computation | async-start | bytes 131072 | tf_op jit(solution)/shard_map/all_to_all | solution.py:54
  105.7 0.6 dynamic-slice
  107.0 5.7 %all-to-all-done = f32[16,2,448]{2,1,0:T(2,128)S(1)} async-done(((f32[16,2,448]{2,1,0:T(2,128)}), f32[16,2,448]{2,1,0:T(2,128)S(1)}, u32[]{:S(2)}, u32[]{:S(2)}) %all-to-all-start) | async-done | bytes 57376 | tf_op jit(solution)/shard_map/all_to_all | solution.py:54
  112.7 0.1 all_to_all.17
  112.8 48.8 %all-reduce.3.cloned.1.call-done = f32[32,7168]{1,0:T(8,128)} async-done(((f32[32,7168]{1,0:T(8,128)}), f32[32,7168]{1,0:T(8,128)}) %all-reduce.3.cloned.1.call-update) | async-done | bytes 917520
  161.6 1.6 fusion.11
  (9 shorter events, 0.0 us)
Async XLA Ops:
  6.5 155.1 %all-reduce.3.cloned.1.call-start = ((), (), s32[]{:S(2)}) async-start(), calls=%async_computation.1 | async-start | bytes 1835008
  47.9 57.8 %copy-start.1 = (u32[32]{0:T(128)S(1)}, u32[32]{0:T(128)}, u32[]{:S(2)}) copy-start(u32[32]{0:T(128)} %constant.57) | copy-start | bytes 388
  47.9 113.7 %copy-start = (bf16[2,7168]{1,0:T(2,128)(2,1)S(1)}, bf16[2,7168]{1,0:T(2,128)(2,1)}, u32[]{:S(2)}) copy-start(bf16[2,7168]{1,0:T(2,128)(2,1)} %param.9) | copy-start | bytes 86020
  102.2 10.5 %all-to-all-start = ((f32[16,2,448]{2,1,0:T(2,128)}), f32[16,2,448]{2,1,0:T(2,128)S(1)}, u32[]{:S(2)}, u32[]{:S(2)}) async-start(f32[16,2,448]{2,1,0:T(2,128)} %all_to_all.14), calls=%async_computation | async-start | bytes 131072 | tf_op jit(solution)/shard_map/all_to_all | solution.py:54
Sparse Core Ops, SparseCore 0:
  71.5 90.0 all-reduce.2
where the time goes:
time: 170 us
  waiting for transfers between devices  54.6 us (32%)
  matrix products  43.5 us (26%)
  blocking collectives  43.4 us (26%)
  between operations  14.2 us (8%)
  local copies, waits for them, and re-layouts  5.76 us (3%)
  other arithmetic  5.13 us (3%)
  starting transfers between devices  3.5 us (2%)
    unnamed x2, waiting for transfers between devices  48.8 us
    all_gather x1, blocking collectives, per_device(): gathered = lax.all_gather(tokens, 'gx', axis=0, tiled=True)  24.6 us
    dot_general x1, matrix products, swiglu(): return jnp.dot(hidden, w_down, preferred_element_type=jnp.float32)  20.8 us
    all_gather x1, blocking collectives, per_device(): lax.all_gather(dense_hidden, 'gx', axis=1, tiled=True)  18.9 us
    dot_general x1, matrix products, swiglu(): gate = jnp.dot(row_block, w_gate, preferred_element_type=jnp.float32)  12 us
    all_to_all x1, waiting for transfers between devices, per_device(): lax.all_to_all(dense_part, 'gx', split_axis=0, concat_axis=1, tiled=True)  5.72 us
    dot_general x1, matrix products, per_device(): upward = jnp.dot(gathered, dense_up, preferred_element_type=jnp.float32)  3.63 us
    dot_general x1, matrix products, per_device(): gate = jnp.dot(gathered, dense_gate, preferred_element_type=jnp.float32)  3.56 us
  transfers between devices with their start and end apart: 2, of which 2 were waited for; matrix products, arithmetic and copies ran while one was open for 7% of the time, Pallas kernels for 0%

commit v1 on v0

v1 whole, which is shorter than its diff:
```python
import jax
import jax.numpy as jnp
from jax import lax
from jax.sharding import PartitionSpec as P

EH = 4096


def exchange(value, bit, size):
    return lax.ppermute(value, "gx", [(i, i ^ bit) for i in range(size)])


def gather_xor(rows, size):
    blocks = rows[None]
    bits = []
    bit = size // 2
    while bit:
        bits.append(bit)
        other = exchange(blocks, bit, size)
        blocks = jnp.concatenate([blocks, other], axis=0)
        bit //= 2
    order = [0]
    for taken in bits:
        order = order + [held ^ taken for held in order]
    return blocks, order


def per_device(
    tokens,
    route_ids,
    route_gates,
    dense_gate,
    dense_up,
    dense_down,
    expert_gate,
    expert_up,
    expert_down,
):
    size = lax.axis_size("gx")
    own = lax.axis_index("gx")
    owned, width = tokens.shape
    total = owned * size
    blocks, order = gather_xor(tokens, size)
    rows = blocks.reshape(total, width)
    owners = own ^ jnp.array(order, jnp.int32)
    row_ids = (owners[:, None] * owned + jnp.arange(owned, dtype=jnp.int32)[None, :]).reshape(-1)

    gate = jnp.dot(rows, dense_gate, preferred_element_type=jnp.float32)
    upward = jnp.dot(rows, dense_up, preferred_element_type=jnp.float32)
    dense_hidden = (jax.nn.silu(gate) * upward).astype(jnp.bfloat16)
    place = (row_ids[None, :] == jnp.arange(total, dtype=jnp.int32)[:, None]).astype(jnp.bfloat16)
    dense_hidden = jnp.dot(place, dense_hidden, preferred_element_type=jnp.float32).astype(jnp.bfloat16)
    sent = jnp.broadcast_to(dense_hidden[None], (size,) + dense_hidden.shape)
    hidden_blocks = lax.all_to_all(sent, "gx", split_axis=0, concat_axis=0, tiled=True)

    expert = own * expert_gate.shape[1] // EH
    weights = jnp.sum(jnp.where(route_ids == expert, route_gates, jnp.zeros_like(route_gates)), axis=1)
    weights = jnp.sum(jnp.where(row_ids[:, None] == jnp.arange(total, dtype=jnp.int32)[None, :], weights[None, :], 0.0), axis=1)

    gate = jnp.dot(rows, expert_gate, preferred_element_type=jnp.float32)
    upward = jnp.dot(rows, expert_up, preferred_element_type=jnp.float32)
    hidden = (jax.nn.silu(gate) * upward).astype(jnp.bfloat16)
    partial = weights[:, None] * jnp.dot(hidden, expert_down, preferred_element_type=jnp.float32)

    all_hidden = hidden_blocks.transpose(1, 0, 2).reshape(total, -1)
    dense_part = jnp.dot(all_hidden, dense_down, preferred_element_type=jnp.float32)
    dense_rows = lax.all_to_all(dense_part, "gx", split_axis=0, concat_axis=1, tiled=True)

    partial = partial.reshape(size, owned, width)
    bit = 1
    while bit < size:
        half = partial.shape[0] // 2
        other = exchange(partial[half:].astype(jnp.bfloat16), bit, size)
        partial = partial[:half] + other.astype(jnp.float32)
        bit *= 2
    result = tokens.astype(jnp.float32) + dense_rows + partial[0]
    return result.astype(jnp.bfloat16)


def solution(mesh):
    in_specs = (
        P(("groups", "gx"), None),
        P("groups", None),
        P("groups", None),
        P(None, "gx"),
        P(None, "gx"),
        P(None, "gx"),
        P(None, "gx"),
        P(None, "gx"),
        P("gx", None),
    )
    out_specs = P(("groups", "gx"), None)
    return jax.shard_map(
        per_device, mesh=mesh, in_specs=in_specs, out_specs=out_specs, check_vma=False
    )
```

time: 170 us -> 98.5 us (0.58)
  blocking collectives: 43.4 us -> 0 us
  waiting for transfers between devices: 54.6 us -> 21.9 us
  starting transfers between devices: 3.5 us -> 22.4 us
  between operations: 14.2 us -> 0.23 us
    unnamed x2 -> x0, waiting for transfers between devices: 48.8 us -> none
    all_gather x2 -> x0, blocking collectives: 43.4 us -> none  [the longest x1 24.6 us: per_device(): gathered = lax.all_gather(tokens, 'gx', axis=0, tiled=True)]
    ppermute x0 -> x8, starting transfers between devices: none -> 13.9 us  [exchange(): return lax.ppermute(value, 'gx', [(i, i ^ bit) for i in range(size)])]
    all_to_all x0 -> x1, waiting for transfers between devices: none -> 10.5 us  [per_device(): lax.all_to_all(sent, 'gx', split_axis=0, concat_axis=0, tiled=True)]
    ppermute x0 -> x8, waiting for transfers between devices: none -> 7.23 us  [exchange(): return lax.ppermute(value, 'gx', [(i, i ^ bit) for i in range(size)])]
    all_to_all x0 -> x1, starting transfers between devices: none -> 4.99 us  [per_device(): lax.all_to_all(sent, 'gx', split_axis=0, concat_axis=0, tiled=True)]
    concatenate x0 -> x3, other arithmetic: none -> 2.82 us  [gather_xor(): blocks = jnp.concatenate([blocks, other], axis=0)]
    scatter-add x1 -> x0, other arithmetic: 2.63 us -> none  [per_device(): jnp.zeros((total_rows, model_width), jnp.float32).at[slot_rows]]
  transfers between devices with their start and end apart: 2 -> 10, of which waited for: 2 -> 5; matrix products, arithmetic and copies ran while one was open for 7% -> 16% of each run, Pallas kernels for 0% -> 0%
where the time goes in v1:
time: 98.5 us; the launch traced here: 97.9 us
  matrix products  43.6 us (44%)
  starting transfers between devices  22.4 us (23%)
  waiting for transfers between devices  21.9 us (22%)
  other arithmetic  5.34 us (5%)
  local copies, waits for them, and re-layouts  4.35 us (4%)
    dot_general x1, matrix products, per_device(): jnp.dot(hidden, expert_down, preferred_element_type=jnp.float32)  20.8 us
    ppermute x8, starting transfers between devices, exchange(): return lax.ppermute(value, 'gx', [(i, i ^ bit) for i in range(size)])  13.9 us
    dot_general x1, matrix products, per_device(): gate = jnp.dot(rows, expert_gate, preferred_element_type=jnp.float32)  12 us
    all_to_all x1, waiting for transfers between devices, per_device(): lax.all_to_all(sent, 'gx', split_axis=0, concat_axis=0, tiled=True)  10.5 us
    ppermute x8, waiting for transfers between devices, exchange(): return lax.ppermute(value, 'gx', [(i, i ^ bit) for i in range(size)])  7.23 us
    all_to_all x1, starting transfers between devices, per_device(): lax.all_to_all(sent, 'gx', split_axis=0, concat_axis=0, tiled=True)  4.99 us
    all_to_all x1, waiting for transfers between devices, per_device(): lax.all_to_all(dense_part, 'gx', split_axis=0, concat_axis=1, tiled=True)  4.23 us
    dot_general x1, matrix products, per_device(): jnp.dot(place, dense_hidden, preferred_element_type=jnp.float32)  3.72 us
  transfers between devices with their start and end apart: 10, of which 5 were waited for; matrix products, arithmetic and copies ran while one was open for 16% of the time, Pallas kernels for 0%

profile of v1, /device:TPU:0, one launch (start us, length us, event | category | flops | bytes accessed | tf_op | source)
XLA Modules:
  0.0 97.9 jit_solution(2658051968495770336)
XLA Ops:
  0.0 4.0 %collective-permute-start = (bf16[1,2,7168]{2,1,0:T(2,128)(2,1)}, bf16[1,2,7168]{2,1,0:T(2,128)(2,1)S(1)}, u32[]{:S(2)}, u32[]{:S(2)}) collective-permute-start(bf16[1,2,7168]{2,1,0:T(2,128)(2,1)} %bitcast.29), channel_id=1, source_target_pairs={{0,8},{1,9},{2,10},{3,11},{4,12},{5,13},{6,14},{7,15},{8,0},{9,1},... | collective-permute-start | bytes 86024 | tf_op jit(solution)/shard_map/ppermute | solution.py:10
  4.0 0.8 constant_dynamic-update-slice_fusion.4
  4.8 0.7 xor_multiply_fusion
  5.7 0.7 fusion.8
  6.4 0.2 select_reduce_fusion
  6.6 0.8 pad_maximum_fusion.2
  7.4 1.6 %collective-permute-start.1 = (bf16[2,2,7168]{2,1,0:T(2,128)(2,1)S(1)}, bf16[2,2,7168]{2,1,0:T(2,128)(2,1)S(1)}, u32[]{:S(2)}, u32[]{:S(2)}) collective-permute-start(bf16[2,2,7168]{2,1,0:T(2,128)(2,1)S(1)} %pad_maximum_fusion.2), channel_id=1, source_target_pairs={{0,4},{1,5},{2,6},{3,7},{4,0},{5,1},{6,2},{7,3},{8,12},{9,13},{10,... | collective-permute-start | bytes 172040 | tf_op jit(solution)/shard_map/ppermute | solution.py:10
  9.1 2.6 %collective-permute-done.1 = bf16[2,2,7168]{2,1,0:T(2,128)(2,1)S(1)} collective-permute-done((bf16[2,2,7168]{2,1,0:T(2,128)(2,1)S(1)}, bf16[2,2,7168]{2,1,0:T(2,128)(2,1)S(1)}, u32[]{:S(2)}, u32[]{:S(2)}) %collective-permute-start.1) | collective-permute-done | bytes 57376 | tf_op jit(solution)/shard_map/ppermute | solution.py:10
  11.7 0.9 pad_maximum_fusion.1
  12.6 1.6 %collective-permute-start.2 = (bf16[4,2,7168]{2,1,0:T(2,128)(2,1)S(1)}, bf16[4,2,7168]{2,1,0:T(2,128)(2,1)S(1)}, u32[]{:S(2)}, u32[]{:S(2)}) collective-permute-start(bf16[4,2,7168]{2,1,0:T(2,128)(2,1)S(1)} %pad_maximum_fusion.1), channel_id=1, source_target_pairs={{0,2},{1,3},{2,0},{3,1},{4,6},{5,7},{6,4},{7,5},{8,10},{9,11},{10,... | collective-permute-start | bytes 344072 | tf_op jit(solution)/shard_map/ppermute | solution.py:10
  14.2 3.2 %collective-permute-done.2 = bf16[4,2,7168]{2,1,0:T(2,128)(2,1)S(1)} collective-permute-done((bf16[4,2,7168]{2,1,0:T(2,128)(2,1)S(1)}, bf16[4,2,7168]{2,1,0:T(2,128)(2,1)S(1)}, u32[]{:S(2)}, u32[]{:S(2)}) %collective-permute-start.2) | collective-permute-done | bytes 114720 | tf_op jit(solution)/shard_map/ppermute | solution.py:10
  17.4 1.1 %pad_maximum_fusion = bf16[8,2,7168]{2,1,0:T(2,128)(2,1)S(1)} fusion(bf16[4,2,7168]{2,1,0:T(2,128)(2,1)S(1)} %collective-permute-done.2, bf16[2,2,7168]{2,1,0:T(2,128)(2,1)S(1)} %collective-permute-done.1, bf16[1,2,7168]{2,1,0:T(2,128)(2,1)S(1)} %collective-permute-done, bf16[1,2,7168]{2,1,0:T(2,128)(2,1)} %bitcast.32), kind=kLoop, calls=%fused_computation.10 | loop fusion | flops 344064 | bytes 458752 | tf_op jit(solution)/shard_map/concatenate | solution.py:20
  18.7 1.4 %collective-permute-done.3 = bf16[8,2,7168]{2,1,0:T(2,128)(2,1)S(1)} collective-permute-done((bf16[8,2,7168]{2,1,0:T(2,128)(2,1)S(1)}, bf16[8,2,7168]{2,1,0:T(2,128)(2,1)S(1)}, u32[]{:S(2)}, u32[]{:S(2)}) %collective-permute-start.3) | collective-permute-done | bytes 229408 | tf_op jit(solution)/shard_map/ppermute | solution.py:10
  20.1 0.2 constant_dynamic-update-slice_fusion
  20.4 12.0 %fusion.16 = f32[32,2048]{1,0:T(8,128)S(1)} fusion(bf16[32,7168]{1,0:T(8,128)(2,1)S(1)} %reshape.45, bf16[7168,2048]{1,0:T(8,128)(2,1)} %param.16), kind=kOutput, calls=%fused_computation.40 | convolution fusion | flops 939524096 | bytes 30081024 | tf_op jit(solution)/shard_map/dot_general | solution.py:60
  32.4 20.8 %convolution_multiply_fusion = f32[32,7168]{1,0:T(8,128)S(1)} fusion(bf16[2048,7168]{1,0:T(8,128)(2,1)} %param.18, f32[32]{0:T(128)S(1)} %select_reduce_fusion, f32[32,2048]{1,0:T(8,128)S(1)} %fusion.16, bf16[32,7168]{1,0:T(8,128)(2,1)S(1)} %reshape.45, bf16[7168,2048]{1,0:T(8,128)(2,1)} %param.17), kind=kOutput, calls=%fused_computation | convolution fusion | flops 1879670784 | bytes 60358784 | tf_op jit(solution)/shard_map/dot_general | solution.py:63
  53.3 0.3 slice.33
  53.7 0.2 collective-permute-start.4
  53.9 3.6 %fusion.15 = f32[32,304]{1,0:T(8,128)S(1)} fusion(bf16[32,7168]{1,0:T(8,128)(2,1)S(1)} %reshape.45, bf16[7168,304]{0,1:T(8,128)(2,1)} %param.13), kind=kOutput, calls=%fused_computation.39 | convolution fusion | flops 139460608 | bytes 4855808 | tf_op jit(solution)/shard_map/dot_general | solution.py:48
  57.6 1.6 %collective-permute-start.5 = (bf16[4,2,7168]{2,1,0:T(2,128)(2,1)S(1)}, bf16[4,2,7168]{2,1,0:T(2,128)(2,1)S(1)}, u32[]{:S(2)}, u32[]{:S(2)}) collective-permute-start(bf16[4,2,7168]{2,1,0:T(2,128)(2,1)S(1)} %slice.63), channel_id=1, source_target_pairs={{0,2},{1,3},{2,0},{3,1},{4,6},{5,7},{6,4},{7,5},{8,10},{9,11},{10,... | collective-permute-start | bytes 344072 | tf_op jit(solution)/shard_map/ppermute | solution.py:10
  59.2 3.7 %convolution_convert_fusion = bf16[32,304]{1,0:T(8,128)(2,1)S(1)} fusion(f32[32,304]{1,0:T(8,128)S(1)} %fusion.15, s32[32]{0:T(128)S(1)} %add.54, bf16[32,7168]{1,0:T(8,128)(2,1)S(1)} %reshape.45, bf16[7168,304]{0,1:T(8,128)(2,1)} %param.14), kind=kOutput, calls=%fused_computation.3 | convolution fusion | flops 140152320 | bytes 4875392 | tf_op jit(solution)/shard_map/dot_general | solution.py:52
  63.0 0.8 broadcast_in_dim.19
  63.7 5.0 %all-to-all-start = ((bf16[16,32,304]{2,1,0:T(8,128)(2,1)}), bf16[16,32,304]{2,1,0:T(8,128)(2,1)S(1)}, u32[]{:S(2)}, u32[]{:S(2)}) async-start(bf16[16,32,304]{2,1,0:T(8,128)(2,1)} %broadcast_in_dim.19), calls=%async_computation | async-start | bytes 786432 | tf_op jit(solution)/shard_map/all_to_all | solution.py:54
  68.9 2.0 %collective-permute-start.6 = (bf16[2,2,7168]{2,1,0:T(2,128)(2,1)S(1)}, bf16[2,2,7168]{2,1,0:T(2,128)(2,1)S(1)}, u32[]{:S(2)}, u32[]{:S(2)}) collective-permute-start(bf16[2,2,7168]{2,1,0:T(2,128)(2,1)S(1)} %slice.64), channel_id=1, source_target_pairs={{0,4},{1,5},{2,6},{3,7},{4,0},{5,1},{6,2},{7,3},{8,12},{9,13},{10,... | collective-permute-start | bytes 172040 | tf_op jit(solution)/shard_map/ppermute | solution.py:10
  70.9 10.5 %all-to-all-done = bf16[16,32,304]{2,1,0:T(8,128)(2,1)S(1)} async-done(((bf16[16,32,304]{2,1,0:T(8,128)(2,1)}), bf16[16,32,304]{2,1,0:T(8,128)(2,1)S(1)}, u32[]{:S(2)}, u32[]{:S(2)}) %all-to-all-start) | async-done | bytes 311328 | tf_op jit(solution)/shard_map/all_to_all | solution.py:54
  81.5 0.6 dot_general.26
  82.2 3.5 %fusion = f32[16,2,448]{2,0,1:T(8,128)S(1)} fusion(bf16[4864,448]{0,1:T(8,128)(2,1)} %param.15, bf16[16,2,4864]{2,1,0:T(2,128)(2,1)S(1)} %dot_general.26), kind=kOutput, calls=%fused_computation.1 | convolution fusion | flops 139460608 | bytes 4726784 | tf_op jit(solution)/shard_map/dot_general | solution.py:66
  85.7 0.7 copy.21
  86.4 3.5 %all-to-all-start.1 = ((f32[16,2,448]{2,1,0:T(2,128)}), f32[16,2,448]{2,1,0:T(2,128)S(1)}, u32[]{:S(2)}, u32[]{:S(2)}) async-start(f32[16,2,448]{2,1,0:T(2,128)} %copy.21), calls=%async_computation.1 | async-start | bytes 131072 | tf_op jit(solution)/shard_map/all_to_all | solution.py:67
  90.0 2.8 %collective-permute-start.7 = (bf16[1,2,7168]{2,1,0:T(2,128)(2,1)S(1)}, bf16[1,2,7168]{2,1,0:T(2,128)(2,1)S(1)}, u32[]{:S(2)}, u32[]{:S(2)}) collective-permute-start(bf16[1,2,7168]{2,1,0:T(2,128)(2,1)S(1)} %slice.65), channel_id=1, source_target_pairs={{0,8},{1,9},{2,10},{3,11},{4,12},{5,13},{6,14},{7,15},{8,0},{9,1},... | collective-permute-start | bytes 86024 | tf_op jit(solution)/shard_map/ppermute | solution.py:10
  92.8 4.2 %all-to-all-done.1 = f32[16,2,448]{2,1,0:T(2,128)S(1)} async-done(((f32[16,2,448]{2,1,0:T(2,128)}), f32[16,2,448]{2,1,0:T(2,128)S(1)}, u32[]{:S(2)}, u32[]{:S(2)}) %all-to-all-start.1) | async-done | bytes 57376 | tf_op jit(solution)/shard_map/all_to_all | solution.py:67
  97.2 0.7 fusion.6
  (26 shorter events, 1.4 us)
Async XLA Ops:
  0.0 6.6 %collective-permute-start = (bf16[1,2,7168]{2,1,0:T(2,128)(2,1)}, bf16[1,2,7168]{2,1,0:T(2,128)(2,1)S(1)}, u32[]{:S(2)}, u32[]{:S(2)}) collective-permute-start(bf16[1,2,7168]{2,1,0:T(2,128)(2,1)} %bitcast.29), channel_id=1, source_target_pairs={{0,8},{1,9},{2,10},{3,11},{4,12},{5,13},{6,14},{7,15},{8,0},{9,1},... | collective-permute-start | bytes 86024 | tf_op jit(solution)/shard_map/ppermute | solution.py:10
  7.4 4.2 %collective-permute-start.1 = (bf16[2,2,7168]{2,1,0:T(2,128)(2,1)S(1)}, bf16[2,2,7168]{2,1,0:T(2,128)(2,1)S(1)}, u32[]{:S(2)}, u32[]{:S(2)}) collective-permute-start(bf16[2,2,7168]{2,1,0:T(2,128)(2,1)S(1)} %pad_maximum_fusion.2), channel_id=1, source_target_pairs={{0,4},{1,5},{2,6},{3,7},{4,0},{5,1},{6,2},{7,3},{8,12},{9,13},{10,... | collective-permute-start | bytes 172040 | tf_op jit(solution)/shard_map/ppermute | solution.py:10
  12.6 4.9 %collective-permute-start.2 = (bf16[4,2,7168]{2,1,0:T(2,128)(2,1)S(1)}, bf16[4,2,7168]{2,1,0:T(2,128)(2,1)S(1)}, u32[]{:S(2)}, u32[]{:S(2)}) collective-permute-start(bf16[4,2,7168]{2,1,0:T(2,128)(2,1)S(1)} %pad_maximum_fusion.1), channel_id=1, source_target_pairs={{0,2},{1,3},{2,0},{3,1},{4,6},{5,7},{6,4},{7,5},{8,10},{9,11},{10,... | collective-permute-start | bytes 344072 | tf_op jit(solution)/shard_map/ppermute | solution.py:10
  18.5 1.6 %collective-permute-start.3 = (bf16[8,2,7168]{2,1,0:T(2,128)(2,1)S(1)}, bf16[8,2,7168]{2,1,0:T(2,128)(2,1)S(1)}, u32[]{:S(2)}, u32[]{:S(2)}) collective-permute-start(bf16[8,2,7168]{2,1,0:T(2,128)(2,1)S(1)} %pad_maximum_fusion), channel_id=1, source_target_pairs={{0,1},{1,0},{2,3},{3,2},{4,5},{5,4},{6,7},{7,6},{8,9},{9,8},{10,11... | collective-permute-start | bytes 688136 | tf_op jit(solution)/shard_map/ppermute | solution.py:10
  32.4 64.8 %copy-start = (bf16[2,7168]{1,0:T(2,128)(2,1)S(1)}, bf16[2,7168]{1,0:T(2,128)(2,1)}, u32[]{:S(2)}) copy-start(bf16[2,7168]{1,0:T(2,128)(2,1)} %param.10) | copy-start | bytes 86020
  53.7 3.8 %collective-permute-start.4 = (bf16[8,2,7168]{2,1,0:T(2,128)(2,1)S(1)}, bf16[8,2,7168]{2,1,0:T(2,128)(2,1)S(1)}, u32[]{:S(2)}, u32[]{:S(2)}) collective-permute-start(bf16[8,2,7168]{2,1,0:T(2,128)(2,1)S(1)} %convert_element_type.39), channel_id=1, source_target_pairs={{0,1},{1,0},{2,3},{3,2},{4,5},{5,4},{6,7},{7,6},{8,9},{9,8},{10,11... | collective-permute-start | bytes 688136 | tf_op jit(solution)/shard_map/ppermute | solution.py:10
  57.6 11.1 %collective-permute-start.5 = (bf16[4,2,7168]{2,1,0:T(2,128)(2,1)S(1)}, bf16[4,2,7168]{2,1,0:T(2,128)(2,1)S(1)}, u32[]{:S(2)}, u32[]{:S(2)}) collective-permute-start(bf16[4,2,7168]{2,1,0:T(2,128)(2,1)S(1)} %slice.63), channel_id=1, source_target_pairs={{0,2},{1,3},{2,0},{3,1},{4,6},{5,7},{6,4},{7,5},{8,10},{9,11},{10,... | collective-permute-start | bytes 344072 | tf_op jit(solution)/shard_map/ppermute | solution.py:10
  63.7 17.7 %all-to-all-start = ((bf16[16,32,304]{2,1,0:T(8,128)(2,1)}), bf16[16,32,304]{2,1,0:T(8,128)(2,1)S(1)}, u32[]{:S(2)}, u32[]{:S(2)}) async-start(bf16[16,32,304]{2,1,0:T(8,128)(2,1)} %broadcast_in_dim.19), calls=%async_computation | async-start | bytes 786432 | tf_op jit(solution)/shard_map/all_to_all | solution.py:54
  68.9 21.0 %collective-permute-start.6 = (bf16[2,2,7168]{2,1,0:T(2,128)(2,1)S(1)}, bf16[2,2,7168]{2,1,0:T(2,128)(2,1)S(1)}, u32[]{:S(2)}, u32[]{:S(2)}) collective-permute-start(bf16[2,2,7168]{2,1,0:T(2,128)(2,1)S(1)} %slice.64), channel_id=1, source_target_pairs={{0,4},{1,5},{2,6},{3,7},{4,0},{5,1},{6,2},{7,3},{8,12},{9,13},{10,... | collective-permute-start | bytes 172040 | tf_op jit(solution)/shard_map/ppermute | solution.py:10
  86.4 10.6 %all-to-all-start.1 = ((f32[16,2,448]{2,1,0:T(2,128)}), f32[16,2,448]{2,1,0:T(2,128)S(1)}, u32[]{:S(2)}, u32[]{:S(2)}) async-start(f32[16,2,448]{2,1,0:T(2,128)} %copy.21), calls=%async_computation.1 | async-start | bytes 131072 | tf_op jit(solution)/shard_map/all_to_all | solution.py:67
  90.0 7.2 %collective-permute-start.7 = (bf16[1,2,7168]{2,1,0:T(2,128)(2,1)S(1)}, bf16[1,2,7168]{2,1,0:T(2,128)(2,1)S(1)}, u32[]{:S(2)}, u32[]{:S(2)}) collective-permute-start(bf16[1,2,7168]{2,1,0:T(2,128)(2,1)S(1)} %slice.65), channel_id=1, source_target_pairs={{0,8},{1,9},{2,10},{3,11},{4,12},{5,13},{6,14},{7,15},{8,0},{9,1},... | collective-permute-start | bytes 86024 | tf_op jit(solution)/shard_map/ppermute | solution.py:10

commit v2 on v0

--- a/solution.py
+++ b/solution.py
@@ -1,9 +1,390 @@
+import functools
+
 import jax
 import jax.numpy as jnp
 from jax import lax
+from jax.experimental import pallas as pl
+from jax.experimental.pallas import tpu as pltpu
 from jax.sharding import PartitionSpec as P
 
 EH = 4096
+CHUNK = 1024
+SLOTS = 5
+AHEAD = 2
+MIB = 1 << 20
+
+VMEM = pl.BlockSpec(memory_space=pltpu.VMEM)
+SMEM = pl.BlockSpec(memory_space=pltpu.SMEM)
+ANY = pl.BlockSpec(memory_space=pl.ANY)
+
+
+def in_hbm(x):
+    return pltpu.with_memory_space_constraint(x, pltpu.HBM)
+
+
+def in_vmem(x):
+    return pltpu.with_memory_space_constraint(x, pltpu.VMEM)
+
+
+def cost(flops, moved):
+    return pl.CostEstimate(flops=flops, bytes_accessed=moved, transcendentals=0)
+
+
+def limit(mib):
+    return pltpu.CompilerParams(vmem_limit_bytes=mib * MIB)
+
+
+def dot(x, w):
+    return jnp.dot(x, w, preferred_element_type=jnp.float32)
+
+
+def dot_t(x, w):
+    return lax.dot_general(x, w, (((1,), (1,)), ((), ())), preferred_element_type=jnp.float32)
+
+
+def swiglu_hidden(gate, upward):
+    return (jax.nn.silu(gate) * upward).astype(jnp.bfloat16)
+
+
+def tokens_at(shape, axis, owned):
+    p = lax.broadcasted_iota(jnp.int32, shape, axis)
+    block, row = p // owned, p % owned
+    step = (block & 3) * 4 + ((block >> 2) & 1) * 2 + ((block >> 3) & 1)
+    return (lax.axis_index("gx") ^ step) * owned + row
+
+
+def swap_matrix(rows, owned, to_tokens):
+    shape = (rows, rows)
+    token = lax.broadcasted_iota(jnp.int32, shape, 0 if to_tokens else 1)
+    held = tokens_at(shape, 1 if to_tokens else 0, owned)
+    return jnp.where(token == held, 1.0, 0.0).astype(jnp.bfloat16)
+
+
+def fetch_kernel(ranges, after_ref, *refs):
+    count = len(ranges)
+    sources, held, done, sems = refs[:count], refs[count : 2 * count], refs[2 * count], refs[2 * count + 1]
+    copies = []
+    for source, target, (begin, size, pieces) in zip(sources, held, ranges):
+        step = size // pieces
+        for piece in range(pieces):
+            copies.append(
+                pltpu.make_async_copy(
+                    source.at[pl.ds(begin + piece * step, step)],
+                    target.at[pl.ds(piece * step, step)],
+                    sems.at[len(copies)],
+                )
+            )
+    for copy in copies:
+        copy.start()
+    done[0] = 0
+    for copy in copies:
+        copy.wait()
+
+
+def fetch(after, *wanted):
+    arrays = [w for w, _ in wanted]
+    ranges = [r for _, r in wanted]
+    *held, done = pl.pallas_call(
+        functools.partial(fetch_kernel, ranges),
+        out_shape=(
+            *[pltpu.VMEM((r[1], w.shape[1]), w.dtype) for w, r in wanted],
+            jax.ShapeDtypeStruct((1,), jnp.int32),
+        ),
+        in_specs=[SMEM] + [ANY] * len(arrays),
+        out_specs=(*[VMEM] * len(arrays), SMEM),
+        scratch_shapes=[pltpu.SemaphoreType.DMA((sum(r[2] for r in ranges),))],
+        cost_estimate=cost(0, sum(2 * r[1] * w.shape[1] for w, r in wanted)),
+        compiler_params=limit(1),
+    )(after, *[in_hbm(w) for w in arrays])
+    return held, done
+
+
+def join_kernel(count, done_ref, *refs):
+    blocks, joined = refs[:count], refs[count]
+    at = 0
+    for block in blocks:
+        size = block.shape[0]
+        joined[at : at + size] = block[...]
+        at += size
+
+
+def join(done, *blocks):
+    shape = (sum(b.shape[0] for b in blocks),) + blocks[0].shape[1:]
+    return pl.pallas_call(
+        functools.partial(join_kernel, len(blocks)),
+        out_shape=jax.ShapeDtypeStruct(shape, blocks[0].dtype),
+        in_specs=[SMEM] + [VMEM] * len(blocks),
+        out_specs=VMEM,
+        cost_estimate=cost(0, 4 * sum(b.size for b in blocks)),
+        compiler_params=limit(4),
+    )(done, *blocks)
+
+
+def dense_in_kernel(owned, mine_ref, other_ref, gate_ref, up_ref, hidden_ref, x):
+    half = mine_ref.shape[0]
+    x[0:half] = mine_ref[...]
+    x[half : 2 * half] = other_ref[...]
+    hidden = swiglu_hidden(dot_t(x[...], gate_ref[...]), dot_t(x[...], up_ref[...]))
+    hidden_ref[0] = dot(swap_matrix(2 * half, owned, True), hidden).astype(jnp.bfloat16)
+
+
+def dense_in(owned, mine, other, gate, up):
+    rows, width = 2 * mine.shape[0], mine.shape[1]
+    return pl.pallas_call(
+        functools.partial(dense_in_kernel, owned),
+        out_shape=jax.ShapeDtypeStruct((1, rows, gate.shape[0]), jnp.bfloat16),
+        in_specs=[VMEM] * 4,
+        out_specs=VMEM,
+        scratch_shapes=[pltpu.VMEM((rows, width), jnp.bfloat16)],
+        cost_estimate=cost(4 * rows * gate.size, 4 * gate.size),
+        compiler_params=limit(4),
+    )(mine, other, in_vmem(gate), in_vmem(up))
+
+
+def expert_in_kernel(count, mine_ref, other_ref, *refs):
+    gates = refs[:count]
+    up_ref, down_ref, hidden_ref, ahead_ref, x, ring, gate_sum, up_sum, sems, ahead_sems = refs[count:]
+    half, width = mine_ref.shape
+    units = up_ref.shape[1]
+    ups = width // CHUNK
+    slots = ring.shape[0]
+
+    def up_copy(chunk):
+        slot = lax.rem(chunk, slots)
+        row = pl.multiple_of(chunk * CHUNK, CHUNK)
+        return pltpu.make_async_copy(up_ref.at[pl.ds(row, CHUNK)], ring.at[slot], sems.at[slot])
+
+    def ahead_copy(part):
+        row = pl.multiple_of(part * CHUNK, CHUNK)
+        return pltpu.make_async_copy(
+            down_ref.at[pl.ds(row, CHUNK), pl.ds(0, units)], ahead_ref.at[part], ahead_sems.at[part]
+        )
+
+    for chunk in range(slots):
+        up_copy(chunk).start()
+    x[0:half] = mine_ref[...]
+    x[half : 2 * half] = other_ref[...]
+    gate_sum[...] = jnp.zeros_like(gate_sum)
+    up_sum[...] = jnp.zeros_like(up_sum)
+
+    begin = 0
+    for gate_ref in gates:
+
+        @pl.loop(0, gate_ref.shape[0] // CHUNK)
+        def _(chunk, gate_ref=gate_ref, begin=begin):
+            at = pl.multiple_of(chunk * CHUNK, CHUNK)
+            gate_sum[...] += dot(x[:, pl.ds(begin + at, CHUNK)], gate_ref[pl.ds(at, CHUNK), :])
+
+        begin += gate_ref.shape[0]
+
+    @pl.loop(0, ups)
+    def _(chunk):
+        up_copy(chunk).wait()
+        at = pl.ds(pl.multiple_of(chunk * CHUNK, CHUNK), CHUNK)
+        up_sum[...] += dot(x[:, at], ring[lax.rem(chunk, slots)])
+
+        @pl.when(chunk + slots < ups)
+        def _():
+            up_copy(chunk + slots).start()
+
+        @pl.when((chunk + slots >= ups) & (chunk + slots < ups + AHEAD))
+        def _():
+            ahead_copy(chunk + slots - ups).start()
+
+    hidden_ref[...] = swiglu_hidden(gate_sum[...], up_sum[...])
+    for part in range(AHEAD):
+        ahead_copy(part).wait()
+
+
+def expert_in(mine, other, gates, up, down):
+    rows, width = 2 * mine.shape[0], mine.shape[1]
+    units = up.shape[1]
+    return pl.pallas_call(
+        functools.partial(expert_in_kernel, len(gates)),
+        out_shape=(
+            jax.ShapeDtypeStruct((rows, units), jnp.bfloat16),
+            pltpu.VMEM((AHEAD, CHUNK, units), jnp.bfloat16),
+        ),
+        in_specs=[VMEM] * (2 + len(gates)) + [ANY] * 2,
+        out_specs=(VMEM, VMEM),
+        scratch_shapes=[
+            pltpu.VMEM((rows, width), jnp.bfloat16),
+            pltpu.VMEM((SLOTS, CHUNK, units), jnp.bfloat16),
+            pltpu.VMEM((rows, units), jnp.float32),
+            pltpu.VMEM((rows, units), jnp.float32),
+            pltpu.SemaphoreType.DMA((SLOTS,)),
+            pltpu.SemaphoreType.DMA((AHEAD,)),
+        ],
+        cost_estimate=cost(4 * rows * up.size, 2 * up.size),
+        compiler_params=limit(23),
+    )(mine, other, *[in_vmem(g) for g in gates], in_hbm(up), in_hbm(down))
+
+
+def expert_out_kernel(
+    owned, hidden_ref, ids_ref, gates_ref, ahead_ref, down_ref, dense_ref, out_ref, held_ref, ring, sems
+):
+    rows, units = hidden_ref.shape
+    width = out_ref.shape[1]
+    blocks = width // units
+    copies = []
+    for block in range(1, blocks):
+        for part in range(2):
+            copies.append(
+                pltpu.make_async_copy(
+                    down_ref.at[pl.ds(part * CHUNK, CHUNK), pl.ds(block * units, units)],
+                    ring.at[len(copies)],
+                    sems.at[len(copies)],
+                )
+            )
+    last = len(copies)
+    for part in range(2):
+        copies.append(
+            pltpu.make_async_copy(
+                down_ref.at[pl.ds(part * CHUNK, CHUNK), pl.ds(blocks * units, CHUNK)],
+                ring.at[last, :, pl.ds(part * CHUNK, CHUNK)],
+                sems.at[len(copies)],
+            )
+        )
+    copies.append(pltpu.make_async_copy(dense_ref, held_ref, sems.at[len(copies)]))
+    for copy in copies:
+        copy.start()
+
+    expert = lax.axis_index("gx") * units // EH
+    weights = jnp.sum(jnp.where(ids_ref[...] == expert, gates_ref[...], 0.0), axis=0, keepdims=True)
+    token = lax.broadcasted_iota(jnp.int32, (rows, rows), 1)
+    scale = jnp.sum(jnp.where(token == tokens_at((rows, rows), 0, owned), weights, 0.0), axis=1, keepdims=True)
+
+    first, second = hidden_ref[:, 0:CHUNK], hidden_ref[:, CHUNK : 2 * CHUNK]
+    out_ref[:, 0:units] = scale * (dot(first, ahead_ref[0]) + dot(second, ahead_ref[1]))
+    for block in range(1, blocks):
+        n = 2 * (block - 1)
+        copies[n].wait()
+        copies[n + 1].wait()
+        out_ref[:, block * units : (block + 1) * units] = scale * (dot(first, ring[n]) + dot(second, ring[n + 1]))
+    copies[last].wait()
+    copies[last + 1].wait()
+    out_ref[:, blocks * units :] = scale * (
+        dot(first, ring[last, :, 0:CHUNK]) + dot(second, ring[last, :, CHUNK : 2 * CHUNK])
+    )
+    copies[last + 2].wait()
+
+
+def expert_out(owned, hidden, ids, gates, ahead, down, dense_down):
+    rows, units = hidden.shape
+    width = down.shape[1]
+    chunks = down.size // (CHUNK * units) - AHEAD
+    return pl.pallas_call(
+        functools.partial(expert_out_kernel, owned),
+        out_shape=(
+            jax.ShapeDtypeStruct((rows, width), jnp.float32),
+            pltpu.VMEM(dense_down.shape, dense_down.dtype),
+        ),
+        in_specs=[VMEM] * 4 + [ANY] * 2,
+        out_specs=(VMEM, VMEM),
+        scratch_shapes=[
+            pltpu.VMEM((chunks, CHUNK, units), jnp.bfloat16),
+            pltpu.SemaphoreType.DMA((chunks + 2,)),
+        ],
+        cost_estimate=cost(2 * rows * down.size, 2 * down.size),
+        compiler_params=limit(24),
+    )(hidden, ids, gates, in_vmem(ahead), in_hbm(down), in_hbm(dense_down))
+
+
+def dense_out_kernel(owned, part_ref, b0, b1, b2, b3, down_ref, keep_ref, send_ref, held, joined, wide):
+    near, rows, units = b0.shape
+    half = rows // 2
+    columns, width = down_ref.shape[0], part_ref.shape[1]
+    own = lax.axis_index("gx")
+    for z, blocks in enumerate((b0, b1, b2, b3)):
+        held[z * near : (z + 1) * near] = blocks[...]
+    for j in range(4 * near):
+        joined[:, j * units : (j + 1) * units] = held[own ^ j]
+    dense_rows = dot(swap_matrix(rows, owned, False), joined[...]).astype(jnp.bfloat16)
+    wide[...] = jnp.zeros_like(wide)
+    wide[:, 0:columns] = dot_t(dense_rows, down_ref[...])
+    start = own * columns
+    base = jnp.minimum(start // 128 * 128, width - wide.shape[1])
+    moved = pltpu.roll(wide[...], start - base, 1)
+    at = pl.ds(pl.multiple_of(base, 128), wide.shape[1])
+    keep_ref[...] = part_ref[0:half]
+    send_ref[...] = part_ref[half:].astype(jnp.bfloat16)
+    keep_ref[:, at] += moved[:half]
+    send_ref[:, at] = (part_ref[half:, at] + moved[half:]).astype(jnp.bfloat16)
+
+
+def dense_out(owned, part, blocks, down):
+    near, rows, units = blocks[0].shape
+    columns, inner = down.shape
+    width = part.shape[1]
+    window = -(-(columns + 64) // 128) * 128 if columns % 64 == 0 else -(-(columns + 127) // 128) * 128
+    return pl.pallas_call(
+        functools.partial(dense_out_kernel, owned),
+        out_shape=(
+            jax.ShapeDtypeStruct((rows // 2, width), jnp.float32),
+            jax.ShapeDtypeStruct((rows // 2, width), jnp.bfloat16),
+        ),
+        in_specs=[VMEM] * 6,
+        out_specs=(VMEM, VMEM),
+        scratch_shapes=[
+            pltpu.VMEM((4 * near, rows, units), jnp.bfloat16),
+            pltpu.VMEM((rows, inner), jnp.bfloat16),
+            pltpu.VMEM((rows, window), jnp.float32),
+        ],
+        cost_estimate=cost(2 * rows * down.size, 2 * down.size),
+        compiler_params=limit(8),
+    )(part, *blocks, in_vmem(down))
+
+
+def four_by_two(
+    tokens,
+    route_ids,
+    route_gates,
+    dense_gate,
+    dense_up,
+    dense_down,
+    expert_gate,
+    expert_up,
+    expert_down,
+):
+    owned, width = tokens.shape
+    dense_gate, dense_up, dense_down = dense_gate.T, dense_up.T, dense_down.T
+
+    def swap(value, step):
+        return lax.ppermute(value, "gx", [(i, i ^ step) for i in range(16)])
+
+    none = jnp.zeros((1,), jnp.int32)
+    along_z = [swap(tokens, 4 * z) for z in (1, 2, 3)]
+    (gate_a,), done = fetch(none, (expert_gate, (0, 3 * CHUNK, 3)))
+    mine = join(done, tokens, *along_z)
+    along_x = swap(mine, 2)
+    (gate_b,), done = fetch(done, (expert_gate, (3 * CHUNK, 3 * CHUNK, 3)))
+    mine = join(done, mine, along_x)
+    other = swap(mine, 1)
+    units = dense_gate.shape[0]
+    (gate_c, dense_gate, dense_up), done = fetch(
+        done,
+        (expert_gate, (6 * CHUNK, width - 6 * CHUNK, 1)),
+        (dense_gate, (0, units, 1)),
+        (dense_up, (0, units, 1)),
+    )
+
+    block = dense_in(owned, mine, other, dense_gate, dense_up)
+    block = join(done, block, swap(block, 1))
+    along_x = swap(block, 2)
+    hidden, ahead = expert_in(mine, other, (gate_a, gate_b, gate_c), expert_up, expert_down)
+    block = join(done, block, along_x)
+    blocks = [block] + [swap(block, 4 * z) for z in (1, 2, 3)]
+    part, dense_down = expert_out(owned, hidden, route_ids.T, route_gates.T, ahead, expert_down, dense_down)
+    keep, send = dense_out(owned, part, blocks, dense_down)
+
+    half = keep.shape[0] // 2
+    keep = keep + swap(send, 1).astype(jnp.float32)
+    keep = keep[:half] + swap(keep[half:].astype(jnp.bfloat16), 2).astype(jnp.float32)
+    rest = keep.astype(jnp.bfloat16)
+    total = tokens.astype(jnp.float32) + keep[:owned]
+    for z in (1, 2, 3):
+        total = total + swap(rest[z * owned : (z + 1) * owned], 4 * z).astype(jnp.float32)
+    return total.astype(jnp.bfloat16)
 
 
 def swiglu(row_block, w_gate, w_up, w_down):
@@ -13,7 +394,7 @@
     return jnp.dot(hidden, w_down, preferred_element_type=jnp.float32)
 
 
-def per_device(
+def any_size(
     tokens,
     route_ids,
     route_gates,
@@ -69,6 +450,13 @@
         P("gx", None),
     )
     out_specs = P(("groups", "gx"), None)
-    return jax.shard_map(
-        per_device, mesh=mesh, in_specs=in_specs, out_specs=out_specs, check_vma=False
-    )
+
+    def layer(tokens, *rest):
+        size = mesh.shape["gx"]
+        width, units = tokens.shape[1], rest[-3].shape[1] // size
+        fits = size == 16 and units == 2 * CHUNK and width == 7 * CHUNK
+        body = four_by_two if fits else any_size
+        whole = jax.shard_map(body, mesh=mesh, in_specs=in_specs, out_specs=out_specs, check_vma=False)
+        return whole(tokens, *rest)
+
+    return layer

time: 170 us -> 80.7 us (0.47)
  Pallas kernels: 0 us -> 47.8 us
  matrix products: 43.5 us -> 0 us
  blocking collectives: 43.4 us -> 0 us
  waiting for transfers between devices: 54.6 us -> 11.7 us
  starting transfers between devices: 3.5 us -> 18.9 us
  between operations: 14.2 us -> 0.23 us
  local copies, waits for them, and re-layouts: 5.76 us -> 1.02 us
  other arithmetic: 5.13 us -> 0.76 us
    unnamed x2 -> x0, waiting for transfers between devices: 48.8 us -> none
    pallas_call x0 -> x11, Pallas kernels: none -> 47.8 us  [the longest x3 16.9 us: fetch(): pl.pallas_call(functools.partial(fetch_kernel, ranges), out_shape=(*[pltp...]
    dot_general x5 -> x0, matrix products: 43.5 us -> none  [the longest x1 20.8 us: swiglu(): return jnp.dot(hidden, w_down, preferred_element_type=jnp.float32)]
    all_gather x2 -> x0, blocking collectives: 43.4 us -> none  [the longest x1 24.6 us: per_device(): gathered = lax.all_gather(tokens, 'gx', axis=0, tiled=True)]
    ppermute x0 -> x15, starting transfers between devices: none -> 18.9 us  [swap(): return lax.ppermute(value, 'gx', [(i, i ^ step) for i in range(16)])]
    ppermute x0 -> x15, waiting for transfers between devices: none -> 11.7 us  [swap(): return lax.ppermute(value, 'gx', [(i, i ^ step) for i in range(16)])]
    all_to_all x1 -> x0, waiting for transfers between devices: 5.72 us -> none  [per_device(): lax.all_to_all(dense_part, 'gx', split_axis=0, concat_axis=1, tiled=True)]
    all_to_all x1 -> x0, starting transfers between devices: 3.5 us -> none  [per_device(): lax.all_to_all(dense_part, 'gx', split_axis=0, concat_axis=1, tiled=True)]
  transfers between devices with their start and end apart: 2 -> 15, of which waited for: 2 -> 6; matrix products, arithmetic and copies ran while one was open for 7% -> 0% of each run, Pallas kernels for 0% -> 51%
where the time goes in v2:
time: 80.7 us; the launch traced here: 80.5 us
  Pallas kernels  47.8 us (59%)
  starting transfers between devices  18.9 us (23%)
  waiting for transfers between devices  11.7 us (14%)
  local copies, waits for them, and re-layouts  1.02 us (1%)
    ppermute x15, starting transfers between devices, swap(): return lax.ppermute(value, 'gx', [(i, i ^ step) for i in range(16)])  18.9 us
    pallas_call x3, Pallas kernels, fetch(): pl.pallas_call(functools.partial(fetch_kernel, ranges), out_shape=(*[pltp...  16.9 us
    pallas_call x1, Pallas kernels, expert_in(): pl.pallas_call(functools.partial(expert_in_kernel, len(gates)), out_shape...  14.4 us
    ppermute x15, waiting for transfers between devices, swap(): return lax.ppermute(value, 'gx', [(i, i ^ step) for i in range(16)])  11.7 us
    pallas_call x1, Pallas kernels, expert_out(): pl.pallas_call(functools.partial(expert_out_kernel, owned), out_shape=(ja...  9.82 us
    pallas_call x4, Pallas kernels, join(): pl.pallas_call(functools.partial(join_kernel, len(blocks)), out_shape=jax...  2.61 us
    pallas_call x1, Pallas kernels, dense_in(): pl.pallas_call(functools.partial(dense_in_kernel, owned), out_shape=jax.S...  2.49 us
    pallas_call x1, Pallas kernels, dense_out(): pl.pallas_call(functools.partial(dense_out_kernel, owned), out_shape=(jax...  1.63 us
  transfers between devices with their start and end apart: 15, of which 6 were waited for; matrix products, arithmetic and copies ran while one was open for 0% of the time, Pallas kernels for 51%

profile of v2, /device:TPU:0, one launch (start us, length us, event | category | flops | bytes accessed | tf_op | source)
XLA Modules:
  0.0 80.5 jit_solution(5041563103641930860)
XLA Ops:
  0.0 3.0 %collective-permute-start = (bf16[2,7168]{1,0:T(2,128)(2,1)}, bf16[2,7168]{1,0:T(2,128)(2,1)S(1)}, u32[]{:S(2)}, u32[]{:S(2)}) collective-permute-start(bf16[2,7168]{1,0:T(2,128)(2,1)} %refs_0_.6), channel_id=1, source_target_pairs={{0,4},{1,5},{2,6},{3,7},{4,0},{5,1},{6,2},{7,3},{8,12},{9,13},{10,... | collective-permute-start | bytes 86024 | tf_op jit(solution)/shard_map/ppermute | solution.py:353
  3.0 2.6 %collective-permute-start.1 = (bf16[2,7168]{1,0:T(2,128)(2,1)}, bf16[2,7168]{1,0:T(2,128)(2,1)S(1)}, u32[]{:S(2)}, u32[]{:S(2)}) collective-permute-start(bf16[2,7168]{1,0:T(2,128)(2,1)} %refs_0_.6), channel_id=1, source_target_pairs={{0,8},{1,9},{2,10},{3,11},{4,12},{5,13},{6,14},{7,15},{8,0},{9,1},... | collective-permute-start | bytes 86024 | tf_op jit(solution)/shard_map/ppermute | solution.py:353
  5.6 5.2 %shard_map.91 = (bf16[3072,2048]{1,0:T(8,128)(2,1)S(1)}, s32[1]{0:T(128)}) custom-call(s32[1]{0:T(128)} %constant.0.clone.1.after_ref, bf16[7168,2048]{1,0:T(8,128)(2,1)} %refs_0_.7), custom_call_target="tpu_custom_call" | custom-call | bytes 12582912 | tf_op jit(solution)/shard_map/pallas_call | solution.py:87
  10.8 0.6 collective-permute-done.2.refs_3_
  11.5 0.7 shard_map.93.refs_0_
  12.2 1.6 %collective-permute-start.3 = (bf16[8,7168]{1,0:T(8,128)(2,1)S(1)}, bf16[8,7168]{1,0:T(8,128)(2,1)S(1)}, u32[]{:S(2)}, u32[]{:S(2)}) collective-permute-start(bf16[8,7168]{1,0:T(8,128)(2,1)S(1)} %shard_map.93.refs_0_), channel_id=1, source_target_pairs={{0,2},{1,3},{2,0},{3,1},{4,6},{5,7},{6,4},{7,5},{8,10},{9,11},{10,... | collective-permute-start | bytes 344072 | tf_op jit(solution)/shard_map/ppermute | solution.py:353
  13.8 5.8 %shard_map.92 = (bf16[3072,2048]{1,0:T(8,128)(2,1)S(1)}, s32[1]{0:T(128)}) custom-call(s32[1]{0:T(128)} %get-tuple-element.19.after_ref.done_ref, bf16[7168,2048]{1,0:T(8,128)(2,1)} %refs_0_.7), custom_call_target="tpu_custom_call" | custom-call | bytes 12582912 | tf_op jit(solution)/shard_map/pallas_call | solution.py:87
  19.6 0.6 shard_map.94.mine_ref
  20.2 0.1 collective-permute-start.4
  20.3 5.9 %shard_map.95 = (bf16[1024,2048]{1,0:T(8,128)(2,1)S(1)}, bf16[304,7168]{1,0:T(8,128)(2,1)S(1)}, bf16[304,7168]{1,0:T(8,128)(2,1)S(1)}, s32[1]{0:T(128)}) custom-call(s32[1]{0:T(128)} %get-tuple-element.20.done_ref.after_ref, bf16[7168,2048]{1,0:T(8,128)(2,1)} %refs_0_.7, bf16[304,7168]{1,0:T(8,128)(2,1)} %bitcast.7, bf16[304,7168]{1,0:T(8,128)(2,1)} %bitcast.8), custom_call_target="tpu_custom_call" | custom-call | bytes 12910592 | tf_op jit(solution)/shard_map/pallas_call | solution.py:87
  26.2 2.5 %shard_map.98.refs_0_ = bf16[1,32,304]{2,1,0:T(8,128)(2,1)S(1)} custom-call(bf16[16,7168]{1,0:T(8,128)(2,1)S(1)} %shard_map.94.mine_ref, bf16[16,7168]{1,0:T(8,128)(2,1)S(1)} %collective-permute-done.4.other_ref, bf16[304,7168]{1,0:T(8,128)(2,1)S(1)} %get-tuple-element.28.gate_ref, bf16[304,7168]{1,0:T(8,128)(2,1)S(1)} %get-tuple-element.29.up_ref), custom_call_target="tpu_custom_call" | custom-call | flops 278921216 | bytes 8716288 | tf_op jit(solution)/shard_map/pallas_call | solution.py:133
  28.7 0.6 collective-permute-start.5
  29.3 0.8 %collective-permute-done.5.refs_1_ = bf16[1,32,304]{2,1,0:T(8,128)(2,1)S(1)} collective-permute-done((bf16[1,32,304]{2,1,0:T(8,128)(2,1)S(1)}, bf16[1,32,304]{2,1,0:T(8,128)(2,1)S(1)}, u32[]{:S(2)}, u32[]{:S(2)}) %collective-permute-start.5) | collective-permute-done | bytes 19488 | tf_op jit(solution)/shard_map/ppermute | solution.py:353
  30.1 0.6 shard_map.99.refs_0_
  30.8 0.6 collective-permute-start.6
  31.4 14.4 %shard_map.96 = (bf16[32,2048]{1,0:T(8,128)(2,1)}, bf16[2,1024,2048]{2,1,0:T(8,128)(2,1)S(1)}) custom-call(bf16[16,7168]{1,0:T(8,128)(2,1)} %copy-done, bf16[16,7168]{1,0:T(8,128)(2,1)} %copy-done.1, bf16[3072,2048]{1,0:T(8,128)(2,1)S(1)} %get-tuple-element.21.refs_0_, bf16[3072,2048]{1,0:T(8,128)(2,1)S(1)} %get-tuple-element.22.refs_1_, ...), custom_call_target="tpu_custom_call" | custom-call | flops 1879048192 | bytes 29360128 | tf_op jit(solution)/shard_map/pallas_call | solution.py:202
  45.8 0.7 shard_map.100.b0
  46.5 0.3 collective-permute-start.7
  46.8 3.5 %collective-permute-start.8 = (bf16[4,32,304]{2,1,0:T(8,128)(2,1)S(1)}, bf16[4,32,304]{2,1,0:T(8,128)(2,1)S(1)}, u32[]{:S(2)}, u32[]{:S(2)}) collective-permute-start(bf16[4,32,304]{2,1,0:T(8,128)(2,1)S(1)} %shard_map.100.b0), channel_id=1, source_target_pairs={{0,8},{1,9},{2,10},{3,11},{4,12},{5,13},{6,14},{7,15},{8,0},{9,1},... | collective-permute-start | bytes 233480 | tf_op jit(solution)/shard_map/ppermute | solution.py:353
  50.3 0.6 collective-permute-start.9
  50.9 0.9 %copy-done.2 = bf16[32,2048]{1,0:T(8,128)(2,1)S(1)} copy-done((bf16[32,2048]{1,0:T(8,128)(2,1)S(1)}, bf16[32,2048]{1,0:T(8,128)(2,1)}, u32[]{:S(2)}) %copy-start.2) | copy-done | bytes 131096
  51.8 9.8 %shard_map.97 = (f32[32,7168]{1,0:T(8,128)S(1)}, bf16[448,4864]{1,0:T(8,128)(2,1)S(1)}) custom-call(bf16[32,2048]{1,0:T(8,128)(2,1)S(1)} %copy-done.2, s32[2,32]{1,0:T(2,128)S(1)} %bitcast.5, f32[2,32]{1,0:T(2,128)S(1)} %bitcast.6, bf16[2,1024,2048]{2,1,0:T(8,128)(2,1)S(1)} %get-tuple-element.25.ahead_ref, bf16[2048,7168]{1,0:T(8,128)(2,1)} %down_ref.1, ...), custom_call_target="tpu_custom_call" | custom-call | flops 939524096 | bytes 29360128 | tf_op jit(solution)/shard_map/pallas_call | solution.py:276
  61.7 1.6 %shard_map.101 = (f32[16,7168]{1,0:T(8,128)S(1)}, bf16[16,7168]{1,0:T(8,128)(2,1)S(1)}) custom-call(f32[32,7168]{1,0:T(8,128)S(1)} %get-tuple-element.26.part_ref, bf16[4,32,304]{2,1,0:T(8,128)(2,1)S(1)} %shard_map.100.b0, bf16[4,32,304]{2,1,0:T(8,128)(2,1)S(1)} %collective-permute-done.7.b1, bf16[4,32,304]{2,1,0:T(8,128)(2,1)S(1)} %collective-permute-done.8.b2, ...), custom_call_target="tpu_custom_call" | custom-call | flops 139460608 | bytes 4358144 | tf_op jit(solution)/shard_map/pallas_call | solution.py:320
  63.4 1.5 %collective-permute-done.10 = bf16[16,7168]{1,0:T(8,128)(2,1)S(1)} collective-permute-done((bf16[16,7168]{1,0:T(8,128)(2,1)S(1)}, bf16[16,7168]{1,0:T(8,128)(2,1)S(1)}, u32[]{:S(2)}, u32[]{:S(2)}) %collective-permute-start.10) | collective-permute-done | bytes 229408 | tf_op jit(solution)/shard_map/ppermute | solution.py:353
  64.9 1.6 %collective-permute-start.11 = (bf16[8,7168]{1,0:T(8,128)(2,1)S(1)}, bf16[8,7168]{1,0:T(8,128)(2,1)S(1)}, u32[]{:S(2)}, u32[]{:S(2)}) collective-permute-start(bf16[8,7168]{1,0:T(8,128)(2,1)S(1)} %slice.42), channel_id=1, source_target_pairs={{0,2},{1,3},{2,0},{3,1},{4,6},{5,7},{6,4},{7,5},{8,10},{9,11},{10,... | collective-permute-start | bytes 344072 | tf_op jit(solution)/shard_map/ppermute | solution.py:353
  66.5 3.7 %collective-permute-done.11 = bf16[8,7168]{1,0:T(8,128)(2,1)S(1)} collective-permute-done((bf16[8,7168]{1,0:T(8,128)(2,1)S(1)}, bf16[8,7168]{1,0:T(8,128)(2,1)S(1)}, u32[]{:S(2)}, u32[]{:S(2)}) %collective-permute-start.11) | collective-permute-done | bytes 114720 | tf_op jit(solution)/shard_map/ppermute | solution.py:353
  70.2 0.1 fusion.5
  70.4 3.7 %collective-permute-start.13 = (bf16[2,7168]{1,0:T(2,128)(2,1)S(1)}, bf16[2,7168]{1,0:T(2,128)(2,1)S(1)}, u32[]{:S(2)}, u32[]{:S(2)}) collective-permute-start(bf16[2,7168]{1,0:T(2,128)(2,1)S(1)} %get-tuple-element.37), channel_id=1, source_target_pairs={{0,8},{1,9},{2,10},{3,11},{4,12},{5,13},{6,14},{7,15},{8,0},{9,1},... | collective-permute-start | bytes 86024 | tf_op jit(solution)/shard_map/ppermute | solution.py:353
  74.1 0.6 collective-permute-start.14
  74.8 1.2 %collective-permute-done.13 = bf16[2,7168]{1,0:T(2,128)(2,1)S(1)} collective-permute-done((bf16[2,7168]{1,0:T(2,128)(2,1)S(1)}, bf16[2,7168]{1,0:T(2,128)(2,1)S(1)}, u32[]{:S(2)}, u32[]{:S(2)}) %collective-permute-start.13) | collective-permute-done | bytes 28704 | tf_op jit(solution)/shard_map/ppermute | solution.py:353
  76.0 3.8 %collective-permute-done.14 = bf16[2,7168]{1,0:T(2,128)(2,1)S(1)} collective-permute-done((bf16[2,7168]{1,0:T(2,128)(2,1)S(1)}, bf16[2,7168]{1,0:T(2,128)(2,1)S(1)}, u32[]{:S(2)}, u32[]{:S(2)}) %collective-permute-start.14) | collective-permute-done | bytes 28704 | tf_op jit(solution)/shard_map/ppermute | solution.py:353
  79.8 0.7 fusion.3
  (26 shorter events, 0.3 us)
Async XLA Ops:
  0.0 11.5 %copy-start.3 = (bf16[2,7168]{1,0:T(2,128)(2,1)S(1)}, bf16[2,7168]{1,0:T(2,128)(2,1)}, u32[]{:S(2)}) copy-start(bf16[2,7168]{1,0:T(2,128)(2,1)} %refs_0_.6) | copy-start | bytes 86020
  0.0 10.8 %collective-permute-start = (bf16[2,7168]{1,0:T(2,128)(2,1)}, bf16[2,7168]{1,0:T(2,128)(2,1)S(1)}, u32[]{:S(2)}, u32[]{:S(2)}) collective-permute-start(bf16[2,7168]{1,0:T(2,128)(2,1)} %refs_0_.6), channel_id=1, source_target_pairs={{0,4},{1,5},{2,6},{3,7},{4,0},{5,1},{6,2},{7,3},{8,12},{9,13},{10,... | collective-permute-start | bytes 86024 | tf_op jit(solution)/shard_map/ppermute | solution.py:353
  3.0 7.8 %collective-permute-start.1 = (bf16[2,7168]{1,0:T(2,128)(2,1)}, bf16[2,7168]{1,0:T(2,128)(2,1)S(1)}, u32[]{:S(2)}, u32[]{:S(2)}) collective-permute-start(bf16[2,7168]{1,0:T(2,128)(2,1)} %refs_0_.6), channel_id=1, source_target_pairs={{0,8},{1,9},{2,10},{3,11},{4,12},{5,13},{6,14},{7,15},{8,0},{9,1},... | collective-permute-start | bytes 86024 | tf_op jit(solution)/shard_map/ppermute | solution.py:353
  5.6 5.9 %collective-permute-start.2 = (bf16[2,7168]{1,0:T(2,128)(2,1)}, bf16[2,7168]{1,0:T(2,128)(2,1)S(1)}, u32[]{:S(2)}, u32[]{:S(2)}) collective-permute-start(bf16[2,7168]{1,0:T(2,128)(2,1)} %refs_0_.6), channel_id=1, source_target_pairs={{0,12},{1,13},{2,14},{3,15},{4,8},{5,9},{6,10},{7,11},{8,4},{9,5},... | collective-permute-start | bytes 86024 | tf_op jit(solution)/shard_map/ppermute | solution.py:353
  12.2 7.4 %collective-permute-start.3 = (bf16[8,7168]{1,0:T(8,128)(2,1)S(1)}, bf16[8,7168]{1,0:T(8,128)(2,1)S(1)}, u32[]{:S(2)}, u32[]{:S(2)}) collective-permute-start(bf16[8,7168]{1,0:T(8,128)(2,1)S(1)} %shard_map.93.refs_0_), channel_id=1, source_target_pairs={{0,2},{1,3},{2,0},{3,1},{4,6},{5,7},{6,4},{7,5},{8,10},{9,11},{10,... | collective-permute-start | bytes 344072 | tf_op jit(solution)/shard_map/ppermute | solution.py:353
  20.2 6.0 %copy-start = (bf16[16,7168]{1,0:T(8,128)(2,1)}, bf16[16,7168]{1,0:T(8,128)(2,1)S(1)}, u32[]{:S(2)}) copy-start(bf16[16,7168]{1,0:T(8,128)(2,1)S(1)} %shard_map.94.mine_ref) | copy-start | bytes 688132
  20.2 6.0 %collective-permute-start.4 = (bf16[16,7168]{1,0:T(8,128)(2,1)S(1)}, bf16[16,7168]{1,0:T(8,128)(2,1)S(1)}, u32[]{:S(2)}, u32[]{:S(2)}) collective-permute-start(bf16[16,7168]{1,0:T(8,128)(2,1)S(1)} %shard_map.94.mine_ref), channel_id=1, source_target_pairs={{0,1},{1,0},{2,3},{3,2},{4,5},{5,4},{6,7},{7,6},{8,9},{9,8},{10,11... | collective-permute-start | bytes 688136 | tf_op jit(solution)/shard_map/ppermute | solution.py:353
  26.2 2.5 %copy-start.1 = (bf16[16,7168]{1,0:T(8,128)(2,1)}, bf16[16,7168]{1,0:T(8,128)(2,1)S(1)}, u32[]{:S(2)}) copy-start(bf16[16,7168]{1,0:T(8,128)(2,1)S(1)} %collective-permute-done.4.other_ref) | copy-start | bytes 688132
  28.7 1.4 %collective-permute-start.5 = (bf16[1,32,304]{2,1,0:T(8,128)(2,1)S(1)}, bf16[1,32,304]{2,1,0:T(8,128)(2,1)S(1)}, u32[]{:S(2)}, u32[]{:S(2)}) collective-permute-start(bf16[1,32,304]{2,1,0:T(8,128)(2,1)S(1)} %shard_map.98.refs_0_), channel_id=1, source_target_pairs={{0,1},{1,0},{2,3},{3,2},{4,5},{5,4},{6,7},{7,6},{8,9},{9,8},{10,11... | collective-permute-start | bytes 58376 | tf_op jit(solution)/shard_map/ppermute | solution.py:353
  30.8 15.0 %collective-permute-start.6 = (bf16[2,32,304]{2,1,0:T(8,128)(2,1)S(1)}, bf16[2,32,304]{2,1,0:T(8,128)(2,1)S(1)}, u32[]{:S(2)}, u32[]{:S(2)}) collective-permute-start(bf16[2,32,304]{2,1,0:T(8,128)(2,1)S(1)} %shard_map.99.refs_0_), channel_id=1, source_target_pairs={{0,2},{1,3},{2,0},{3,1},{4,6},{5,7},{6,4},{7,5},{8,10},{9,11},{10,... | collective-permute-start | bytes 116744 | tf_op jit(solution)/shard_map/ppermute | solution.py:353
  31.4 19.5 %copy-start.4 = (s32[32,2]{0,1:T(2,128)S(1)}, s32[32,2]{0,1:T(2,128)}, u32[]{:S(2)}) copy-start(s32[32,2]{0,1:T(2,128)} %param.10) | copy-start | bytes 772
  31.4 19.5 %copy-start.5 = (f32[32,2]{0,1:T(2,128)S(1)}, f32[32,2]{0,1:T(2,128)}, u32[]{:S(2)}) copy-start(f32[32,2]{0,1:T(2,128)} %param.11) | copy-start | bytes 772
  46.5 15.2 %collective-permute-start.7 = (bf16[4,32,304]{2,1,0:T(8,128)(2,1)S(1)}, bf16[4,32,304]{2,1,0:T(8,128)(2,1)S(1)}, u32[]{:S(2)}, u32[]{:S(2)}) collective-permute-start(bf16[4,32,304]{2,1,0:T(8,128)(2,1)S(1)} %shard_map.100.b0), channel_id=1, source_target_pairs={{0,4},{1,5},{2,6},{3,7},{4,0},{5,1},{6,2},{7,3},{8,12},{9,13},{10,... | collective-permute-start | bytes 233480 | tf_op jit(solution)/shard_map/ppermute | solution.py:353
  46.8 14.9 %collective-permute-start.8 = (bf16[4,32,304]{2,1,0:T(8,128)(2,1)S(1)}, bf16[4,32,304]{2,1,0:T(8,128)(2,1)S(1)}, u32[]{:S(2)}, u32[]{:S(2)}) collective-permute-start(bf16[4,32,304]{2,1,0:T(8,128)(2,1)S(1)} %shard_map.100.b0), channel_id=1, source_target_pairs={{0,8},{1,9},{2,10},{3,11},{4,12},{5,13},{6,14},{7,15},{8,0},{9,1},... | collective-permute-start | bytes 233480 | tf_op jit(solution)/shard_map/ppermute | solution.py:353
  50.3 11.4 %collective-permute-start.9 = (bf16[4,32,304]{2,1,0:T(8,128)(2,1)S(1)}, bf16[4,32,304]{2,1,0:T(8,128)(2,1)S(1)}, u32[]{:S(2)}, u32[]{:S(2)}) collective-permute-start(bf16[4,32,304]{2,1,0:T(8,128)(2,1)S(1)} %shard_map.100.b0), channel_id=1, source_target_pairs={{0,12},{1,13},{2,14},{3,15},{4,8},{5,9},{6,10},{7,11},{8,4},{9,5},... | collective-permute-start | bytes 233480 | tf_op jit(solution)/shard_map/ppermute | solution.py:353
  50.9 0.9 %copy-start.2 = (bf16[32,2048]{1,0:T(8,128)(2,1)S(1)}, bf16[32,2048]{1,0:T(8,128)(2,1)}, u32[]{:S(2)}) copy-start(bf16[32,2048]{1,0:T(8,128)(2,1)} %get-tuple-element.24.hidden_ref) | copy-start | bytes 393220
  63.3 1.6 %collective-permute-start.10 = (bf16[16,7168]{1,0:T(8,128)(2,1)S(1)}, bf16[16,7168]{1,0:T(8,128)(2,1)S(1)}, u32[]{:S(2)}, u32[]{:S(2)}) collective-permute-start(bf16[16,7168]{1,0:T(8,128)(2,1)S(1)} %get-tuple-element.32), channel_id=1, source_target_pairs={{0,1},{1,0},{2,3},{3,2},{4,5},{5,4},{6,7},{7,6},{8,9},{9,8},{10,11... | collective-permute-start | bytes 688136 | tf_op jit(solution)/shard_map/ppermute | solution.py:353
  64.9 5.3 %collective-permute-start.11 = (bf16[8,7168]{1,0:T(8,128)(2,1)S(1)}, bf16[8,7168]{1,0:T(8,128)(2,1)S(1)}, u32[]{:S(2)}, u32[]{:S(2)}) collective-permute-start(bf16[8,7168]{1,0:T(8,128)(2,1)S(1)} %slice.42), channel_id=1, source_target_pairs={{0,2},{1,3},{2,0},{3,1},{4,6},{5,7},{6,4},{7,5},{8,10},{9,11},{10,... | collective-permute-start | bytes 344072 | tf_op jit(solution)/shard_map/ppermute | solution.py:353
  70.3 4.5 %collective-permute-start.12 = (bf16[2,7168]{1,0:T(2,128)(2,1)S(1)}, bf16[2,7168]{1,0:T(2,128)(2,1)S(1)}, u32[]{:S(2)}, u32[]{:S(2)}) collective-permute-start(bf16[2,7168]{1,0:T(2,128)(2,1)S(1)} %get-tuple-element.35), channel_id=1, source_target_pairs={{0,4},{1,5},{2,6},{3,7},{4,0},{5,1},{6,2},{7,3},{8,12},{9,13},{10,... | collective-permute-start | bytes 86024 | tf_op jit(solution)/shard_map/ppermute | solution.py:353
  70.4 5.6 %collective-permute-start.13 = (bf16[2,7168]{1,0:T(2,128)(2,1)S(1)}, bf16[2,7168]{1,0:T(2,128)(2,1)S(1)}, u32[]{:S(2)}, u32[]{:S(2)}) collective-permute-start(bf16[2,7168]{1,0:T(2,128)(2,1)S(1)} %get-tuple-element.37), channel_id=1, source_target_pairs={{0,8},{1,9},{2,10},{3,11},{4,12},{5,13},{6,14},{7,15},{8,0},{9,1},... | collective-permute-start | bytes 86024 | tf_op jit(solution)/shard_map/ppermute | solution.py:353
  74.1 5.7 %collective-permute-start.14 = (bf16[2,7168]{1,0:T(2,128)(2,1)S(1)}, bf16[2,7168]{1,0:T(2,128)(2,1)S(1)}, u32[]{:S(2)}, u32[]{:S(2)}) collective-permute-start(bf16[2,7168]{1,0:T(2,128)(2,1)S(1)} %get-tuple-element.36), channel_id=1, source_target_pairs={{0,12},{1,13},{2,14},{3,15},{4,8},{5,9},{6,10},{7,11},{8,4},{9,5},... | collective-permute-start | bytes 86024 | tf_op jit(solution)/shard_map/ppermute | solution.py:353

commit v3 on v0

--- a/solution.py
+++ b/solution.py
@@ -1,9 +1,374 @@
+import functools
+
 import jax
 import jax.numpy as jnp
 from jax import lax
+from jax.experimental import pallas as pl
+from jax.experimental.pallas import tpu as pltpu
 from jax.sharding import PartitionSpec as P
 
 EH = 4096
+CHUNK = 1024
+PER = 7
+SLOTS = 4
+AHEAD = (3, 2, 0, 2, 0)
+MIB = 1 << 20
+
+VMEM = pl.BlockSpec(memory_space=pltpu.VMEM)
+SMEM = pl.BlockSpec(memory_space=pltpu.SMEM)
+ANY = pl.BlockSpec(memory_space=pl.ANY)
+
+
+def in_hbm(x):
+    return pltpu.with_memory_space_constraint(x, pltpu.HBM)
+
+
+def in_vmem(x):
+    return pltpu.with_memory_space_constraint(x, pltpu.VMEM)
+
+
+def cost(flops, moved):
+    return pl.CostEstimate(flops=flops, bytes_accessed=moved, transcendentals=0)
+
+
+def limit(mib):
+    return pltpu.CompilerParams(vmem_limit_bytes=mib * MIB)
+
+
+def dot(x, w):
+    return jnp.dot(x, w, preferred_element_type=jnp.float32)
+
+
+def dot_t(x, w):
+    return lax.dot_general(x, w, (((1,), (1,)), ((), ())), preferred_element_type=jnp.float32)
+
+
+def swiglu_hidden(gate, upward):
+    return (jax.nn.silu(gate) * upward).astype(jnp.bfloat16)
+
+
+def tokens_at(shape, axis, owned):
+    p = lax.broadcasted_iota(jnp.int32, shape, axis)
+    block, row = p // owned, p % owned
+    step = (block & 3) * 4 + ((block >> 2) & 1) * 2 + ((block >> 3) & 1)
+    return (lax.axis_index("gx") ^ step) * owned + row
+
+
+def swap_matrix(rows, owned, to_tokens):
+    shape = (rows, rows)
+    token = lax.broadcasted_iota(jnp.int32, shape, 0 if to_tokens else 1)
+    held = tokens_at(shape, 1 if to_tokens else 0, owned)
+    return jnp.where(token == held, 1.0, 0.0).astype(jnp.bfloat16)
+
+
+def chunk_source(chunk, gate_ref, up_ref):
+    source = gate_ref if chunk < PER else up_ref
+    return source.at[pl.ds(chunk % PER * CHUNK, CHUNK)]
+
+
+def start_copies(pairs, sems):
+    copies = [pltpu.make_async_copy(source, target, sems.at[n]) for n, (source, target) in enumerate(pairs)]
+    for copy in copies:
+        copy.start()
+    return copies
+
+
+def wait_copies(copies):
+    for copy in copies:
+        copy.wait()
+
+
+def chunk_shapes(count):
+    return [pltpu.VMEM((CHUNK, 2 * CHUNK), jnp.bfloat16)] * count
+
+
+def fetch_kernel(chunks, whole_count, tied, *refs):
+    refs = refs[1:] if tied else refs
+    gate_ref, up_ref, refs = refs[0], refs[1], refs[2:]
+    wholes, refs = refs[:whole_count], refs[whole_count:]
+    count = len(chunks)
+    held, targets, (done_ref, sems) = refs[:count], refs[count : count + whole_count], refs[count + whole_count :]
+    pairs = [(chunk_source(c, gate_ref, up_ref), ref) for c, ref in zip(chunks, held)]
+    copies = start_copies(pairs + list(zip(wholes, targets)), sems)
+    done_ref[...] = jnp.zeros_like(done_ref)
+    wait_copies(copies)
+
+
+def fetch(after, chunks, gate, up, *wholes):
+    tied = after is not None
+    count = len(chunks)
+    found = pl.pallas_call(
+        functools.partial(fetch_kernel, chunks, len(wholes), tied),
+        out_shape=(
+            *chunk_shapes(count),
+            *[pltpu.VMEM(w.shape, w.dtype) for w in wholes],
+            pltpu.VMEM((8, 128), jnp.float32),
+        ),
+        in_specs=[VMEM] * tied + [ANY] * (2 + len(wholes)),
+        out_specs=(VMEM,) * (count + len(wholes) + 1),
+        scratch_shapes=[pltpu.SemaphoreType.DMA((count + len(wholes),))],
+        cost_estimate=cost(0, 4 * count * CHUNK * CHUNK + sum(2 * w.size for w in wholes)),
+        compiler_params=limit(1),
+    )(*([in_vmem(after)] if tied else []), in_hbm(gate), in_hbm(up), *[in_hbm(w) for w in wholes])
+    return list(found[:count]), *found[count:]
+
+
+def join_kernel(count, *refs):
+    blocks, joined = refs[-1 - count : -1], refs[-1]
+    at = 0
+    for block in blocks:
+        size = block.shape[0]
+        joined[at : at + size] = block[...]
+        at += size
+
+
+def join(done, *blocks):
+    shape = (sum(b.shape[0] for b in blocks),) + blocks[0].shape[1:]
+    ties = [] if done is None else [in_vmem(done)]
+    return pl.pallas_call(
+        functools.partial(join_kernel, len(blocks)),
+        out_shape=pltpu.VMEM(shape, blocks[0].dtype),
+        in_specs=[VMEM] * (len(ties) + len(blocks)),
+        out_specs=VMEM,
+        cost_estimate=cost(0, 4 * sum(b.size for b in blocks)),
+        compiler_params=limit(4),
+    )(*ties, *blocks)
+
+
+def dense_in_kernel(
+    owned, chunks, mine_ref, other_ref, dense_gate, dense_up, gate_ref, up_ref, hidden_ref, x_ref, *refs
+):
+    held, sems = refs[:-1], refs[-1]
+    copies = start_copies([(chunk_source(c, gate_ref, up_ref), ref) for c, ref in zip(chunks, held)], sems)
+    half = mine_ref.shape[0]
+    x_ref[0:half] = mine_ref[...]
+    x_ref[half : 2 * half] = other_ref[...]
+    hidden = swiglu_hidden(dot_t(x_ref[...], dense_gate[...]), dot_t(x_ref[...], dense_up[...]))
+    hidden_ref[0] = dot(swap_matrix(2 * half, owned, True), hidden).astype(jnp.bfloat16)
+    wait_copies(copies)
+
+
+def dense_in(owned, chunks, mine, other, dense_gate, dense_up, gate, up):
+    rows, width = 2 * mine.shape[0], mine.shape[1]
+    count = len(chunks)
+    hidden, x, *held = pl.pallas_call(
+        functools.partial(dense_in_kernel, owned, chunks),
+        out_shape=(
+            pltpu.VMEM((1, rows, dense_gate.shape[0]), jnp.bfloat16),
+            pltpu.VMEM((rows, width), jnp.bfloat16),
+            *chunk_shapes(count),
+        ),
+        in_specs=[VMEM] * 4 + [ANY] * 2,
+        out_specs=(VMEM,) * (2 + count),
+        scratch_shapes=[pltpu.SemaphoreType.DMA((max(count, 1),))],
+        cost_estimate=cost(4 * rows * dense_gate.size, 4 * dense_gate.size),
+        compiler_params=limit(4),
+    )(in_vmem(mine), other, in_vmem(dense_gate), in_vmem(dense_up), in_hbm(gate), in_hbm(up))
+    return hidden, x, held
+
+
+def expert_kernel(owned, there, x_ref, ids_ref, gates_ref, *refs):
+    ready, refs = refs[:there], refs[there:]
+    gate_ref, up_ref, down_ref, dense_ref, out_ref, dense_held, gate_sum, up_sum, hidden, ring, sems = refs
+    rows, units = gate_sum.shape
+    slots = ring.shape[0]
+    blocks = PER // 2
+    pieces = [[(chunk_source(c, gate_ref, up_ref), 0)] for c in range(there, 2 * PER)]
+    streamed = len(pieces)
+    for block in range(blocks):
+        for part in range(2):
+            held = down_ref.at[pl.ds(part * CHUNK, CHUNK), pl.ds(block * units, units)]
+            pieces.append([(held, 0)])
+    parts = [down_ref.at[pl.ds(part * CHUNK, CHUNK), pl.ds(blocks * units, CHUNK)] for part in range(2)]
+    pieces.append([(parts[0], 0), (parts[1], CHUNK)])
+    total = len(pieces)
+    found = {}
+    dense_copy = pltpu.make_async_copy(dense_ref, dense_held, sems.at[slots + 1])
+
+    def issue(n):
+        if n < total:
+            found[n] = []
+            for source, column in pieces[n]:
+                slot = ring.at[n % slots]
+                target = slot if len(pieces[n]) == 1 else slot.at[:, pl.ds(column, CHUNK)]
+                copy = pltpu.make_async_copy(source, target, sems.at[slots if column else n % slots])
+                copy.start()
+                found[n].append(copy)
+        elif n == total:
+            dense_copy.start()
+
+    def arrived(n):
+        wait_copies(found[n])
+        return ring.at[n % slots]
+
+    for n in range(slots):
+        issue(n)
+
+    begun = set()
+
+    def add(chunk, weights):
+        target = gate_sum if chunk < PER else up_sum
+        at = chunk % PER * CHUNK
+        product = dot(x_ref[:, at : at + CHUNK], weights[...])
+        target[...] = target[...] + product if chunk // PER in begun else product
+        begun.add(chunk // PER)
+
+    lead = max(there - streamed, 1)
+    for n in range(lead):
+        add(n, ready[n])
+    for n in range(max(there - lead, streamed)):
+        if n < streamed:
+            add(there + n, arrived(n))
+            issue(n + slots)
+        if lead + n < there:
+            add(lead + n, ready[lead + n])
+    hidden[...] = swiglu_hidden(gate_sum[...], up_sum[...])
+
+    expert = lax.axis_index("gx") * units // EH
+    weights = jnp.sum(jnp.where(ids_ref[...] == expert, gates_ref[...], 0.0), axis=0, keepdims=True)
+    token = lax.broadcasted_iota(jnp.int32, (rows, rows), 1)
+    scale = jnp.sum(jnp.where(token == tokens_at((rows, rows), 0, owned), weights, 0.0), axis=1, keepdims=True)
+
+    first, second = hidden[:, 0:CHUNK], hidden[:, CHUNK : 2 * CHUNK]
+    for block in range(blocks):
+        n = streamed + 2 * block
+        at = pl.ds(block * units, units)
+        out_ref[:, at] = dot(first, arrived(n)[...])
+        issue(n + slots)
+        out_ref[:, at] = scale * (out_ref[:, at] + dot(second, arrived(n + 1)[...]))
+        issue(n + 1 + slots)
+    last = arrived(total - 1)
+    both = dot(first, last[:, 0:CHUNK]) + dot(second, last[:, CHUNK : 2 * CHUNK])
+    out_ref[:, blocks * units :] = scale * both
+    dense_copy.wait()
+
+
+def expert_block(owned, x, ids, gates, ready, gate, up, down, dense_down):
+    rows, width = x.shape
+    units = gate.shape[1]
+    return pl.pallas_call(
+        functools.partial(expert_kernel, owned, len(ready)),
+        out_shape=(
+            pltpu.VMEM((rows, width), jnp.float32),
+            pltpu.VMEM(dense_down.shape, dense_down.dtype),
+        ),
+        in_specs=[VMEM] * (3 + len(ready)) + [ANY] * 4,
+        out_specs=(VMEM, VMEM),
+        scratch_shapes=[
+            pltpu.VMEM((rows, units), jnp.float32),
+            pltpu.VMEM((rows, units), jnp.float32),
+            pltpu.VMEM((rows, units), jnp.bfloat16),
+            pltpu.VMEM((SLOTS, CHUNK, units), jnp.bfloat16),
+            pltpu.SemaphoreType.DMA((SLOTS + 2,)),
+        ],
+        cost_estimate=cost(6 * rows * down.size, 4 * down.size),
+        compiler_params=limit(4 * SLOTS + 3),
+    )(
+        in_vmem(x), ids, gates, *[in_vmem(r) for r in ready],
+        in_hbm(gate), in_hbm(up), in_hbm(down), in_hbm(dense_down),
+    )
+
+
+def dense_out_kernel(owned, part_ref, b0, b1, b2, b3, down_ref, keep_ref, send_ref, held, joined, wide):
+    near, rows, units = b0.shape
+    half = rows // 2
+    columns, width = down_ref.shape[0], part_ref.shape[1]
+    own = lax.axis_index("gx")
+    for z, blocks in enumerate((b0, b1, b2, b3)):
+        held[z * near : (z + 1) * near] = blocks[...]
+    for j in range(4 * near):
+        joined[:, j * units : (j + 1) * units] = held[own ^ j]
+    dense_rows = dot(swap_matrix(rows, owned, False), joined[...]).astype(jnp.bfloat16)
+    wide[...] = jnp.zeros_like(wide)
+    wide[:, 0:columns] = dot_t(dense_rows, down_ref[...])
+    start = own * columns
+    base = jnp.minimum(start // 128 * 128, width - wide.shape[1])
+    moved = pltpu.roll(wide[...], start - base, 1)
+    at = pl.ds(pl.multiple_of(base, 128), wide.shape[1])
+    keep_ref[...] = part_ref[0:half]
+    send_ref[...] = part_ref[half:].astype(jnp.bfloat16)
+    keep_ref[:, at] += moved[:half]
+    send_ref[:, at] = (part_ref[half:, at] + moved[half:]).astype(jnp.bfloat16)
+
+
+def dense_out(owned, part, blocks, down):
+    near, rows, units = blocks[0].shape
+    columns, inner = down.shape
+    width = part.shape[1]
+    window = -(-(columns + 64) // 128) * 128 if columns % 64 == 0 else -(-(columns + 127) // 128) * 128
+    return pl.pallas_call(
+        functools.partial(dense_out_kernel, owned),
+        out_shape=(
+            jax.ShapeDtypeStruct((rows // 2, width), jnp.float32),
+            jax.ShapeDtypeStruct((rows // 2, width), jnp.bfloat16),
+        ),
+        in_specs=[VMEM] * 6,
+        out_specs=(VMEM, VMEM),
+        scratch_shapes=[
+            pltpu.VMEM((4 * near, rows, units), jnp.bfloat16),
+            pltpu.VMEM((rows, inner), jnp.bfloat16),
+            pltpu.VMEM((rows, window), jnp.float32),
+        ],
+        cost_estimate=cost(2 * rows * down.size, 2 * down.size),
+        compiler_params=limit(8),
+    )(in_vmem(part), *blocks, in_vmem(down))
+
+
+def four_by_two(
+    tokens,
+    route_ids,
+    route_gates,
+    dense_gate,
+    dense_up,
+    dense_down,
+    expert_gate,
+    expert_up,
+    expert_down,
+):
+    owned, width = tokens.shape
+    dense_gate, dense_up, dense_down = dense_gate.T, dense_up.T, dense_down.T
+
+    def swap(value, step):
+        return lax.ppermute(value, "gx", [(i, i ^ step) for i in range(16)])
+
+    ends = [sum(AHEAD[: n + 1]) for n in range(len(AHEAD))]
+    chunks = [range(end - count, end) for count, end in zip(AHEAD, ends)]
+    streams = (expert_gate, expert_up)
+    along_z = [swap(tokens, 4 * z) for z in (1, 2, 3)]
+    ready, done = fetch(None, chunks[0], *streams)
+    mine = join(done, tokens, *along_z)
+    along_x = swap(mine, 2)
+    more, done = fetch(done, chunks[1], *streams)
+    ready += more
+    mine = join(done, mine, along_x)
+    other = swap(mine, 1)
+    more, dense_gate, dense_up, _ = fetch(done, chunks[2], *streams, dense_gate, dense_up)
+    ready += more
+
+    block, x, more = dense_in(owned, chunks[3], mine, other, dense_gate, dense_up, *streams)
+    ready += more
+    block = join(None, block, swap(block, 1))
+    along_x = swap(block, 2)
+    if AHEAD[4]:
+        more, done = fetch(done, chunks[4], *streams)
+        ready += more
+        block = join(done, block, along_x)
+    else:
+        block = join(None, block, along_x)
+    blocks = [block] + [swap(block, 4 * z) for z in (1, 2, 3)]
+    part, dense_down = expert_block(
+        owned, x, route_ids.T, route_gates.T, ready, expert_gate, expert_up, expert_down, dense_down
+    )
+    keep, send = dense_out(owned, part, blocks, dense_down)
+
+    half = keep.shape[0] // 2
+    keep = keep + swap(send, 1).astype(jnp.float32)
+    keep = keep[:half] + swap(keep[half:].astype(jnp.bfloat16), 2).astype(jnp.float32)
+    rest = keep.astype(jnp.bfloat16)
+    total = tokens.astype(jnp.float32) + keep[:owned]
+    for z in (1, 2, 3):
+        total = total + swap(rest[z * owned : (z + 1) * owned], 4 * z).astype(jnp.float32)
+    return total.astype(jnp.bfloat16)
 
 
 def swiglu(row_block, w_gate, w_up, w_down):
@@ -13,7 +378,7 @@
     return jnp.dot(hidden, w_down, preferred_element_type=jnp.float32)
 
 
-def per_device(
+def any_size(
     tokens,
     route_ids,
     route_gates,
@@ -69,6 +434,13 @@
         P("gx", None),
     )
     out_specs = P(("groups", "gx"), None)
-    return jax.shard_map(
-        per_device, mesh=mesh, in_specs=in_specs, out_specs=out_specs, check_vma=False
-    )
+
+    def layer(tokens, *rest):
+        size = mesh.shape["gx"]
+        width, units = tokens.shape[1], rest[-3].shape[1] // size
+        fits = size == 16 and units == 2 * CHUNK and width == PER * CHUNK
+        body = four_by_two if fits else any_size
+        whole = jax.shard_map(body, mesh=mesh, in_specs=in_specs, out_specs=out_specs, check_vma=False)
+        return whole(tokens, *rest)
+
+    return layer

time: 170 us -> 70.9 us (0.42)
  matrix products: 43.5 us -> 0 us
  blocking collectives: 43.4 us -> 0 us
  waiting for transfers between devices: 54.6 us -> 14.3 us
  Pallas kernels: 0 us -> 36.9 us
  starting transfers between devices: 3.5 us -> 18.5 us
  between operations: 14.2 us -> 0.19 us
  local copies, waits for them, and re-layouts: 5.76 us -> 0.11 us
  other arithmetic: 5.13 us -> 0.76 us
    unnamed x2 -> x0, waiting for transfers between devices: 48.8 us -> none
    dot_general x5 -> x0, matrix products: 43.5 us -> none  [the longest x1 20.8 us: swiglu(): return jnp.dot(hidden, w_down, preferred_element_type=jnp.float32)]
    all_gather x2 -> x0, blocking collectives: 43.4 us -> none  [the longest x1 24.6 us: per_device(): gathered = lax.all_gather(tokens, 'gx', axis=0, tiled=True)]
    pallas_call x0 -> x10, Pallas kernels: none -> 36.9 us  [the longest x1 19.4 us: expert_block(): pl.pallas_call(functools.partial(expert_kernel, owned, len(ready)), out_s...]
    ppermute x0 -> x15, starting transfers between devices: none -> 18.5 us  [swap(): return lax.ppermute(value, 'gx', [(i, i ^ step) for i in range(16)])]
    ppermute x0 -> x15, waiting for transfers between devices: none -> 14.3 us  [swap(): return lax.ppermute(value, 'gx', [(i, i ^ step) for i in range(16)])]
    all_to_all x1 -> x0, waiting for transfers between devices: 5.72 us -> none  [per_device(): lax.all_to_all(dense_part, 'gx', split_axis=0, concat_axis=1, tiled=True)]
    all_to_all x1 -> x0, starting transfers between devices: 3.5 us -> none  [per_device(): lax.all_to_all(dense_part, 'gx', split_axis=0, concat_axis=1, tiled=True)]
  transfers between devices with their start and end apart: 2 -> 15, of which waited for: 2 -> 8; matrix products, arithmetic and copies ran while one was open for 7% -> 0% of each run, Pallas kernels for 0% -> 45%
where the time goes in v3:
time: 70.9 us; the launch traced here: 70.8 us
  Pallas kernels  36.9 us (52%)
  starting transfers between devices  18.5 us (26%)
  waiting for transfers between devices  14.3 us (20%)
  other arithmetic  0.76 us (1%)
    pallas_call x1, Pallas kernels, expert_block(): pl.pallas_call(functools.partial(expert_kernel, owned, len(ready)), out_s...  19.4 us
    ppermute x15, starting transfers between devices, swap(): return lax.ppermute(value, 'gx', [(i, i ^ step) for i in range(16)])  18.5 us
    ppermute x15, waiting for transfers between devices, swap(): return lax.ppermute(value, 'gx', [(i, i ^ step) for i in range(16)])  14.3 us
    pallas_call x3, Pallas kernels, fetch(): pl.pallas_call(functools.partial(fetch_kernel, chunks, len(wholes), tied)...  12.3 us
    pallas_call x1, Pallas kernels, dense_in(): pl.pallas_call(functools.partial(dense_in_kernel, owned, chunks), out_sha...  3.49 us
    pallas_call x1, Pallas kernels, dense_out(): pl.pallas_call(functools.partial(dense_out_kernel, owned), out_shape=(jax...  1.64 us
  transfers between devices with their start and end apart: 15, of which 8 were waited for; matrix products, arithmetic and copies ran while one was open for 0% of the time, Pallas kernels for 45%

profile of v3, /device:TPU:0, one launch (start us, length us, event | category | flops | bytes accessed | tf_op | source)
XLA Modules:
  0.0 70.8 jit_solution(10828174552816128522)
XLA Ops:
  0.0 4.0 %collective-permute-start.1 = (bf16[2,7168]{1,0:T(2,128)(2,1)}, bf16[2,7168]{1,0:T(2,128)(2,1)S(1)}, u32[]{:S(2)}, u32[]{:S(2)}) collective-permute-start(bf16[2,7168]{1,0:T(2,128)(2,1)} %refs_1_.6), channel_id=1, source_target_pairs={{0,8},{1,9},{2,10},{3,11},{4,12},{5,13},{6,14},{7,15},{8,0},{9,1},... | collective-permute-start | bytes 86024 | tf_op jit(solution)/shard_map/ppermute | solution.py:332
  4.0 1.6 %collective-permute-start = (bf16[2,7168]{1,0:T(2,128)(2,1)}, bf16[2,7168]{1,0:T(2,128)(2,1)S(1)}, u32[]{:S(2)}, u32[]{:S(2)}) collective-permute-start(bf16[2,7168]{1,0:T(2,128)(2,1)} %refs_1_.6), channel_id=1, source_target_pairs={{0,4},{1,5},{2,6},{3,7},{4,0},{5,1},{6,2},{7,3},{8,12},{9,13},{10,... | collective-permute-start | bytes 86024 | tf_op jit(solution)/shard_map/ppermute | solution.py:332
  5.6 4.7 %shard_map.91 = (bf16[1024,2048]{1,0:T(8,128)(2,1)S(1)}, bf16[1024,2048]{1,0:T(8,128)(2,1)S(1)}, bf16[1024,2048]{1,0:T(8,128)(2,1)S(1)}, f32[8,128]{1,0:T(8,128)S(1)}) custom-call(bf16[7168,2048]{1,0:T(8,128)(2,1)} %refs_7_.1, bf16[7168,2048]{1,0:T(8,128)(2,1)} %refs_8_.1), custom_call_target="tpu_custom_call" | custom-call | bytes 12582912 | tf_op jit(solution)/shard_map/pallas_call | solution.py:100
  10.3 1.2 %collective-permute-done.2.refs_4_ = bf16[2,7168]{1,0:T(2,128)(2,1)S(1)} collective-permute-done((bf16[2,7168]{1,0:T(2,128)(2,1)}, bf16[2,7168]{1,0:T(2,128)(2,1)S(1)}, u32[]{:S(2)}, u32[]{:S(2)}) %collective-permute-start.2) | collective-permute-done | bytes 28704 | tf_op jit(solution)/shard_map/ppermute | solution.py:332
  11.5 0.1 shard_map.93.refs_1_
  11.6 1.6 %collective-permute-start.3 = (bf16[8,7168]{1,0:T(8,128)(2,1)S(1)}, bf16[8,7168]{1,0:T(8,128)(2,1)S(1)}, u32[]{:S(2)}, u32[]{:S(2)}) collective-permute-start(bf16[8,7168]{1,0:T(8,128)(2,1)S(1)} %shard_map.93.refs_1_), channel_id=1, source_target_pairs={{0,2},{1,3},{2,0},{3,1},{4,6},{5,7},{6,4},{7,5},{8,10},{9,11},{10,... | collective-permute-start | bytes 344072 | tf_op jit(solution)/shard_map/ppermute | solution.py:332
  13.1 3.5 %shard_map.92 = (bf16[1024,2048]{1,0:T(8,128)(2,1)S(1)}, bf16[1024,2048]{1,0:T(8,128)(2,1)S(1)}, f32[8,128]{1,0:T(8,128)S(1)}) custom-call(f32[8,128]{1,0:T(8,128)S(1)} %get-tuple-element.22.refs_0_, bf16[7168,2048]{1,0:T(8,128)(2,1)} %refs_7_.1, bf16[7168,2048]{1,0:T(8,128)(2,1)} %refs_8_.1), custom_call_target="tpu_custom_call" | custom-call | bytes 8388608 | tf_op jit(solution)/shard_map/pallas_call | solution.py:100
  16.7 0.1 collective-permute-start.4
  16.7 4.2 %shard_map.95 = (bf16[304,7168]{1,0:T(8,128)(2,1)S(1)}, bf16[304,7168]{1,0:T(8,128)(2,1)S(1)}, f32[8,128]{1,0:T(8,128)}) custom-call(f32[8,128]{1,0:T(8,128)S(1)} %get-tuple-element.23.refs_0_, bf16[7168,2048]{1,0:T(8,128)(2,1)} %refs_7_.1, bf16[7168,2048]{1,0:T(8,128)(2,1)} %refs_8_.1, bf16[304,7168]{1,0:T(8,128)(2,1)} %bitcast.7, bf16[304,7168]{1,0:T(8,128)(2,1)} %bitcast.8), custom_call_target="tpu_custom_call" | custom-call | bytes 8716288 | tf_op jit(solution)/shard_map/pallas_call | solution.py:100
  20.9 0.0 copy-start.1
  20.9 0.0 copy-start.2
  20.9 3.5 %shard_map.96 = (bf16[1,32,304]{2,1,0:T(8,128)(2,1)S(1)}, bf16[32,7168]{1,0:T(8,128)(2,1)S(1)}, bf16[1024,2048]{1,0:T(8,128)(2,1)S(1)}, bf16[1024,2048]{1,0:T(8,128)(2,1)S(1)}) custom-call(bf16[16,7168]{1,0:T(8,128)(2,1)S(1)} %shard_map.94.mine_ref, bf16[16,7168]{1,0:T(8,128)(2,1)S(1)} %collective-permute-done.4.other_ref, ...), custom_call_target="tpu_custom_call" | custom-call | flops 278921216 | bytes 8716288 | tf_op jit(solution)/shard_map/pallas_call | solution.py:154
  24.4 0.6 collective-permute-start.5
  25.0 0.8 %collective-permute-done.5.refs_1_ = bf16[1,32,304]{2,1,0:T(8,128)(2,1)S(1)} collective-permute-done((bf16[1,32,304]{2,1,0:T(8,128)(2,1)S(1)}, bf16[1,32,304]{2,1,0:T(8,128)(2,1)S(1)}, u32[]{:S(2)}, u32[]{:S(2)}) %collective-permute-start.5) | collective-permute-done | bytes 19488 | tf_op jit(solution)/shard_map/ppermute | solution.py:332
  25.9 1.3 %collective-permute-start.6 = (bf16[2,32,304]{2,1,0:T(8,128)(2,1)S(1)}, bf16[2,32,304]{2,1,0:T(8,128)(2,1)S(1)}, u32[]{:S(2)}, u32[]{:S(2)}) collective-permute-start(bf16[2,32,304]{2,1,0:T(8,128)(2,1)S(1)} %shard_map.98.refs_0_), channel_id=1, source_target_pairs={{0,2},{1,3},{2,0},{3,1},{4,6},{5,7},{6,4},{7,5},{8,10},{9,11},{10,... | collective-permute-start | bytes 116744 | tf_op jit(solution)/shard_map/ppermute | solution.py:332
  27.1 2.8 %collective-permute-done.6.refs_1_ = bf16[2,32,304]{2,1,0:T(8,128)(2,1)S(1)} collective-permute-done((bf16[2,32,304]{2,1,0:T(8,128)(2,1)S(1)}, bf16[2,32,304]{2,1,0:T(8,128)(2,1)S(1)}, u32[]{:S(2)}, u32[]{:S(2)}) %collective-permute-start.6) | collective-permute-done | bytes 38944 | tf_op jit(solution)/shard_map/ppermute | solution.py:332
  30.0 2.7 %collective-permute-start.9 = (bf16[4,32,304]{2,1,0:T(8,128)(2,1)S(1)}, bf16[4,32,304]{2,1,0:T(8,128)(2,1)S(1)}, u32[]{:S(2)}, u32[]{:S(2)}) collective-permute-start(bf16[4,32,304]{2,1,0:T(8,128)(2,1)S(1)} %shard_map.99.b0), channel_id=1, source_target_pairs={{0,12},{1,13},{2,14},{3,15},{4,8},{5,9},{6,10},{7,11},{8,4},{9,5},... | collective-permute-start | bytes 233480 | tf_op jit(solution)/shard_map/ppermute | solution.py:332
  32.7 1.7 %collective-permute-start.7 = (bf16[4,32,304]{2,1,0:T(8,128)(2,1)S(1)}, bf16[4,32,304]{2,1,0:T(8,128)(2,1)S(1)}, u32[]{:S(2)}, u32[]{:S(2)}) collective-permute-start(bf16[4,32,304]{2,1,0:T(8,128)(2,1)S(1)} %shard_map.99.b0), channel_id=1, source_target_pairs={{0,4},{1,5},{2,6},{3,7},{4,0},{5,1},{6,2},{7,3},{8,12},{9,13},{10,... | collective-permute-start | bytes 233480 | tf_op jit(solution)/shard_map/ppermute | solution.py:332
  34.4 19.4 %shard_map.97 = (f32[32,7168]{1,0:T(8,128)S(1)}, bf16[448,4864]{1,0:T(8,128)(2,1)S(1)}) custom-call(bf16[32,7168]{1,0:T(8,128)(2,1)S(1)} %get-tuple-element.26.x_ref, s32[2,32]{1,0:T(2,128)S(1)} %bitcast.5, f32[2,32]{1,0:T(2,128)S(1)} %bitcast.6, bf16[1024,2048]{1,0:T(8,128)(2,1)S(1)} %get-tuple-element.27.refs_0_, ...), custom_call_target="tpu_custom_call" | custom-call | flops 2818572288 | bytes 58720256 | tf_op jit(solution)/shard_map/pallas_call | solution.py:249
  53.8 1.6 %shard_map.100 = (f32[16,7168]{1,0:T(8,128)S(1)}, bf16[16,7168]{1,0:T(8,128)(2,1)S(1)}) custom-call(f32[32,7168]{1,0:T(8,128)S(1)} %get-tuple-element.34.part_ref, bf16[4,32,304]{2,1,0:T(8,128)(2,1)S(1)} %shard_map.99.b0, bf16[4,32,304]{2,1,0:T(8,128)(2,1)S(1)} %collective-permute-done.7.b1, bf16[4,32,304]{2,1,0:T(8,128)(2,1)S(1)} %collective-permute-done.8.b2, ...), custom_call_target="tpu_custom_call" | custom-call | flops 139460608 | bytes 4358144 | tf_op jit(solution)/shard_map/pallas_call | solution.py:299
  55.5 0.1 collective-permute-start.10
  55.6 1.5 %collective-permute-done.10 = bf16[16,7168]{1,0:T(8,128)(2,1)S(1)} collective-permute-done((bf16[16,7168]{1,0:T(8,128)(2,1)S(1)}, bf16[16,7168]{1,0:T(8,128)(2,1)S(1)}, u32[]{:S(2)}, u32[]{:S(2)}) %collective-permute-start.10) | collective-permute-done | bytes 229408 | tf_op jit(solution)/shard_map/ppermute | solution.py:332
  57.1 1.3 %collective-permute-start.11 = (bf16[8,7168]{1,0:T(8,128)(2,1)S(1)}, bf16[8,7168]{1,0:T(8,128)(2,1)S(1)}, u32[]{:S(2)}, u32[]{:S(2)}) collective-permute-start(bf16[8,7168]{1,0:T(8,128)(2,1)S(1)} %slice.42), channel_id=1, source_target_pairs={{0,2},{1,3},{2,0},{3,1},{4,6},{5,7},{6,4},{7,5},{8,10},{9,11},{10,... | collective-permute-start | bytes 344072 | tf_op jit(solution)/shard_map/ppermute | solution.py:332
  58.5 3.9 %collective-permute-done.11 = bf16[8,7168]{1,0:T(8,128)(2,1)S(1)} collective-permute-done((bf16[8,7168]{1,0:T(8,128)(2,1)S(1)}, bf16[8,7168]{1,0:T(8,128)(2,1)S(1)}, u32[]{:S(2)}, u32[]{:S(2)}) %collective-permute-start.11) | collective-permute-done | bytes 114720 | tf_op jit(solution)/shard_map/ppermute | solution.py:332
  62.4 0.1 fusion.5
  62.5 0.4 collective-permute-start.12
  62.9 2.4 %collective-permute-start.14 = (bf16[2,7168]{1,0:T(2,128)(2,1)S(1)}, bf16[2,7168]{1,0:T(2,128)(2,1)S(1)}, u32[]{:S(2)}, u32[]{:S(2)}) collective-permute-start(bf16[2,7168]{1,0:T(2,128)(2,1)S(1)} %get-tuple-element.42), channel_id=1, source_target_pairs={{0,12},{1,13},{2,14},{3,15},{4,8},{5,9},{6,10},{7,11},{8,4},{9,5},... | collective-permute-start | bytes 86024 | tf_op jit(solution)/shard_map/ppermute | solution.py:332
  65.3 0.7 %collective-permute-start.13 = (bf16[2,7168]{1,0:T(2,128)(2,1)S(1)}, bf16[2,7168]{1,0:T(2,128)(2,1)S(1)}, u32[]{:S(2)}, u32[]{:S(2)}) collective-permute-start(bf16[2,7168]{1,0:T(2,128)(2,1)S(1)} %get-tuple-element.43), channel_id=1, source_target_pairs={{0,8},{1,9},{2,10},{3,11},{4,12},{5,13},{6,14},{7,15},{8,0},{9,1},... | collective-permute-start | bytes 86024 | tf_op jit(solution)/shard_map/ppermute | solution.py:332
  66.0 0.4 collective-permute-done.12
  66.4 2.3 %collective-permute-done.14 = bf16[2,7168]{1,0:T(2,128)(2,1)S(1)} collective-permute-done((bf16[2,7168]{1,0:T(2,128)(2,1)S(1)}, bf16[2,7168]{1,0:T(2,128)(2,1)S(1)}, u32[]{:S(2)}, u32[]{:S(2)}) %collective-permute-start.14) | collective-permute-done | bytes 28704 | tf_op jit(solution)/shard_map/ppermute | solution.py:332
  68.7 1.3 %collective-permute-done.13 = bf16[2,7168]{1,0:T(2,128)(2,1)S(1)} collective-permute-done((bf16[2,7168]{1,0:T(2,128)(2,1)S(1)}, bf16[2,7168]{1,0:T(2,128)(2,1)S(1)}, u32[]{:S(2)}, u32[]{:S(2)}) %collective-permute-start.13) | collective-permute-done | bytes 28704 | tf_op jit(solution)/shard_map/ppermute | solution.py:332
  70.1 0.7 fusion.3
  (19 shorter events, 0.2 us)
Async XLA Ops:
  0.0 11.5 %copy-start = (bf16[2,7168]{1,0:T(2,128)(2,1)S(1)}, bf16[2,7168]{1,0:T(2,128)(2,1)}, u32[]{:S(2)}) copy-start(bf16[2,7168]{1,0:T(2,128)(2,1)} %refs_1_.6) | copy-start | bytes 86020
  0.0 10.3 %collective-permute-start.1 = (bf16[2,7168]{1,0:T(2,128)(2,1)}, bf16[2,7168]{1,0:T(2,128)(2,1)S(1)}, u32[]{:S(2)}, u32[]{:S(2)}) collective-permute-start(bf16[2,7168]{1,0:T(2,128)(2,1)} %refs_1_.6), channel_id=1, source_target_pairs={{0,8},{1,9},{2,10},{3,11},{4,12},{5,13},{6,14},{7,15},{8,0},{9,1},... | collective-permute-start | bytes 86024 | tf_op jit(solution)/shard_map/ppermute | solution.py:332
  4.0 6.3 %collective-permute-start = (bf16[2,7168]{1,0:T(2,128)(2,1)}, bf16[2,7168]{1,0:T(2,128)(2,1)S(1)}, u32[]{:S(2)}, u32[]{:S(2)}) collective-permute-start(bf16[2,7168]{1,0:T(2,128)(2,1)} %refs_1_.6), channel_id=1, source_target_pairs={{0,4},{1,5},{2,6},{3,7},{4,0},{5,1},{6,2},{7,3},{8,12},{9,13},{10,... | collective-permute-start | bytes 86024 | tf_op jit(solution)/shard_map/ppermute | solution.py:332
  5.6 5.9 %collective-permute-start.2 = (bf16[2,7168]{1,0:T(2,128)(2,1)}, bf16[2,7168]{1,0:T(2,128)(2,1)S(1)}, u32[]{:S(2)}, u32[]{:S(2)}) collective-permute-start(bf16[2,7168]{1,0:T(2,128)(2,1)} %refs_1_.6), channel_id=1, source_target_pairs={{0,12},{1,13},{2,14},{3,15},{4,8},{5,9},{6,10},{7,11},{8,4},{9,5},... | collective-permute-start | bytes 86024 | tf_op jit(solution)/shard_map/ppermute | solution.py:332
  11.6 5.1 %collective-permute-start.3 = (bf16[8,7168]{1,0:T(8,128)(2,1)S(1)}, bf16[8,7168]{1,0:T(8,128)(2,1)S(1)}, u32[]{:S(2)}, u32[]{:S(2)}) collective-permute-start(bf16[8,7168]{1,0:T(8,128)(2,1)S(1)} %shard_map.93.refs_1_), channel_id=1, source_target_pairs={{0,2},{1,3},{2,0},{3,1},{4,6},{5,7},{6,4},{7,5},{8,10},{9,11},{10,... | collective-permute-start | bytes 344072 | tf_op jit(solution)/shard_map/ppermute | solution.py:332
  16.7 4.3 %collective-permute-start.4 = (bf16[16,7168]{1,0:T(8,128)(2,1)S(1)}, bf16[16,7168]{1,0:T(8,128)(2,1)S(1)}, u32[]{:S(2)}, u32[]{:S(2)}) collective-permute-start(bf16[16,7168]{1,0:T(8,128)(2,1)S(1)} %shard_map.94.mine_ref), channel_id=1, source_target_pairs={{0,1},{1,0},{2,3},{3,2},{4,5},{5,4},{6,7},{7,6},{8,9},{9,8},{10,11... | collective-permute-start | bytes 688136 | tf_op jit(solution)/shard_map/ppermute | solution.py:332
  20.9 13.5 %copy-start.1 = (s32[32,2]{0,1:T(2,128)S(1)}, s32[32,2]{0,1:T(2,128)}, u32[]{:S(2)}) copy-start(s32[32,2]{0,1:T(2,128)} %param.10) | copy-start | bytes 772
  20.9 13.5 %copy-start.2 = (f32[32,2]{0,1:T(2,128)S(1)}, f32[32,2]{0,1:T(2,128)}, u32[]{:S(2)}) copy-start(f32[32,2]{0,1:T(2,128)} %param.11) | copy-start | bytes 772
  24.4 1.4 %collective-permute-start.5 = (bf16[1,32,304]{2,1,0:T(8,128)(2,1)S(1)}, bf16[1,32,304]{2,1,0:T(8,128)(2,1)S(1)}, u32[]{:S(2)}, u32[]{:S(2)}) collective-permute-start(bf16[1,32,304]{2,1,0:T(8,128)(2,1)S(1)} %get-tuple-element.35.refs_0_), channel_id=1, source_target_pairs={{0,1},{1,0},{2,3},{3,2},{4,5},{5,4},{6,7},{7,6},{8,9},{9,8},{10,11... | collective-permute-start | bytes 58376 | tf_op jit(solution)/shard_map/ppermute | solution.py:332
  25.9 4.1 %collective-permute-start.6 = (bf16[2,32,304]{2,1,0:T(8,128)(2,1)S(1)}, bf16[2,32,304]{2,1,0:T(8,128)(2,1)S(1)}, u32[]{:S(2)}, u32[]{:S(2)}) collective-permute-start(bf16[2,32,304]{2,1,0:T(8,128)(2,1)S(1)} %shard_map.98.refs_0_), channel_id=1, source_target_pairs={{0,2},{1,3},{2,0},{3,1},{4,6},{5,7},{6,4},{7,5},{8,10},{9,11},{10,... | collective-permute-start | bytes 116744 | tf_op jit(solution)/shard_map/ppermute | solution.py:332
  30.0 23.8 %collective-permute-start.9 = (bf16[4,32,304]{2,1,0:T(8,128)(2,1)S(1)}, bf16[4,32,304]{2,1,0:T(8,128)(2,1)S(1)}, u32[]{:S(2)}, u32[]{:S(2)}) collective-permute-start(bf16[4,32,304]{2,1,0:T(8,128)(2,1)S(1)} %shard_map.99.b0), channel_id=1, source_target_pairs={{0,12},{1,13},{2,14},{3,15},{4,8},{5,9},{6,10},{7,11},{8,4},{9,5},... | collective-permute-start | bytes 233480 | tf_op jit(solution)/shard_map/ppermute | solution.py:332
  32.7 21.1 %collective-permute-start.8 = (bf16[4,32,304]{2,1,0:T(8,128)(2,1)S(1)}, bf16[4,32,304]{2,1,0:T(8,128)(2,1)S(1)}, u32[]{:S(2)}, u32[]{:S(2)}) collective-permute-start(bf16[4,32,304]{2,1,0:T(8,128)(2,1)S(1)} %shard_map.99.b0), channel_id=1, source_target_pairs={{0,8},{1,9},{2,10},{3,11},{4,12},{5,13},{6,14},{7,15},{8,0},{9,1},... | collective-permute-start | bytes 233480 | tf_op jit(solution)/shard_map/ppermute | solution.py:332
  32.7 21.1 %collective-permute-start.7 = (bf16[4,32,304]{2,1,0:T(8,128)(2,1)S(1)}, bf16[4,32,304]{2,1,0:T(8,128)(2,1)S(1)}, u32[]{:S(2)}, u32[]{:S(2)}) collective-permute-start(bf16[4,32,304]{2,1,0:T(8,128)(2,1)S(1)} %shard_map.99.b0), channel_id=1, source_target_pairs={{0,4},{1,5},{2,6},{3,7},{4,0},{5,1},{6,2},{7,3},{8,12},{9,13},{10,... | collective-permute-start | bytes 233480 | tf_op jit(solution)/shard_map/ppermute | solution.py:332
  55.5 1.6 %collective-permute-start.10 = (bf16[16,7168]{1,0:T(8,128)(2,1)S(1)}, bf16[16,7168]{1,0:T(8,128)(2,1)S(1)}, u32[]{:S(2)}, u32[]{:S(2)}) collective-permute-start(bf16[16,7168]{1,0:T(8,128)(2,1)S(1)} %get-tuple-element.38), channel_id=1, source_target_pairs={{0,1},{1,0},{2,3},{3,2},{4,5},{5,4},{6,7},{7,6},{8,9},{9,8},{10,11... | collective-permute-start | bytes 688136 | tf_op jit(solution)/shard_map/ppermute | solution.py:332
  57.1 5.3 %collective-permute-start.11 = (bf16[8,7168]{1,0:T(8,128)(2,1)S(1)}, bf16[8,7168]{1,0:T(8,128)(2,1)S(1)}, u32[]{:S(2)}, u32[]{:S(2)}) collective-permute-start(bf16[8,7168]{1,0:T(8,128)(2,1)S(1)} %slice.42), channel_id=1, source_target_pairs={{0,2},{1,3},{2,0},{3,1},{4,6},{5,7},{6,4},{7,5},{8,10},{9,11},{10,... | collective-permute-start | bytes 344072 | tf_op jit(solution)/shard_map/ppermute | solution.py:332
  62.5 3.9 %collective-permute-start.12 = (bf16[2,7168]{1,0:T(2,128)(2,1)S(1)}, bf16[2,7168]{1,0:T(2,128)(2,1)S(1)}, u32[]{:S(2)}, u32[]{:S(2)}) collective-permute-start(bf16[2,7168]{1,0:T(2,128)(2,1)S(1)} %get-tuple-element.41), channel_id=1, source_target_pairs={{0,4},{1,5},{2,6},{3,7},{4,0},{5,1},{6,2},{7,3},{8,12},{9,13},{10,... | collective-permute-start | bytes 86024 | tf_op jit(solution)/shard_map/ppermute | solution.py:332
  62.9 5.9 %collective-permute-start.14 = (bf16[2,7168]{1,0:T(2,128)(2,1)S(1)}, bf16[2,7168]{1,0:T(2,128)(2,1)S(1)}, u32[]{:S(2)}, u32[]{:S(2)}) collective-permute-start(bf16[2,7168]{1,0:T(2,128)(2,1)S(1)} %get-tuple-element.42), channel_id=1, source_target_pairs={{0,12},{1,13},{2,14},{3,15},{4,8},{5,9},{6,10},{7,11},{8,4},{9,5},... | collective-permute-start | bytes 86024 | tf_op jit(solution)/shard_map/ppermute | solution.py:332
  65.3 4.8 %collective-permute-start.13 = (bf16[2,7168]{1,0:T(2,128)(2,1)S(1)}, bf16[2,7168]{1,0:T(2,128)(2,1)S(1)}, u32[]{:S(2)}, u32[]{:S(2)}) collective-permute-start(bf16[2,7168]{1,0:T(2,128)(2,1)S(1)} %get-tuple-element.43), channel_id=1, source_target_pairs={{0,8},{1,9},{2,10},{3,11},{4,12},{5,13},{6,14},{7,15},{8,0},{9,1},... | collective-permute-start | bytes 86024 | tf_op jit(solution)/shard_map/ppermute | solution.py:332

commit v4 on v3

--- a/solution.py
+++ b/solution.py
@@ -11,7 +11,7 @@
 CHUNK = 1024
 PER = 7
 SLOTS = 4
-AHEAD = (3, 2, 0, 2, 0)
+AHEAD = (3, 1, 0, 1, 2)
 MIB = 1 << 20
 
 VMEM = pl.BlockSpec(memory_space=pltpu.VMEM)
@@ -335,26 +335,26 @@
     chunks = [range(end - count, end) for count, end in zip(AHEAD, ends)]
     streams = (expert_gate, expert_up)
     along_z = [swap(tokens, 4 * z) for z in (1, 2, 3)]
-    ready, done = fetch(None, chunks[0], *streams)
+    ready, dense_gate, done = fetch(None, chunks[0], *streams, dense_gate)
     mine = join(done, tokens, *along_z)
     along_x = swap(mine, 2)
-    more, done = fetch(done, chunks[1], *streams)
+    more, dense_up, done = fetch(done, chunks[1], *streams, dense_up)
     ready += more
     mine = join(done, mine, along_x)
     other = swap(mine, 1)
-    more, dense_gate, dense_up, _ = fetch(done, chunks[2], *streams, dense_gate, dense_up)
-    ready += more
+    if AHEAD[2]:
+        more, _ = fetch(done, chunks[2], *streams)
+        ready += more
 
     block, x, more = dense_in(owned, chunks[3], mine, other, dense_gate, dense_up, *streams)
     ready += more
-    block = join(None, block, swap(block, 1))
-    along_x = swap(block, 2)
+    near = [block] + [swap(block, step) for step in (1, 2, 3)]
     if AHEAD[4]:
-        more, done = fetch(done, chunks[4], *streams)
+        more, done = fetch(block, chunks[4], *streams)
         ready += more
-        block = join(done, block, along_x)
     else:
-        block = join(None, block, along_x)
+        done = None
+    block = join(done, *near)
     blocks = [block] + [swap(block, 4 * z) for z in (1, 2, 3)]
     part, dense_down = expert_block(
         owned, x, route_ids.T, route_gates.T, ready, expert_gate, expert_up, expert_down, dense_down

time: 70.9 us -> 68.4 us (0.965)
  waiting for transfers between devices: 14.3 us -> 10.9 us
  starting transfers between devices: 18.5 us -> 19.7 us
    ppermute x15 -> x16, waiting for transfers between devices: 14.3 us -> 10.9 us  [swap(): return lax.ppermute(value, 'gx', [(i, i ^ step) for i in range(16)])]
    ppermute x15 -> x16, starting transfers between devices: 18.5 us -> 19.7 us  [swap(): return lax.ppermute(value, 'gx', [(i, i ^ step) for i in range(16)])]
    pallas_call x1, Pallas kernels: 3.49 us -> 2.51 us  [dense_in(): pl.pallas_call(functools.partial(dense_in_kernel, owned, chunks), out_sha...]
  transfers between devices with their start and end apart: 15 -> 16, of which waited for: 8 -> 5; matrix products, arithmetic and copies ran while one was open for 0% -> 0% of each run, Pallas kernels for 45% -> 47%
where the time goes in v4:
time: 68.4 us; the launch traced here: 68.2 us
  Pallas kernels  36.6 us (54%)
  starting transfers between devices  19.7 us (29%)
  waiting for transfers between devices  10.9 us (16%)
  other arithmetic  0.77 us (1%)
    ppermute x16, starting transfers between devices, swap(): return lax.ppermute(value, 'gx', [(i, i ^ step) for i in range(16)])  19.7 us
    pallas_call x1, Pallas kernels, expert_block(): pl.pallas_call(functools.partial(expert_kernel, owned, len(ready)), out_s...  19.4 us
    pallas_call x3, Pallas kernels, fetch(): pl.pallas_call(functools.partial(fetch_kernel, chunks, len(wholes), tied)...  13 us
    ppermute x16, waiting for transfers between devices, swap(): return lax.ppermute(value, 'gx', [(i, i ^ step) for i in range(16)])  10.9 us
    pallas_call x1, Pallas kernels, dense_in(): pl.pallas_call(functools.partial(dense_in_kernel, owned, chunks), out_sha...  2.51 us
    pallas_call x1, Pallas kernels, dense_out(): pl.pallas_call(functools.partial(dense_out_kernel, owned), out_shape=(jax...  1.64 us
  transfers between devices with their start and end apart: 16, of which 5 were waited for; matrix products, arithmetic and copies ran while one was open for 0% of the time, Pallas kernels for 47%

profile of v4, /device:TPU:0, one launch (start us, length us, event | category | flops | bytes accessed | tf_op | source)
XLA Modules:
  0.0 68.2 jit_solution(9472088491945546568)
XLA Ops:
  0.0 3.0 %collective-permute-start = (bf16[2,7168]{1,0:T(2,128)(2,1)}, bf16[2,7168]{1,0:T(2,128)(2,1)S(1)}, u32[]{:S(2)}, u32[]{:S(2)}) collective-permute-start(bf16[2,7168]{1,0:T(2,128)(2,1)} %refs_1_.6), channel_id=1, source_target_pairs={{0,4},{1,5},{2,6},{3,7},{4,0},{5,1},{6,2},{7,3},{8,12},{9,13},{10,... | collective-permute-start | bytes 86024 | tf_op jit(solution)/shard_map/ppermute | solution.py:332
  3.0 2.6 %collective-permute-start.1 = (bf16[2,7168]{1,0:T(2,128)(2,1)}, bf16[2,7168]{1,0:T(2,128)(2,1)S(1)}, u32[]{:S(2)}, u32[]{:S(2)}) collective-permute-start(bf16[2,7168]{1,0:T(2,128)(2,1)} %refs_1_.6), channel_id=1, source_target_pairs={{0,8},{1,9},{2,10},{3,11},{4,12},{5,13},{6,14},{7,15},{8,0},{9,1},... | collective-permute-start | bytes 86024 | tf_op jit(solution)/shard_map/ppermute | solution.py:332
  5.6 5.9 %shard_map.91 = (bf16[1024,2048]{1,0:T(8,128)(2,1)S(1)}, bf16[1024,2048]{1,0:T(8,128)(2,1)S(1)}, bf16[1024,2048]{1,0:T(8,128)(2,1)S(1)}, bf16[304,7168]{1,0:T(8,128)(2,1)S(1)}, f32[8,128]{1,0:T(8,128)S(1)}) custom-call(bf16[7168,2048]{1,0:T(8,128)(2,1)} %refs_7_.1, bf16[7168,2048]{1,0:T(8,128)(2,1)} %refs_8_.1, bf16[304,7168]{1,0:T(8,128)(2,1)} %bitcast.8), custom_call_target="tpu_custom_call" | custom-call | bytes 16941056 | tf_op jit(solution)/shard_map/pallas_call | solution.py:100
  11.6 0.0 collective-permute-done.refs_2_
  11.6 0.1 shard_map.93.refs_1_
  11.7 1.8 %collective-permute-start.3 = (bf16[8,7168]{1,0:T(8,128)(2,1)S(1)}, bf16[8,7168]{1,0:T(8,128)(2,1)S(1)}, u32[]{:S(2)}, u32[]{:S(2)}) collective-permute-start(bf16[8,7168]{1,0:T(8,128)(2,1)S(1)} %shard_map.93.refs_1_), channel_id=1, source_target_pairs={{0,2},{1,3},{2,0},{3,1},{4,6},{5,7},{6,4},{7,5},{8,10},{9,11},{10,... | collective-permute-start | bytes 344072 | tf_op jit(solution)/shard_map/ppermute | solution.py:332
  13.5 3.5 %shard_map.92 = (bf16[1024,2048]{1,0:T(8,128)(2,1)S(1)}, bf16[304,7168]{1,0:T(8,128)(2,1)S(1)}, f32[8,128]{1,0:T(8,128)S(1)}) custom-call(f32[8,128]{1,0:T(8,128)S(1)} %get-tuple-element.23.refs_0_, bf16[7168,2048]{1,0:T(8,128)(2,1)} %refs_7_.1, bf16[7168,2048]{1,0:T(8,128)(2,1)} %refs_8_.1, bf16[304,7168]{1,0:T(8,128)(2,1)} %bitcast.7), custom_call_target="tpu_custom_call" | custom-call | bytes 8552448 | tf_op jit(solution)/shard_map/pallas_call | solution.py:100
  17.0 0.1 collective-permute-start.4
  17.1 1.5 %collective-permute-done.4.other_ref = bf16[16,7168]{1,0:T(8,128)(2,1)S(1)} collective-permute-done((bf16[16,7168]{1,0:T(8,128)(2,1)S(1)}, bf16[16,7168]{1,0:T(8,128)(2,1)S(1)}, u32[]{:S(2)}, u32[]{:S(2)}) %collective-permute-start.4) | collective-permute-done | bytes 229408 | tf_op jit(solution)/shard_map/ppermute | solution.py:332
  18.6 2.5 %shard_map.95 = (bf16[1,32,304]{2,1,0:T(8,128)(2,1)S(1)}, bf16[32,7168]{1,0:T(8,128)(2,1)S(1)}, bf16[1024,2048]{1,0:T(8,128)(2,1)S(1)}) custom-call(bf16[16,7168]{1,0:T(8,128)(2,1)S(1)} %shard_map.94.mine_ref, bf16[16,7168]{1,0:T(8,128)(2,1)S(1)} %collective-permute-done.4.other_ref, bf16[304,7168]{1,0:T(8,128)(2,1)S(1)} %get-tuple-element.25.dense_gate, ...), custom_call_target="tpu_custom_call" | custom-call | flops 278921216 | bytes 8716288 | tf_op jit(solution)/shard_map/pallas_call | solution.py:154
  21.1 0.0 copy-start.1
  21.1 0.0 copy-start.2
  21.1 0.2 collective-permute-start.5
  21.3 1.3 %collective-permute-start.6 = (bf16[1,32,304]{2,1,0:T(8,128)(2,1)S(1)}, bf16[1,32,304]{2,1,0:T(8,128)(2,1)S(1)}, u32[]{:S(2)}, u32[]{:S(2)}) collective-permute-start(bf16[1,32,304]{2,1,0:T(8,128)(2,1)S(1)} %get-tuple-element.33.refs_0_.refs_1_), channel_id=1, source_target_pairs={{0,2},{1,3},{2,0},{3,1},{4,6},{5,7},{6,4},{7,5},{8,10},{9,11},{10,... | collective-permute-start | bytes 58376 | tf_op jit(solution)/shard_map/ppermute | solution.py:332
  22.6 0.5 collective-permute-start.7
  23.1 3.5 %shard_map.96 = (bf16[1024,2048]{1,0:T(8,128)(2,1)S(1)}, bf16[1024,2048]{1,0:T(8,128)(2,1)S(1)}, f32[8,128]{1,0:T(8,128)S(1)}) custom-call(bf16[1,32,304]{2,1,0:T(8,128)(2,1)S(1)} %get-tuple-element.33.refs_0_.refs_1_, bf16[7168,2048]{1,0:T(8,128)(2,1)} %refs_7_.1, bf16[7168,2048]{1,0:T(8,128)(2,1)} %refs_8_.1), custom_call_target="tpu_custom_call" | custom-call | bytes 8388608 | tf_op jit(solution)/shard_map/pallas_call | solution.py:100
  26.5 0.0 collective-permute-done.5.refs_2_
  26.6 0.7 %collective-permute-start.8 = (bf16[4,32,304]{2,1,0:T(8,128)(2,1)S(1)}, bf16[4,32,304]{2,1,0:T(8,128)(2,1)S(1)}, u32[]{:S(2)}, u32[]{:S(2)}) collective-permute-start(bf16[4,32,304]{2,1,0:T(8,128)(2,1)S(1)} %shard_map.98.b0), channel_id=1, source_target_pairs={{0,4},{1,5},{2,6},{3,7},{4,0},{5,1},{6,2},{7,3},{8,12},{9,13},{10,... | collective-permute-start | bytes 233480 | tf_op jit(solution)/shard_map/ppermute | solution.py:332
  27.3 3.5 %collective-permute-start.9 = (bf16[4,32,304]{2,1,0:T(8,128)(2,1)S(1)}, bf16[4,32,304]{2,1,0:T(8,128)(2,1)S(1)}, u32[]{:S(2)}, u32[]{:S(2)}) collective-permute-start(bf16[4,32,304]{2,1,0:T(8,128)(2,1)S(1)} %shard_map.98.b0), channel_id=1, source_target_pairs={{0,8},{1,9},{2,10},{3,11},{4,12},{5,13},{6,14},{7,15},{8,0},{9,1},... | collective-permute-start | bytes 233480 | tf_op jit(solution)/shard_map/ppermute | solution.py:332
  30.8 0.2 collective-permute-start.10
  31.1 19.4 %shard_map.97 = (f32[32,7168]{1,0:T(8,128)S(1)}, bf16[448,4864]{1,0:T(8,128)(2,1)S(1)}) custom-call(bf16[32,7168]{1,0:T(8,128)(2,1)S(1)} %get-tuple-element.27.x_ref, s32[2,32]{1,0:T(2,128)S(1)} %bitcast.5, f32[2,32]{1,0:T(2,128)S(1)} %bitcast.6, bf16[1024,2048]{1,0:T(8,128)(2,1)S(1)} %get-tuple-element.28.refs_0_, ...), custom_call_target="tpu_custom_call" | custom-call | flops 2818572288 | bytes 58720256 | tf_op jit(solution)/shard_map/pallas_call | solution.py:249
  50.5 1.6 %shard_map.99 = (f32[16,7168]{1,0:T(8,128)S(1)}, bf16[16,7168]{1,0:T(8,128)(2,1)S(1)}) custom-call(f32[32,7168]{1,0:T(8,128)S(1)} %get-tuple-element.36.part_ref, bf16[4,32,304]{2,1,0:T(8,128)(2,1)S(1)} %shard_map.98.b0, bf16[4,32,304]{2,1,0:T(8,128)(2,1)S(1)} %collective-permute-done.8.b1, bf16[4,32,304]{2,1,0:T(8,128)(2,1)S(1)} %collective-permute-done.9.b2, ...), custom_call_target="tpu_custom_call" | custom-call | flops 139460608 | bytes 4358144 | tf_op jit(solution)/shard_map/pallas_call | solution.py:299
  52.1 0.1 collective-permute-start.11
  52.2 1.5 %collective-permute-done.11 = bf16[16,7168]{1,0:T(8,128)(2,1)S(1)} collective-permute-done((bf16[16,7168]{1,0:T(8,128)(2,1)S(1)}, bf16[16,7168]{1,0:T(8,128)(2,1)S(1)}, u32[]{:S(2)}, u32[]{:S(2)}) %collective-permute-start.11) | collective-permute-done | bytes 229408 | tf_op jit(solution)/shard_map/ppermute | solution.py:332
  53.7 1.3 %collective-permute-start.12 = (bf16[8,7168]{1,0:T(8,128)(2,1)S(1)}, bf16[8,7168]{1,0:T(8,128)(2,1)S(1)}, u32[]{:S(2)}, u32[]{:S(2)}) collective-permute-start(bf16[8,7168]{1,0:T(8,128)(2,1)S(1)} %slice.42), channel_id=1, source_target_pairs={{0,2},{1,3},{2,0},{3,1},{4,6},{5,7},{6,4},{7,5},{8,10},{9,11},{10,... | collective-permute-start | bytes 344072 | tf_op jit(solution)/shard_map/ppermute | solution.py:332
  55.0 3.9 %collective-permute-done.12 = bf16[8,7168]{1,0:T(8,128)(2,1)S(1)} collective-permute-done((bf16[8,7168]{1,0:T(8,128)(2,1)S(1)}, bf16[8,7168]{1,0:T(8,128)(2,1)S(1)}, u32[]{:S(2)}, u32[]{:S(2)}) %collective-permute-start.12) | collective-permute-done | bytes 114720 | tf_op jit(solution)/shard_map/ppermute | solution.py:332
  59.0 0.1 fusion.5
  59.1 3.7 %collective-permute-start.15 = (bf16[2,7168]{1,0:T(2,128)(2,1)S(1)}, bf16[2,7168]{1,0:T(2,128)(2,1)S(1)}, u32[]{:S(2)}, u32[]{:S(2)}) collective-permute-start(bf16[2,7168]{1,0:T(2,128)(2,1)S(1)} %get-tuple-element.44), channel_id=1, source_target_pairs={{0,12},{1,13},{2,14},{3,15},{4,8},{5,9},{6,10},{7,11},{8,4},{9,5},... | collective-permute-start | bytes 86024 | tf_op jit(solution)/shard_map/ppermute | solution.py:332
  62.8 0.8 %collective-permute-start.13 = (bf16[2,7168]{1,0:T(2,128)(2,1)S(1)}, bf16[2,7168]{1,0:T(2,128)(2,1)S(1)}, u32[]{:S(2)}, u32[]{:S(2)}) collective-permute-start(bf16[2,7168]{1,0:T(2,128)(2,1)S(1)} %get-tuple-element.43), channel_id=1, source_target_pairs={{0,4},{1,5},{2,6},{3,7},{4,0},{5,1},{6,2},{7,3},{8,12},{9,13},{10,... | collective-permute-start | bytes 86024 | tf_op jit(solution)/shard_map/ppermute | solution.py:332
  63.6 1.4 %collective-permute-done.15 = bf16[2,7168]{1,0:T(2,128)(2,1)S(1)} collective-permute-done((bf16[2,7168]{1,0:T(2,128)(2,1)S(1)}, bf16[2,7168]{1,0:T(2,128)(2,1)S(1)}, u32[]{:S(2)}, u32[]{:S(2)}) %collective-permute-start.15) | collective-permute-done | bytes 28704 | tf_op jit(solution)/shard_map/ppermute | solution.py:332
  65.0 2.6 %collective-permute-done.14 = bf16[2,7168]{1,0:T(2,128)(2,1)S(1)} collective-permute-done((bf16[2,7168]{1,0:T(2,128)(2,1)S(1)}, bf16[2,7168]{1,0:T(2,128)(2,1)S(1)}, u32[]{:S(2)}, u32[]{:S(2)}) %collective-permute-start.14) | collective-permute-done | bytes 28704 | tf_op jit(solution)/shard_map/ppermute | solution.py:332
  67.5 0.7 %fusion.3 = bf16[2,7168]{1,0:T(2,128)(2,1)} fusion(bf16[2,7168]{1,0:T(2,128)(2,1)S(1)} %collective-permute-done.15, bf16[2,7168]{1,0:T(2,128)(2,1)S(1)} %collective-permute-done.14, bf16[2,7168]{1,0:T(2,128)(2,1)S(1)} %collective-permute-done.13, f32[8,7168]{1,0:T(8,128)S(1)} %get-tuple-element.42, bf16[2,7168]{1,0:T(2,128)(2,1)S(1)} %copy-done), kind=kLoop, calls=%fused_computation.7 | loop fusion | flops 129024 | bytes 200704 | tf_op jit(solution)/shard_map/convert_element_type | solution.py:371
  (20 shorter events, 0.2 us)
Async XLA Ops:
  0.0 11.6 %collective-permute-start = (bf16[2,7168]{1,0:T(2,128)(2,1)}, bf16[2,7168]{1,0:T(2,128)(2,1)S(1)}, u32[]{:S(2)}, u32[]{:S(2)}) collective-permute-start(bf16[2,7168]{1,0:T(2,128)(2,1)} %refs_1_.6), channel_id=1, source_target_pairs={{0,4},{1,5},{2,6},{3,7},{4,0},{5,1},{6,2},{7,3},{8,12},{9,13},{10,... | collective-permute-start | bytes 86024 | tf_op jit(solution)/shard_map/ppermute | solution.py:332
  3.0 8.6 %collective-permute-start.1 = (bf16[2,7168]{1,0:T(2,128)(2,1)}, bf16[2,7168]{1,0:T(2,128)(2,1)S(1)}, u32[]{:S(2)}, u32[]{:S(2)}) collective-permute-start(bf16[2,7168]{1,0:T(2,128)(2,1)} %refs_1_.6), channel_id=1, source_target_pairs={{0,8},{1,9},{2,10},{3,11},{4,12},{5,13},{6,14},{7,15},{8,0},{9,1},... | collective-permute-start | bytes 86024 | tf_op jit(solution)/shard_map/ppermute | solution.py:332
  5.6 6.0 %collective-permute-start.2 = (bf16[2,7168]{1,0:T(2,128)(2,1)}, bf16[2,7168]{1,0:T(2,128)(2,1)S(1)}, u32[]{:S(2)}, u32[]{:S(2)}) collective-permute-start(bf16[2,7168]{1,0:T(2,128)(2,1)} %refs_1_.6), channel_id=1, source_target_pairs={{0,12},{1,13},{2,14},{3,15},{4,8},{5,9},{6,10},{7,11},{8,4},{9,5},... | collective-permute-start | bytes 86024 | tf_op jit(solution)/shard_map/ppermute | solution.py:332
  5.6 6.0 %copy-start = (bf16[2,7168]{1,0:T(2,128)(2,1)S(1)}, bf16[2,7168]{1,0:T(2,128)(2,1)}, u32[]{:S(2)}) copy-start(bf16[2,7168]{1,0:T(2,128)(2,1)} %refs_1_.6) | copy-start | bytes 86020
  11.7 5.3 %collective-permute-start.3 = (bf16[8,7168]{1,0:T(8,128)(2,1)S(1)}, bf16[8,7168]{1,0:T(8,128)(2,1)S(1)}, u32[]{:S(2)}, u32[]{:S(2)}) collective-permute-start(bf16[8,7168]{1,0:T(8,128)(2,1)S(1)} %shard_map.93.refs_1_), channel_id=1, source_target_pairs={{0,2},{1,3},{2,0},{3,1},{4,6},{5,7},{6,4},{7,5},{8,10},{9,11},{10,... | collective-permute-start | bytes 344072 | tf_op jit(solution)/shard_map/ppermute | solution.py:332
  17.0 1.6 %collective-permute-start.4 = (bf16[16,7168]{1,0:T(8,128)(2,1)S(1)}, bf16[16,7168]{1,0:T(8,128)(2,1)S(1)}, u32[]{:S(2)}, u32[]{:S(2)}) collective-permute-start(bf16[16,7168]{1,0:T(8,128)(2,1)S(1)} %shard_map.94.mine_ref), channel_id=1, source_target_pairs={{0,1},{1,0},{2,3},{3,2},{4,5},{5,4},{6,7},{7,6},{8,9},{9,8},{10,11... | collective-permute-start | bytes 688136 | tf_op jit(solution)/shard_map/ppermute | solution.py:332
  21.1 9.9 %copy-start.1 = (s32[32,2]{0,1:T(2,128)S(1)}, s32[32,2]{0,1:T(2,128)}, u32[]{:S(2)}) copy-start(s32[32,2]{0,1:T(2,128)} %param.10) | copy-start | bytes 772
  21.1 9.9 %copy-start.2 = (f32[32,2]{0,1:T(2,128)S(1)}, f32[32,2]{0,1:T(2,128)}, u32[]{:S(2)}) copy-start(f32[32,2]{0,1:T(2,128)} %param.11) | copy-start | bytes 772
  21.1 5.4 %collective-permute-start.5 = (bf16[1,32,304]{2,1,0:T(8,128)(2,1)S(1)}, bf16[1,32,304]{2,1,0:T(8,128)(2,1)S(1)}, u32[]{:S(2)}, u32[]{:S(2)}) collective-permute-start(bf16[1,32,304]{2,1,0:T(8,128)(2,1)S(1)} %get-tuple-element.33.refs_0_.refs_1_), channel_id=1, source_target_pairs={{0,1},{1,0},{2,3},{3,2},{4,5},{5,4},{6,7},{7,6},{8,9},{9,8},{10,11... | collective-permute-start | bytes 58376 | tf_op jit(solution)/shard_map/ppermute | solution.py:332
  21.3 5.2 %collective-permute-start.6 = (bf16[1,32,304]{2,1,0:T(8,128)(2,1)S(1)}, bf16[1,32,304]{2,1,0:T(8,128)(2,1)S(1)}, u32[]{:S(2)}, u32[]{:S(2)}) collective-permute-start(bf16[1,32,304]{2,1,0:T(8,128)(2,1)S(1)} %get-tuple-element.33.refs_0_.refs_1_), channel_id=1, source_target_pairs={{0,2},{1,3},{2,0},{3,1},{4,6},{5,7},{6,4},{7,5},{8,10},{9,11},{10,... | collective-permute-start | bytes 58376 | tf_op jit(solution)/shard_map/ppermute | solution.py:332
  22.6 4.0 %collective-permute-start.7 = (bf16[1,32,304]{2,1,0:T(8,128)(2,1)S(1)}, bf16[1,32,304]{2,1,0:T(8,128)(2,1)S(1)}, u32[]{:S(2)}, u32[]{:S(2)}) collective-permute-start(bf16[1,32,304]{2,1,0:T(8,128)(2,1)S(1)} %get-tuple-element.33.refs_0_.refs_1_), channel_id=1, source_target_pairs={{0,3},{1,2},{2,1},{3,0},{4,7},{5,6},{6,5},{7,4},{8,11},{9,10},{10,... | collective-permute-start | bytes 58376 | tf_op jit(solution)/shard_map/ppermute | solution.py:332
  26.6 23.8 %collective-permute-start.8 = (bf16[4,32,304]{2,1,0:T(8,128)(2,1)S(1)}, bf16[4,32,304]{2,1,0:T(8,128)(2,1)S(1)}, u32[]{:S(2)}, u32[]{:S(2)}) collective-permute-start(bf16[4,32,304]{2,1,0:T(8,128)(2,1)S(1)} %shard_map.98.b0), channel_id=1, source_target_pairs={{0,4},{1,5},{2,6},{3,7},{4,0},{5,1},{6,2},{7,3},{8,12},{9,13},{10,... | collective-permute-start | bytes 233480 | tf_op jit(solution)/shard_map/ppermute | solution.py:332
  27.3 23.1 %collective-permute-start.9 = (bf16[4,32,304]{2,1,0:T(8,128)(2,1)S(1)}, bf16[4,32,304]{2,1,0:T(8,128)(2,1)S(1)}, u32[]{:S(2)}, u32[]{:S(2)}) collective-permute-start(bf16[4,32,304]{2,1,0:T(8,128)(2,1)S(1)} %shard_map.98.b0), channel_id=1, source_target_pairs={{0,8},{1,9},{2,10},{3,11},{4,12},{5,13},{6,14},{7,15},{8,0},{9,1},... | collective-permute-start | bytes 233480 | tf_op jit(solution)/shard_map/ppermute | solution.py:332
  30.8 19.6 %collective-permute-start.10 = (bf16[4,32,304]{2,1,0:T(8,128)(2,1)S(1)}, bf16[4,32,304]{2,1,0:T(8,128)(2,1)S(1)}, u32[]{:S(2)}, u32[]{:S(2)}) collective-permute-start(bf16[4,32,304]{2,1,0:T(8,128)(2,1)S(1)} %shard_map.98.b0), channel_id=1, source_target_pairs={{0,12},{1,13},{2,14},{3,15},{4,8},{5,9},{6,10},{7,11},{8,4},{9,5},... | collective-permute-start | bytes 233480 | tf_op jit(solution)/shard_map/ppermute | solution.py:332
  52.1 1.6 %collective-permute-start.11 = (bf16[16,7168]{1,0:T(8,128)(2,1)S(1)}, bf16[16,7168]{1,0:T(8,128)(2,1)S(1)}, u32[]{:S(2)}, u32[]{:S(2)}) collective-permute-start(bf16[16,7168]{1,0:T(8,128)(2,1)S(1)} %get-tuple-element.40), channel_id=1, source_target_pairs={{0,1},{1,0},{2,3},{3,2},{4,5},{5,4},{6,7},{7,6},{8,9},{9,8},{10,11... | collective-permute-start | bytes 688136 | tf_op jit(solution)/shard_map/ppermute | solution.py:332
  53.7 5.3 %collective-permute-start.12 = (bf16[8,7168]{1,0:T(8,128)(2,1)S(1)}, bf16[8,7168]{1,0:T(8,128)(2,1)S(1)}, u32[]{:S(2)}, u32[]{:S(2)}) collective-permute-start(bf16[8,7168]{1,0:T(8,128)(2,1)S(1)} %slice.42), channel_id=1, source_target_pairs={{0,2},{1,3},{2,0},{3,1},{4,6},{5,7},{6,4},{7,5},{8,10},{9,11},{10,... | collective-permute-start | bytes 344072 | tf_op jit(solution)/shard_map/ppermute | solution.py:332
  59.1 5.8 %collective-permute-start.15 = (bf16[2,7168]{1,0:T(2,128)(2,1)S(1)}, bf16[2,7168]{1,0:T(2,128)(2,1)S(1)}, u32[]{:S(2)}, u32[]{:S(2)}) collective-permute-start(bf16[2,7168]{1,0:T(2,128)(2,1)S(1)} %get-tuple-element.44), channel_id=1, source_target_pairs={{0,12},{1,13},{2,14},{3,15},{4,8},{5,9},{6,10},{7,11},{8,4},{9,5},... | collective-permute-start | bytes 86024 | tf_op jit(solution)/shard_map/ppermute | solution.py:332
  62.8 4.8 %collective-permute-start.14 = (bf16[2,7168]{1,0:T(2,128)(2,1)S(1)}, bf16[2,7168]{1,0:T(2,128)(2,1)S(1)}, u32[]{:S(2)}, u32[]{:S(2)}) collective-permute-start(bf16[2,7168]{1,0:T(2,128)(2,1)S(1)} %get-tuple-element.45), channel_id=1, source_target_pairs={{0,8},{1,9},{2,10},{3,11},{4,12},{5,13},{6,14},{7,15},{8,0},{9,1},... | collective-permute-start | bytes 86024 | tf_op jit(solution)/shard_map/ppermute | solution.py:332
  62.8 4.8 %collective-permute-start.13 = (bf16[2,7168]{1,0:T(2,128)(2,1)S(1)}, bf16[2,7168]{1,0:T(2,128)(2,1)S(1)}, u32[]{:S(2)}, u32[]{:S(2)}) collective-permute-start(bf16[2,7168]{1,0:T(2,128)(2,1)S(1)} %get-tuple-element.43), channel_id=1, source_target_pairs={{0,4},{1,5},{2,6},{3,7},{4,0},{5,1},{6,2},{7,3},{8,12},{9,13},{10,... | collective-permute-start | bytes 86024 | tf_op jit(solution)/shard_map/ppermute | solution.py:332

commit v5 on v4

--- a/solution.py
+++ b/solution.py
@@ -11,7 +11,7 @@
 CHUNK = 1024
 PER = 7
 SLOTS = 4
-AHEAD = (3, 1, 0, 1, 2)
+AHEAD = (1, 0, 0, 0, 0)
 MIB = 1 << 20
 
 VMEM = pl.BlockSpec(memory_space=pltpu.VMEM)
@@ -167,9 +167,11 @@
     return hidden, x, held
 
 
-def expert_kernel(owned, there, x_ref, ids_ref, gates_ref, *refs):
-    ready, refs = refs[:there], refs[there:]
-    gate_ref, up_ref, down_ref, dense_ref, out_ref, dense_held, gate_sum, up_sum, hidden, ring, sems = refs
+def expert_kernel(owned, there, x_ref, ids_ref, gates_ref, gate_ref, *refs):
+    ready = [gate_ref.at[pl.ds(n * CHUNK, CHUNK)] for n in range(PER)] + list(refs[:there])
+    refs = refs[there:]
+    there += PER
+    up_ref, down_ref, out_ref, gate_sum, up_sum, hidden, ring, sems = refs
     rows, units = gate_sum.shape
     slots = ring.shape[0]
     blocks = PER // 2
@@ -183,7 +185,6 @@
     pieces.append([(parts[0], 0), (parts[1], CHUNK)])
     total = len(pieces)
     found = {}
-    dense_copy = pltpu.make_async_copy(dense_ref, dense_held, sems.at[slots + 1])
 
     def issue(n):
         if n < total:
@@ -194,8 +195,6 @@
                 copy = pltpu.make_async_copy(source, target, sems.at[slots if column else n % slots])
                 copy.start()
                 found[n].append(copy)
-        elif n == total:
-            dense_copy.start()
 
     def arrived(n):
         wait_copies(found[n])
@@ -240,32 +239,28 @@
     last = arrived(total - 1)
     both = dot(first, last[:, 0:CHUNK]) + dot(second, last[:, CHUNK : 2 * CHUNK])
     out_ref[:, blocks * units :] = scale * both
-    dense_copy.wait()
-
-
-def expert_block(owned, x, ids, gates, ready, gate, up, down, dense_down):
+
+
+def expert_block(owned, x, ids, gates, ready, gate, up, down):
     rows, width = x.shape
     units = gate.shape[1]
     return pl.pallas_call(
         functools.partial(expert_kernel, owned, len(ready)),
-        out_shape=(
-            pltpu.VMEM((rows, width), jnp.float32),
-            pltpu.VMEM(dense_down.shape, dense_down.dtype),
-        ),
-        in_specs=[VMEM] * (3 + len(ready)) + [ANY] * 4,
-        out_specs=(VMEM, VMEM),
+        out_shape=pltpu.VMEM((rows, width), jnp.float32),
+        in_specs=[VMEM] * (4 + len(ready)) + [ANY] * 2,
+        out_specs=VMEM,
         scratch_shapes=[
             pltpu.VMEM((rows, units), jnp.float32),
             pltpu.VMEM((rows, units), jnp.float32),
             pltpu.VMEM((rows, units), jnp.bfloat16),
             pltpu.VMEM((SLOTS, CHUNK, units), jnp.bfloat16),
-            pltpu.SemaphoreType.DMA((SLOTS + 2,)),
+            pltpu.SemaphoreType.DMA((SLOTS + 1,)),
         ],
         cost_estimate=cost(6 * rows * down.size, 4 * down.size),
         compiler_params=limit(4 * SLOTS + 3),
     )(
-        in_vmem(x), ids, gates, *[in_vmem(r) for r in ready],
-        in_hbm(gate), in_hbm(up), in_hbm(down), in_hbm(dense_down),
+        in_vmem(x), ids, gates, in_vmem(gate), *[in_vmem(r) for r in ready],
+        in_hbm(up), in_hbm(down),
     )
 
 
@@ -332,14 +327,17 @@
         return lax.ppermute(value, "gx", [(i, i ^ step) for i in range(16)])
 
     ends = [sum(AHEAD[: n + 1]) for n in range(len(AHEAD))]
-    chunks = [range(end - count, end) for count, end in zip(AHEAD, ends)]
+    chunks = [range(PER + end - count, PER + end) for count, end in zip(AHEAD, ends)]
     streams = (expert_gate, expert_up)
     along_z = [swap(tokens, 4 * z) for z in (1, 2, 3)]
-    ready, dense_gate, done = fetch(None, chunks[0], *streams, dense_gate)
+    ready, done = [], None
+    if AHEAD[0]:
+        ready, done = fetch(None, chunks[0], *streams)
     mine = join(done, tokens, *along_z)
     along_x = swap(mine, 2)
-    more, dense_up, done = fetch(done, chunks[1], *streams, dense_up)
-    ready += more
+    if AHEAD[1]:
+        more, done = fetch(done, chunks[1], *streams)
+        ready += more
     mine = join(done, mine, along_x)
     other = swap(mine, 1)
     if AHEAD[2]:
@@ -356,9 +354,7 @@
         done = None
     block = join(done, *near)
     blocks = [block] + [swap(block, 4 * z) for z in (1, 2, 3)]
-    part, dense_down = expert_block(
-        owned, x, route_ids.T, route_gates.T, ready, expert_gate, expert_up, expert_down, dense_down
-    )
+    part = expert_block(owned, x, route_ids.T, route_gates.T, ready, expert_gate, expert_up, expert_down)
     keep, send = dense_out(owned, part, blocks, dense_down)
 
     half = keep.shape[0] // 2

time: 68.4 us -> 64.3 us (0.940)
  Pallas kernels: 36.6 us -> 24.2 us
  waiting for transfers between devices: 10.9 us -> 20.8 us
  starting transfers between devices: 19.7 us -> 17.9 us
    pallas_call x3 -> x1, Pallas kernels: 13 us -> 2.2 us  [fetch(): pl.pallas_call(functools.partial(fetch_kernel, chunks, len(wholes), tied)...]
    ppermute x16, waiting for transfers between devices: 10.9 us -> 20.8 us  [swap(): return lax.ppermute(value, 'gx', [(i, i ^ step) for i in range(16)])]
    ppermute x16, starting transfers between devices: 19.7 us -> 17.9 us  [swap(): return lax.ppermute(value, 'gx', [(i, i ^ step) for i in range(16)])]
    pallas_call x1, Pallas kernels: 19.4 us -> 17.8 us  [expert_block(): pl.pallas_call(functools.partial(expert_kernel, owned, len(ready)), out_s...]
  transfers between devices with their start and end apart: 16 -> 16, of which waited for: 5 -> 11; matrix products, arithmetic and copies ran while one was open for 0% -> 0% of each run, Pallas kernels for 47% -> 31%
where the time goes in v5:
time: 64.3 us; the launch traced here: 64.2 us
  Pallas kernels  24.2 us (38%)
  waiting for transfers between devices  20.8 us (32%)
  starting transfers between devices  17.9 us (28%)
  other arithmetic  0.75 us (1%)
    ppermute x16, waiting for transfers between devices, swap(): return lax.ppermute(value, 'gx', [(i, i ^ step) for i in range(16)])  20.8 us
    ppermute x16, starting transfers between devices, swap(): return lax.ppermute(value, 'gx', [(i, i ^ step) for i in range(16)])  17.9 us
    pallas_call x1, Pallas kernels, expert_block(): pl.pallas_call(functools.partial(expert_kernel, owned, len(ready)), out_s...  17.8 us
    pallas_call x1, Pallas kernels, dense_in(): pl.pallas_call(functools.partial(dense_in_kernel, owned, chunks), out_sha...  2.51 us
    pallas_call x1, Pallas kernels, fetch(): pl.pallas_call(functools.partial(fetch_kernel, chunks, len(wholes), tied)...  2.2 us
    pallas_call x1, Pallas kernels, dense_out(): pl.pallas_call(functools.partial(dense_out_kernel, owned), out_shape=(jax...  1.64 us
  transfers between devices with their start and end apart: 16, of which 11 were waited for; matrix products, arithmetic and copies ran while one was open for 0% of the time, Pallas kernels for 31%

profile of v5, /device:TPU:0, one launch (start us, length us, event | category | flops | bytes accessed | tf_op | source)
XLA Modules:
  0.0 64.2 jit_solution(1711481905934828298)
XLA Ops:
  0.0 4.1 %collective-permute-start.1 = (bf16[2,7168]{1,0:T(2,128)(2,1)}, bf16[2,7168]{1,0:T(2,128)(2,1)S(1)}, u32[]{:S(2)}, u32[]{:S(2)}) collective-permute-start(bf16[2,7168]{1,0:T(2,128)(2,1)} %refs_1_.4), channel_id=1, source_target_pairs={{0,8},{1,9},{2,10},{3,11},{4,12},{5,13},{6,14},{7,15},{8,0},{9,1},... | collective-permute-start | bytes 86024 | tf_op jit(solution)/shard_map/ppermute | solution.py:327
  4.1 1.6 %collective-permute-start = (bf16[2,7168]{1,0:T(2,128)(2,1)}, bf16[2,7168]{1,0:T(2,128)(2,1)S(1)}, u32[]{:S(2)}, u32[]{:S(2)}) collective-permute-start(bf16[2,7168]{1,0:T(2,128)(2,1)} %refs_1_.4), channel_id=1, source_target_pairs={{0,4},{1,5},{2,6},{3,7},{4,0},{5,1},{6,2},{7,3},{8,12},{9,13},{10,... | collective-permute-start | bytes 86024 | tf_op jit(solution)/shard_map/ppermute | solution.py:327
  5.7 2.2 %shard_map.91 = (bf16[1024,2048]{1,0:T(8,128)(2,1)S(1)}, f32[8,128]{1,0:T(8,128)S(1)}) custom-call(bf16[7168,2048]{1,0:T(8,128)(2,1)} %gate_ref.3, bf16[7168,2048]{1,0:T(8,128)(2,1)} %refs_1_.5), custom_call_target="tpu_custom_call" | custom-call | bytes 4194304 | tf_op jit(solution)/shard_map/pallas_call | solution.py:100
  7.9 0.3 collective-permute-done.refs_2_
  8.2 3.4 %collective-permute-done.2.refs_4_ = bf16[2,7168]{1,0:T(2,128)(2,1)S(1)} collective-permute-done((bf16[2,7168]{1,0:T(2,128)(2,1)}, bf16[2,7168]{1,0:T(2,128)(2,1)S(1)}, u32[]{:S(2)}, u32[]{:S(2)}) %collective-permute-start.2) | collective-permute-done | bytes 28704 | tf_op jit(solution)/shard_map/ppermute | solution.py:327
  11.6 0.1 shard_map.92.refs_1_
  11.6 1.6 %collective-permute-start.3 = (bf16[8,7168]{1,0:T(8,128)(2,1)S(1)}, bf16[8,7168]{1,0:T(8,128)(2,1)S(1)}, u32[]{:S(2)}, u32[]{:S(2)}) collective-permute-start(bf16[8,7168]{1,0:T(8,128)(2,1)S(1)} %shard_map.92.refs_1_), channel_id=1, source_target_pairs={{0,2},{1,3},{2,0},{3,1},{4,6},{5,7},{6,4},{7,5},{8,10},{9,11},{10,... | collective-permute-start | bytes 344072 | tf_op jit(solution)/shard_map/ppermute | solution.py:327
  13.2 3.3 %collective-permute-done.3.refs_2_ = bf16[8,7168]{1,0:T(8,128)(2,1)S(1)} collective-permute-done((bf16[8,7168]{1,0:T(8,128)(2,1)S(1)}, bf16[8,7168]{1,0:T(8,128)(2,1)S(1)}, u32[]{:S(2)}, u32[]{:S(2)}) %collective-permute-start.3) | collective-permute-done | bytes 114720 | tf_op jit(solution)/shard_map/ppermute | solution.py:327
  16.5 0.1 collective-permute-start.4
  16.6 1.5 %collective-permute-done.4.other_ref = bf16[16,7168]{1,0:T(8,128)(2,1)S(1)} collective-permute-done((bf16[16,7168]{1,0:T(8,128)(2,1)S(1)}, bf16[16,7168]{1,0:T(8,128)(2,1)S(1)}, u32[]{:S(2)}, u32[]{:S(2)}) %collective-permute-start.4) | collective-permute-done | bytes 229408 | tf_op jit(solution)/shard_map/ppermute | solution.py:327
  18.2 2.5 %shard_map.94 = (bf16[1,32,304]{2,1,0:T(8,128)(2,1)S(1)}, bf16[32,7168]{1,0:T(8,128)(2,1)S(1)}) custom-call(bf16[16,7168]{1,0:T(8,128)(2,1)S(1)} %shard_map.93.mine_ref, bf16[16,7168]{1,0:T(8,128)(2,1)S(1)} %collective-permute-done.4.other_ref, bf16[304,7168]{1,0:T(8,128)(2,1)S(1)} %bitcast.7, bf16[304,7168]{1,0:T(8,128)(2,1)S(1)} %bitcast.8, ...), custom_call_target="tpu_custom_call" | custom-call | flops 278921216 | bytes 8716288 | tf_op jit(solution)/shard_map/pallas_call | solution.py:154
  20.7 1.3 %collective-permute-start.7 = (bf16[1,32,304]{2,1,0:T(8,128)(2,1)S(1)}, bf16[1,32,304]{2,1,0:T(8,128)(2,1)S(1)}, u32[]{:S(2)}, u32[]{:S(2)}) collective-permute-start(bf16[1,32,304]{2,1,0:T(8,128)(2,1)S(1)} %get-tuple-element.14.refs_0_), channel_id=1, source_target_pairs={{0,3},{1,2},{2,1},{3,0},{4,7},{5,6},{6,5},{7,4},{8,11},{9,10},{10,... | collective-permute-start | bytes 58376 | tf_op jit(solution)/shard_map/ppermute | solution.py:327
  22.0 0.5 collective-permute-start.6
  22.5 0.1 collective-permute-start.5
  22.6 1.4 %collective-permute-done.7.refs_3_ = bf16[1,32,304]{2,1,0:T(8,128)(2,1)S(1)} collective-permute-done((bf16[1,32,304]{2,1,0:T(8,128)(2,1)S(1)}, bf16[1,32,304]{2,1,0:T(8,128)(2,1)S(1)}, u32[]{:S(2)}, u32[]{:S(2)}) %collective-permute-start.7) | collective-permute-done | bytes 19488 | tf_op jit(solution)/shard_map/ppermute | solution.py:327
  24.0 1.8 %collective-permute-done.6.refs_2_ = bf16[1,32,304]{2,1,0:T(8,128)(2,1)S(1)} collective-permute-done((bf16[1,32,304]{2,1,0:T(8,128)(2,1)S(1)}, bf16[1,32,304]{2,1,0:T(8,128)(2,1)S(1)}, u32[]{:S(2)}, u32[]{:S(2)}) %collective-permute-start.6) | collective-permute-done | bytes 19488 | tf_op jit(solution)/shard_map/ppermute | solution.py:327
  25.8 0.4 collective-permute-start.10
  26.2 4.1 %collective-permute-start.8 = (bf16[4,32,304]{2,1,0:T(8,128)(2,1)S(1)}, bf16[4,32,304]{2,1,0:T(8,128)(2,1)S(1)}, u32[]{:S(2)}, u32[]{:S(2)}) collective-permute-start(bf16[4,32,304]{2,1,0:T(8,128)(2,1)S(1)} %shard_map.96.b0), channel_id=1, source_target_pairs={{0,4},{1,5},{2,6},{3,7},{4,0},{5,1},{6,2},{7,3},{8,12},{9,13},{10,... | collective-permute-start | bytes 233480 | tf_op jit(solution)/shard_map/ppermute | solution.py:327
  30.4 17.8 %shard_map.95.part_ref = f32[32,7168]{1,0:T(8,128)S(1)} custom-call(bf16[32,7168]{1,0:T(8,128)(2,1)S(1)} %get-tuple-element.12.x_ref, s32[2,32]{1,0:T(2,128)S(1)} %bitcast.12, f32[2,32]{1,0:T(2,128)S(1)} %bitcast.13, bf16[7168,2048]{1,0:T(8,128)(2,1)S(1)} %bitcast.6, bf16[1024,2048]{1,0:T(8,128)(2,1)S(1)} %get-tuple-element.13.refs_0_, ...), custom_call_target="tpu_custom_call" | custom-call | flops 2818572288 | bytes 58720256 | tf_op jit(solution)/shard_map/pallas_call | solution.py:247
  48.3 1.6 %shard_map.97 = (f32[16,7168]{1,0:T(8,128)S(1)}, bf16[16,7168]{1,0:T(8,128)(2,1)S(1)}) custom-call(f32[32,7168]{1,0:T(8,128)S(1)} %shard_map.95.part_ref, bf16[4,32,304]{2,1,0:T(8,128)(2,1)S(1)} %shard_map.96.b0, bf16[4,32,304]{2,1,0:T(8,128)(2,1)S(1)} %collective-permute-done.8.b1, bf16[4,32,304]{2,1,0:T(8,128)(2,1)S(1)} %collective-permute-done.9.b2, ...), custom_call_target="tpu_custom_call" | custom-call | flops 139460608 | bytes 4358144 | tf_op jit(solution)/shard_map/pallas_call | solution.py:294
  49.9 0.1 collective-permute-start.11
  50.0 1.5 %collective-permute-done.11 = bf16[16,7168]{1,0:T(8,128)(2,1)S(1)} collective-permute-done((bf16[16,7168]{1,0:T(8,128)(2,1)S(1)}, bf16[16,7168]{1,0:T(8,128)(2,1)S(1)}, u32[]{:S(2)}, u32[]{:S(2)}) %collective-permute-start.11) | collective-permute-done | bytes 229408 | tf_op jit(solution)/shard_map/ppermute | solution.py:327
  51.5 0.6 collective-permute-start.12
  52.1 4.7 %collective-permute-done.12 = bf16[8,7168]{1,0:T(8,128)(2,1)S(1)} collective-permute-done((bf16[8,7168]{1,0:T(8,128)(2,1)S(1)}, bf16[8,7168]{1,0:T(8,128)(2,1)S(1)}, u32[]{:S(2)}, u32[]{:S(2)}) %collective-permute-start.12) | collective-permute-done | bytes 114720 | tf_op jit(solution)/shard_map/ppermute | solution.py:327
  56.8 0.1 fusion.5
  56.9 0.1 collective-permute-start.13
  57.0 1.4 %collective-permute-start.15 = (bf16[2,7168]{1,0:T(2,128)(2,1)S(1)}, bf16[2,7168]{1,0:T(2,128)(2,1)S(1)}, u32[]{:S(2)}, u32[]{:S(2)}) collective-permute-start(bf16[2,7168]{1,0:T(2,128)(2,1)S(1)} %get-tuple-element.20), channel_id=1, source_target_pairs={{0,12},{1,13},{2,14},{3,15},{4,8},{5,9},{6,10},{7,11},{8,4},{9,5},... | collective-permute-start | bytes 86024 | tf_op jit(solution)/shard_map/ppermute | solution.py:327
  58.4 2.0 %collective-permute-start.14 = (bf16[2,7168]{1,0:T(2,128)(2,1)S(1)}, bf16[2,7168]{1,0:T(2,128)(2,1)S(1)}, u32[]{:S(2)}, u32[]{:S(2)}) collective-permute-start(bf16[2,7168]{1,0:T(2,128)(2,1)S(1)} %get-tuple-element.21), channel_id=1, source_target_pairs={{0,8},{1,9},{2,10},{3,11},{4,12},{5,13},{6,14},{7,15},{8,0},{9,1},... | collective-permute-start | bytes 86024 | tf_op jit(solution)/shard_map/ppermute | solution.py:327
  60.4 0.9 %collective-permute-done.13 = bf16[2,7168]{1,0:T(2,128)(2,1)S(1)} collective-permute-done((bf16[2,7168]{1,0:T(2,128)(2,1)S(1)}, bf16[2,7168]{1,0:T(2,128)(2,1)S(1)}, u32[]{:S(2)}, u32[]{:S(2)}) %collective-permute-start.13) | collective-permute-done | bytes 28704 | tf_op jit(solution)/shard_map/ppermute | solution.py:327
  61.3 1.4 %collective-permute-done.15 = bf16[2,7168]{1,0:T(2,128)(2,1)S(1)} collective-permute-done((bf16[2,7168]{1,0:T(2,128)(2,1)S(1)}, bf16[2,7168]{1,0:T(2,128)(2,1)S(1)}, u32[]{:S(2)}, u32[]{:S(2)}) %collective-permute-start.15) | collective-permute-done | bytes 28704 | tf_op jit(solution)/shard_map/ppermute | solution.py:327
  62.7 0.8 %collective-permute-done.14 = bf16[2,7168]{1,0:T(2,128)(2,1)S(1)} collective-permute-done((bf16[2,7168]{1,0:T(2,128)(2,1)S(1)}, bf16[2,7168]{1,0:T(2,128)(2,1)S(1)}, u32[]{:S(2)}, u32[]{:S(2)}) %collective-permute-start.14) | collective-permute-done | bytes 28704 | tf_op jit(solution)/shard_map/ppermute | solution.py:327
  63.5 0.7 %fusion.3 = bf16[2,7168]{1,0:T(2,128)(2,1)} fusion(bf16[2,7168]{1,0:T(2,128)(2,1)S(1)} %collective-permute-done.15, bf16[2,7168]{1,0:T(2,128)(2,1)S(1)} %collective-permute-done.14, bf16[2,7168]{1,0:T(2,128)(2,1)S(1)} %collective-permute-done.13, f32[8,7168]{1,0:T(8,128)S(1)} %get-tuple-element.18, bf16[2,7168]{1,0:T(2,128)(2,1)S(1)} %copy-done.2), kind=kLoop, calls=%fused_computation.7 | loop fusion | flops 129024 | bytes 200704 | tf_op jit(solution)/shard_map/convert_element_type | solution.py:367
  (42 shorter events, 0.2 us)
Async XLA Ops:
  0.0 11.6 %copy-start.2 = (bf16[2,7168]{1,0:T(2,128)(2,1)S(1)}, bf16[2,7168]{1,0:T(2,128)(2,1)}, u32[]{:S(2)}) copy-start(bf16[2,7168]{1,0:T(2,128)(2,1)} %refs_1_.4) | copy-start | bytes 86020
  0.0 18.1 %copy-start.1 = (bf16[7168,304]{0,1:T(8,128)(2,1)S(1)}, bf16[7168,304]{0,1:T(8,128)(2,1)}, u32[]{:S(2)}) copy-start(bf16[7168,304]{0,1:T(8,128)(2,1)} %param.13) | copy-start | bytes 13074436
  0.0 18.1 %copy-start = (bf16[7168,304]{0,1:T(8,128)(2,1)S(1)}, bf16[7168,304]{0,1:T(8,128)(2,1)}, u32[]{:S(2)}) copy-start(bf16[7168,304]{0,1:T(8,128)(2,1)} %param.12) | copy-start | bytes 13074436
  0.0 7.9 %collective-permute-start.1 = (bf16[2,7168]{1,0:T(2,128)(2,1)}, bf16[2,7168]{1,0:T(2,128)(2,1)S(1)}, u32[]{:S(2)}, u32[]{:S(2)}) collective-permute-start(bf16[2,7168]{1,0:T(2,128)(2,1)} %refs_1_.4), channel_id=1, source_target_pairs={{0,8},{1,9},{2,10},{3,11},{4,12},{5,13},{6,14},{7,15},{8,0},{9,1},... | collective-permute-start | bytes 86024 | tf_op jit(solution)/shard_map/ppermute | solution.py:327
  4.1 4.1 %collective-permute-start = (bf16[2,7168]{1,0:T(2,128)(2,1)}, bf16[2,7168]{1,0:T(2,128)(2,1)S(1)}, u32[]{:S(2)}, u32[]{:S(2)}) collective-permute-start(bf16[2,7168]{1,0:T(2,128)(2,1)} %refs_1_.4), channel_id=1, source_target_pairs={{0,4},{1,5},{2,6},{3,7},{4,0},{5,1},{6,2},{7,3},{8,12},{9,13},{10,... | collective-permute-start | bytes 86024 | tf_op jit(solution)/shard_map/ppermute | solution.py:327
  5.7 5.9 %collective-permute-start.2 = (bf16[2,7168]{1,0:T(2,128)(2,1)}, bf16[2,7168]{1,0:T(2,128)(2,1)S(1)}, u32[]{:S(2)}, u32[]{:S(2)}) collective-permute-start(bf16[2,7168]{1,0:T(2,128)(2,1)} %refs_1_.4), channel_id=1, source_target_pairs={{0,12},{1,13},{2,14},{3,15},{4,8},{5,9},{6,10},{7,11},{8,4},{9,5},... | collective-permute-start | bytes 86024 | tf_op jit(solution)/shard_map/ppermute | solution.py:327
  11.6 4.9 %collective-permute-start.3 = (bf16[8,7168]{1,0:T(8,128)(2,1)S(1)}, bf16[8,7168]{1,0:T(8,128)(2,1)S(1)}, u32[]{:S(2)}, u32[]{:S(2)}) collective-permute-start(bf16[8,7168]{1,0:T(8,128)(2,1)S(1)} %shard_map.92.refs_1_), channel_id=1, source_target_pairs={{0,2},{1,3},{2,0},{3,1},{4,6},{5,7},{6,4},{7,5},{8,10},{9,11},{10,... | collective-permute-start | bytes 344072 | tf_op jit(solution)/shard_map/ppermute | solution.py:327
  16.5 1.6 %collective-permute-start.4 = (bf16[16,7168]{1,0:T(8,128)(2,1)S(1)}, bf16[16,7168]{1,0:T(8,128)(2,1)S(1)}, u32[]{:S(2)}, u32[]{:S(2)}) collective-permute-start(bf16[16,7168]{1,0:T(8,128)(2,1)S(1)} %shard_map.93.mine_ref), channel_id=1, source_target_pairs={{0,1},{1,0},{2,3},{3,2},{4,5},{5,4},{6,7},{7,6},{8,9},{9,8},{10,11... | collective-permute-start | bytes 688136 | tf_op jit(solution)/shard_map/ppermute | solution.py:327
  18.1 12.2 %slice-start = ((s8[29360128]{0:T(1024)(128)(4,1)}), s8[4194304]{0:T(1024)(128)(4,1)S(1)}, s32[]{:S(2)}) async-start(s8[29360128]{0:T(1024)(128)(4,1)} %bitcast.5), calls=%async_computation | async-start | bytes 8388608
  18.1 12.2 %slice-start.1 = ((s8[29360128]{0:T(1024)(128)(4,1)}), s8[4194304]{0:T(1024)(128)(4,1)S(1)}, s32[]{:S(2)}) async-start(s8[29360128]{0:T(1024)(128)(4,1)} %bitcast.5), calls=%async_computation.1 | async-start | bytes 8388608
  18.1 12.2 %slice-start.2 = ((s8[29360128]{0:T(1024)(128)(4,1)}), s8[4194304]{0:T(1024)(128)(4,1)S(1)}, s32[]{:S(2)}) async-start(s8[29360128]{0:T(1024)(128)(4,1)} %bitcast.5), calls=%async_computation.2 | async-start | bytes 8388608
  18.1 12.2 %slice-start.3 = ((s8[29360128]{0:T(1024)(128)(4,1)}), s8[4194304]{0:T(1024)(128)(4,1)S(1)}, s32[]{:S(2)}) async-start(s8[29360128]{0:T(1024)(128)(4,1)} %bitcast.5), calls=%async_computation.3 | async-start | bytes 8388608
  18.1 12.2 %slice-start.4 = ((s8[29360128]{0:T(1024)(128)(4,1)}), s8[4194304]{0:T(1024)(128)(4,1)S(1)}, s32[]{:S(2)}) async-start(s8[29360128]{0:T(1024)(128)(4,1)} %bitcast.5), calls=%async_computation.4 | async-start | bytes 8388608
  18.1 12.2 %slice-start.5 = ((s8[29360128]{0:T(1024)(128)(4,1)}), s8[4194304]{0:T(1024)(128)(4,1)S(1)}, s32[]{:S(2)}) async-start(s8[29360128]{0:T(1024)(128)(4,1)} %bitcast.5), calls=%async_computation.5 | async-start | bytes 8388608
  18.1 12.2 %slice-start.6 = ((s8[29360128]{0:T(1024)(128)(4,1)}), s8[4194304]{0:T(1024)(128)(4,1)S(1)}, s32[]{:S(2)}) async-start(s8[29360128]{0:T(1024)(128)(4,1)} %bitcast.5), calls=%async_computation.6 | async-start | bytes 8388608
  18.1 12.2 %copy-start.3 = (s32[32,2]{0,1:T(2,128)S(1)}, s32[32,2]{0,1:T(2,128)}, u32[]{:S(2)}) copy-start(s32[32,2]{0,1:T(2,128)} %param.10) | copy-start | bytes 772
  18.1 12.2 %copy-start.4 = (f32[32,2]{0,1:T(2,128)S(1)}, f32[32,2]{0,1:T(2,128)}, u32[]{:S(2)}) copy-start(f32[32,2]{0,1:T(2,128)} %param.11) | copy-start | bytes 772
  18.2 30.1 %slice-start.7 = ((s8[4358144]{0:T(1024)(128)(4,1)}), s8[4194304]{0:T(1024)(128)(4,1)S(1)}, s32[]{:S(2)}) async-start(s8[4358144]{0:T(1024)(128)(4,1)} %bitcast.9), calls=%async_computation.7 | async-start | bytes 8388608
  20.7 3.3 %collective-permute-start.7 = (bf16[1,32,304]{2,1,0:T(8,128)(2,1)S(1)}, bf16[1,32,304]{2,1,0:T(8,128)(2,1)S(1)}, u32[]{:S(2)}, u32[]{:S(2)}) collective-permute-start(bf16[1,32,304]{2,1,0:T(8,128)(2,1)S(1)} %get-tuple-element.14.refs_0_), channel_id=1, source_target_pairs={{0,3},{1,2},{2,1},{3,0},{4,7},{5,6},{6,5},{7,4},{8,11},{9,10},{10,... | collective-permute-start | bytes 58376 | tf_op jit(solution)/shard_map/ppermute | solution.py:327
  22.0 3.8 %collective-permute-start.6 = (bf16[1,32,304]{2,1,0:T(8,128)(2,1)S(1)}, bf16[1,32,304]{2,1,0:T(8,128)(2,1)S(1)}, u32[]{:S(2)}, u32[]{:S(2)}) collective-permute-start(bf16[1,32,304]{2,1,0:T(8,128)(2,1)S(1)} %get-tuple-element.14.refs_0_), channel_id=1, source_target_pairs={{0,2},{1,3},{2,0},{3,1},{4,6},{5,7},{6,4},{7,5},{8,10},{9,11},{10,... | collective-permute-start | bytes 58376 | tf_op jit(solution)/shard_map/ppermute | solution.py:327
  22.5 3.3 %collective-permute-start.5 = (bf16[1,32,304]{2,1,0:T(8,128)(2,1)S(1)}, bf16[1,32,304]{2,1,0:T(8,128)(2,1)S(1)}, u32[]{:S(2)}, u32[]{:S(2)}) collective-permute-start(bf16[1,32,304]{2,1,0:T(8,128)(2,1)S(1)} %get-tuple-element.14.refs_0_), channel_id=1, source_target_pairs={{0,1},{1,0},{2,3},{3,2},{4,5},{5,4},{6,7},{7,6},{8,9},{9,8},{10,11... | collective-permute-start | bytes 58376 | tf_op jit(solution)/shard_map/ppermute | solution.py:327
  25.8 22.3 %collective-permute-start.10 = (bf16[4,32,304]{2,1,0:T(8,128)(2,1)S(1)}, bf16[4,32,304]{2,1,0:T(8,128)(2,1)S(1)}, u32[]{:S(2)}, u32[]{:S(2)}) collective-permute-start(bf16[4,32,304]{2,1,0:T(8,128)(2,1)S(1)} %shard_map.96.b0), channel_id=1, source_target_pairs={{0,12},{1,13},{2,14},{3,15},{4,8},{5,9},{6,10},{7,11},{8,4},{9,5},... | collective-permute-start | bytes 233480 | tf_op jit(solution)/shard_map/ppermute | solution.py:327
  26.2 22.0 %collective-permute-start.9 = (bf16[4,32,304]{2,1,0:T(8,128)(2,1)S(1)}, bf16[4,32,304]{2,1,0:T(8,128)(2,1)S(1)}, u32[]{:S(2)}, u32[]{:S(2)}) collective-permute-start(bf16[4,32,304]{2,1,0:T(8,128)(2,1)S(1)} %shard_map.96.b0), channel_id=1, source_target_pairs={{0,8},{1,9},{2,10},{3,11},{4,12},{5,13},{6,14},{7,15},{8,0},{9,1},... | collective-permute-start | bytes 233480 | tf_op jit(solution)/shard_map/ppermute | solution.py:327
  26.2 22.0 %collective-permute-start.8 = (bf16[4,32,304]{2,1,0:T(8,128)(2,1)S(1)}, bf16[4,32,304]{2,1,0:T(8,128)(2,1)S(1)}, u32[]{:S(2)}, u32[]{:S(2)}) collective-permute-start(bf16[4,32,304]{2,1,0:T(8,128)(2,1)S(1)} %shard_map.96.b0), channel_id=1, source_target_pairs={{0,4},{1,5},{2,6},{3,7},{4,0},{5,1},{6,2},{7,3},{8,12},{9,13},{10,... | collective-permute-start | bytes 233480 | tf_op jit(solution)/shard_map/ppermute | solution.py:327
  30.4 17.9 %slice-start.8 = ((s8[4358144]{0:T(1024)(128)(4,1)}), s8[163840]{0:T(1024)(128)(4,1)S(1)}, s32[]{:S(2)}) async-start(s8[4358144]{0:T(1024)(128)(4,1)} %bitcast.9), calls=%async_computation.8 | async-start | bytes 327680
  49.9 1.6 %collective-permute-start.11 = (bf16[16,7168]{1,0:T(8,128)(2,1)S(1)}, bf16[16,7168]{1,0:T(8,128)(2,1)S(1)}, u32[]{:S(2)}, u32[]{:S(2)}) collective-permute-start(bf16[16,7168]{1,0:T(8,128)(2,1)S(1)} %get-tuple-element.16), channel_id=1, source_target_pairs={{0,1},{1,0},{2,3},{3,2},{4,5},{5,4},{6,7},{7,6},{8,9},{9,8},{10,11... | collective-permute-start | bytes 688136 | tf_op jit(solution)/shard_map/ppermute | solution.py:327
  51.5 5.3 %collective-permute-start.12 = (bf16[8,7168]{1,0:T(8,128)(2,1)S(1)}, bf16[8,7168]{1,0:T(8,128)(2,1)S(1)}, u32[]{:S(2)}, u32[]{:S(2)}) collective-permute-start(bf16[8,7168]{1,0:T(8,128)(2,1)S(1)} %slice.42), channel_id=1, source_target_pairs={{0,2},{1,3},{2,0},{3,1},{4,6},{5,7},{6,4},{7,5},{8,10},{9,11},{10,... | collective-permute-start | bytes 344072 | tf_op jit(solution)/shard_map/ppermute | solution.py:327
  56.9 4.4 %collective-permute-start.13 = (bf16[2,7168]{1,0:T(2,128)(2,1)S(1)}, bf16[2,7168]{1,0:T(2,128)(2,1)S(1)}, u32[]{:S(2)}, u32[]{:S(2)}) collective-permute-start(bf16[2,7168]{1,0:T(2,128)(2,1)S(1)} %get-tuple-element.19), channel_id=1, source_target_pairs={{0,4},{1,5},{2,6},{3,7},{4,0},{5,1},{6,2},{7,3},{8,12},{9,13},{10,... | collective-permute-start | bytes 86024 | tf_op jit(solution)/shard_map/ppermute | solution.py:327
  57.0 5.7 %collective-permute-start.15 = (bf16[2,7168]{1,0:T(2,128)(2,1)S(1)}, bf16[2,7168]{1,0:T(2,128)(2,1)S(1)}, u32[]{:S(2)}, u32[]{:S(2)}) collective-permute-start(bf16[2,7168]{1,0:T(2,128)(2,1)S(1)} %get-tuple-element.20), channel_id=1, source_target_pairs={{0,12},{1,13},{2,14},{3,15},{4,8},{5,9},{6,10},{7,11},{8,4},{9,5},... | collective-permute-start | bytes 86024 | tf_op jit(solution)/shard_map/ppermute | solution.py:327
  58.4 5.1 %collective-permute-start.14 = (bf16[2,7168]{1,0:T(2,128)(2,1)S(1)}, bf16[2,7168]{1,0:T(2,128)(2,1)S(1)}, u32[]{:S(2)}, u32[]{:S(2)}) collective-permute-start(bf16[2,7168]{1,0:T(2,128)(2,1)S(1)} %get-tuple-element.21), channel_id=1, source_target_pairs={{0,8},{1,9},{2,10},{3,11},{4,12},{5,13},{6,14},{7,15},{8,0},{9,1},... | collective-permute-start | bytes 86024 | tf_op jit(solution)/shard_map/ppermute | solution.py:327

commit v6 on v5

--- a/solution.py
+++ b/solution.py
@@ -273,9 +273,10 @@
         held[z * near : (z + 1) * near] = blocks[...]
     for j in range(4 * near):
         joined[:, j * units : (j + 1) * units] = held[own ^ j]
-    dense_rows = dot(swap_matrix(rows, owned, False), joined[...]).astype(jnp.bfloat16)
     wide[...] = jnp.zeros_like(wide)
-    wide[:, 0:columns] = dot_t(dense_rows, down_ref[...])
+    wide[:, 0:columns] = dot_t(joined[...], down_ref[...])
+    order = swap_matrix(rows, owned, False).astype(jnp.float32)
+    wide[...] = jnp.dot(order, wide[...], precision=lax.Precision.HIGHEST, preferred_element_type=jnp.float32)
     start = own * columns
     base = jnp.minimum(start // 128 * 128, width - wide.shape[1])
     moved = pltpu.roll(wide[...], start - base, 1)

time: 64.3 us -> 64.3 us (level)
  no operation moved by 1% of the time
where the time goes in v6:
time: 64.3 us; the launch traced here: 64.2 us
  Pallas kernels  24.2 us (38%)
  waiting for transfers between devices  20.8 us (32%)
  starting transfers between devices  17.9 us (28%)
  other arithmetic  0.75 us (1%)
    ppermute x16, waiting for transfers between devices, swap(): return lax.ppermute(value, 'gx', [(i, i ^ step) for i in range(16)])  20.8 us
    ppermute x16, starting transfers between devices, swap(): return lax.ppermute(value, 'gx', [(i, i ^ step) for i in range(16)])  17.9 us
    pallas_call x1, Pallas kernels, expert_block(): pl.pallas_call(functools.partial(expert_kernel, owned, len(ready)), out_s...  17.8 us
    pallas_call x1, Pallas kernels, dense_in(): pl.pallas_call(functools.partial(dense_in_kernel, owned, chunks), out_sha...  2.51 us
    pallas_call x1, Pallas kernels, fetch(): pl.pallas_call(functools.partial(fetch_kernel, chunks, len(wholes), tied)...  2.2 us
    pallas_call x1, Pallas kernels, dense_out(): pl.pallas_call(functools.partial(dense_out_kernel, owned), out_shape=(jax...  1.64 us
  transfers between devices with their start and end apart: 16, of which 11 were waited for; matrix products, arithmetic and copies ran while one was open for 0% of the time, Pallas kernels for 31%

profile of v6, /device:TPU:0, one launch (start us, length us, event | category | flops | bytes accessed | tf_op | source)
XLA Modules:
  0.0 64.2 jit_solution(4047847851167457145)
XLA Ops:
  0.0 4.1 %collective-permute-start.1 = (bf16[2,7168]{1,0:T(2,128)(2,1)}, bf16[2,7168]{1,0:T(2,128)(2,1)S(1)}, u32[]{:S(2)}, u32[]{:S(2)}) collective-permute-start(bf16[2,7168]{1,0:T(2,128)(2,1)} %refs_1_.4), channel_id=1, source_target_pairs={{0,8},{1,9},{2,10},{3,11},{4,12},{5,13},{6,14},{7,15},{8,0},{9,1},... | collective-permute-start | bytes 86024 | tf_op jit(solution)/shard_map/ppermute | solution.py:328
  4.1 1.6 %collective-permute-start = (bf16[2,7168]{1,0:T(2,128)(2,1)}, bf16[2,7168]{1,0:T(2,128)(2,1)S(1)}, u32[]{:S(2)}, u32[]{:S(2)}) collective-permute-start(bf16[2,7168]{1,0:T(2,128)(2,1)} %refs_1_.4), channel_id=1, source_target_pairs={{0,4},{1,5},{2,6},{3,7},{4,0},{5,1},{6,2},{7,3},{8,12},{9,13},{10,... | collective-permute-start | bytes 86024 | tf_op jit(solution)/shard_map/ppermute | solution.py:328
  5.7 2.2 %shard_map.91 = (bf16[1024,2048]{1,0:T(8,128)(2,1)S(1)}, f32[8,128]{1,0:T(8,128)S(1)}) custom-call(bf16[7168,2048]{1,0:T(8,128)(2,1)} %gate_ref.3, bf16[7168,2048]{1,0:T(8,128)(2,1)} %refs_1_.5), custom_call_target="tpu_custom_call" | custom-call | bytes 4194304 | tf_op jit(solution)/shard_map/pallas_call | solution.py:100
  7.9 0.3 collective-permute-done.refs_2_
  8.2 3.4 %collective-permute-done.2.refs_4_ = bf16[2,7168]{1,0:T(2,128)(2,1)S(1)} collective-permute-done((bf16[2,7168]{1,0:T(2,128)(2,1)}, bf16[2,7168]{1,0:T(2,128)(2,1)S(1)}, u32[]{:S(2)}, u32[]{:S(2)}) %collective-permute-start.2) | collective-permute-done | bytes 28704 | tf_op jit(solution)/shard_map/ppermute | solution.py:328
  11.6 0.1 shard_map.92.refs_1_
  11.6 1.6 %collective-permute-start.3 = (bf16[8,7168]{1,0:T(8,128)(2,1)S(1)}, bf16[8,7168]{1,0:T(8,128)(2,1)S(1)}, u32[]{:S(2)}, u32[]{:S(2)}) collective-permute-start(bf16[8,7168]{1,0:T(8,128)(2,1)S(1)} %shard_map.92.refs_1_), channel_id=1, source_target_pairs={{0,2},{1,3},{2,0},{3,1},{4,6},{5,7},{6,4},{7,5},{8,10},{9,11},{10,... | collective-permute-start | bytes 344072 | tf_op jit(solution)/shard_map/ppermute | solution.py:328
  13.2 3.3 %collective-permute-done.3.refs_2_ = bf16[8,7168]{1,0:T(8,128)(2,1)S(1)} collective-permute-done((bf16[8,7168]{1,0:T(8,128)(2,1)S(1)}, bf16[8,7168]{1,0:T(8,128)(2,1)S(1)}, u32[]{:S(2)}, u32[]{:S(2)}) %collective-permute-start.3) | collective-permute-done | bytes 114720 | tf_op jit(solution)/shard_map/ppermute | solution.py:328
  16.5 0.1 collective-permute-start.4
  16.6 1.5 %collective-permute-done.4.other_ref = bf16[16,7168]{1,0:T(8,128)(2,1)S(1)} collective-permute-done((bf16[16,7168]{1,0:T(8,128)(2,1)S(1)}, bf16[16,7168]{1,0:T(8,128)(2,1)S(1)}, u32[]{:S(2)}, u32[]{:S(2)}) %collective-permute-start.4) | collective-permute-done | bytes 229408 | tf_op jit(solution)/shard_map/ppermute | solution.py:328
  18.2 2.5 %shard_map.94 = (bf16[1,32,304]{2,1,0:T(8,128)(2,1)S(1)}, bf16[32,7168]{1,0:T(8,128)(2,1)S(1)}) custom-call(bf16[16,7168]{1,0:T(8,128)(2,1)S(1)} %shard_map.93.mine_ref, bf16[16,7168]{1,0:T(8,128)(2,1)S(1)} %collective-permute-done.4.other_ref, bf16[304,7168]{1,0:T(8,128)(2,1)S(1)} %bitcast.7, bf16[304,7168]{1,0:T(8,128)(2,1)S(1)} %bitcast.8, ...), custom_call_target="tpu_custom_call" | custom-call | flops 278921216 | bytes 8716288 | tf_op jit(solution)/shard_map/pallas_call | solution.py:154
  20.7 1.3 %collective-permute-start.7 = (bf16[1,32,304]{2,1,0:T(8,128)(2,1)S(1)}, bf16[1,32,304]{2,1,0:T(8,128)(2,1)S(1)}, u32[]{:S(2)}, u32[]{:S(2)}) collective-permute-start(bf16[1,32,304]{2,1,0:T(8,128)(2,1)S(1)} %get-tuple-element.14.refs_0_), channel_id=1, source_target_pairs={{0,3},{1,2},{2,1},{3,0},{4,7},{5,6},{6,5},{7,4},{8,11},{9,10},{10,... | collective-permute-start | bytes 58376 | tf_op jit(solution)/shard_map/ppermute | solution.py:328
  22.0 0.5 collective-permute-start.6
  22.5 0.1 collective-permute-start.5
  22.6 1.4 %collective-permute-done.7.refs_3_ = bf16[1,32,304]{2,1,0:T(8,128)(2,1)S(1)} collective-permute-done((bf16[1,32,304]{2,1,0:T(8,128)(2,1)S(1)}, bf16[1,32,304]{2,1,0:T(8,128)(2,1)S(1)}, u32[]{:S(2)}, u32[]{:S(2)}) %collective-permute-start.7) | collective-permute-done | bytes 19488 | tf_op jit(solution)/shard_map/ppermute | solution.py:328
  24.0 1.8 %collective-permute-done.6.refs_2_ = bf16[1,32,304]{2,1,0:T(8,128)(2,1)S(1)} collective-permute-done((bf16[1,32,304]{2,1,0:T(8,128)(2,1)S(1)}, bf16[1,32,304]{2,1,0:T(8,128)(2,1)S(1)}, u32[]{:S(2)}, u32[]{:S(2)}) %collective-permute-start.6) | collective-permute-done | bytes 19488 | tf_op jit(solution)/shard_map/ppermute | solution.py:328
  25.8 0.4 collective-permute-start.10
  26.2 4.1 %collective-permute-start.8 = (bf16[4,32,304]{2,1,0:T(8,128)(2,1)S(1)}, bf16[4,32,304]{2,1,0:T(8,128)(2,1)S(1)}, u32[]{:S(2)}, u32[]{:S(2)}) collective-permute-start(bf16[4,32,304]{2,1,0:T(8,128)(2,1)S(1)} %shard_map.96.b0), channel_id=1, source_target_pairs={{0,4},{1,5},{2,6},{3,7},{4,0},{5,1},{6,2},{7,3},{8,12},{9,13},{10,... | collective-permute-start | bytes 233480 | tf_op jit(solution)/shard_map/ppermute | solution.py:328
  30.4 17.8 %shard_map.95.part_ref = f32[32,7168]{1,0:T(8,128)S(1)} custom-call(bf16[32,7168]{1,0:T(8,128)(2,1)S(1)} %get-tuple-element.12.x_ref, s32[2,32]{1,0:T(2,128)S(1)} %bitcast.12, f32[2,32]{1,0:T(2,128)S(1)} %bitcast.13, bf16[7168,2048]{1,0:T(8,128)(2,1)S(1)} %bitcast.6, bf16[1024,2048]{1,0:T(8,128)(2,1)S(1)} %get-tuple-element.13.refs_0_, ...), custom_call_target="tpu_custom_call" | custom-call | flops 2818572288 | bytes 58720256 | tf_op jit(solution)/shard_map/pallas_call | solution.py:247
  48.3 1.6 %shard_map.97 = (f32[16,7168]{1,0:T(8,128)S(1)}, bf16[16,7168]{1,0:T(8,128)(2,1)S(1)}) custom-call(f32[32,7168]{1,0:T(8,128)S(1)} %shard_map.95.part_ref, bf16[4,32,304]{2,1,0:T(8,128)(2,1)S(1)} %shard_map.96.b0, bf16[4,32,304]{2,1,0:T(8,128)(2,1)S(1)} %collective-permute-done.8.b1, bf16[4,32,304]{2,1,0:T(8,128)(2,1)S(1)} %collective-permute-done.9.b2, ...), custom_call_target="tpu_custom_call" | custom-call | flops 139460608 | bytes 4358144 | tf_op jit(solution)/shard_map/pallas_call | solution.py:295
  49.9 0.1 collective-permute-start.11
  50.0 1.5 %collective-permute-done.11 = bf16[16,7168]{1,0:T(8,128)(2,1)S(1)} collective-permute-done((bf16[16,7168]{1,0:T(8,128)(2,1)S(1)}, bf16[16,7168]{1,0:T(8,128)(2,1)S(1)}, u32[]{:S(2)}, u32[]{:S(2)}) %collective-permute-start.11) | collective-permute-done | bytes 229408 | tf_op jit(solution)/shard_map/ppermute | solution.py:328
  51.5 0.6 collective-permute-start.12
  52.1 4.7 %collective-permute-done.12 = bf16[8,7168]{1,0:T(8,128)(2,1)S(1)} collective-permute-done((bf16[8,7168]{1,0:T(8,128)(2,1)S(1)}, bf16[8,7168]{1,0:T(8,128)(2,1)S(1)}, u32[]{:S(2)}, u32[]{:S(2)}) %collective-permute-start.12) | collective-permute-done | bytes 114720 | tf_op jit(solution)/shard_map/ppermute | solution.py:328
  56.8 0.1 fusion.5
  56.9 0.1 collective-permute-start.13
  57.0 1.4 %collective-permute-start.15 = (bf16[2,7168]{1,0:T(2,128)(2,1)S(1)}, bf16[2,7168]{1,0:T(2,128)(2,1)S(1)}, u32[]{:S(2)}, u32[]{:S(2)}) collective-permute-start(bf16[2,7168]{1,0:T(2,128)(2,1)S(1)} %get-tuple-element.20), channel_id=1, source_target_pairs={{0,12},{1,13},{2,14},{3,15},{4,8},{5,9},{6,10},{7,11},{8,4},{9,5},... | collective-permute-start | bytes 86024 | tf_op jit(solution)/shard_map/ppermute | solution.py:328
  58.4 2.0 %collective-permute-start.14 = (bf16[2,7168]{1,0:T(2,128)(2,1)S(1)}, bf16[2,7168]{1,0:T(2,128)(2,1)S(1)}, u32[]{:S(2)}, u32[]{:S(2)}) collective-permute-start(bf16[2,7168]{1,0:T(2,128)(2,1)S(1)} %get-tuple-element.21), channel_id=1, source_target_pairs={{0,8},{1,9},{2,10},{3,11},{4,12},{5,13},{6,14},{7,15},{8,0},{9,1},... | collective-permute-start | bytes 86024 | tf_op jit(solution)/shard_map/ppermute | solution.py:328
  60.4 0.9 %collective-permute-done.13 = bf16[2,7168]{1,0:T(2,128)(2,1)S(1)} collective-permute-done((bf16[2,7168]{1,0:T(2,128)(2,1)S(1)}, bf16[2,7168]{1,0:T(2,128)(2,1)S(1)}, u32[]{:S(2)}, u32[]{:S(2)}) %collective-permute-start.13) | collective-permute-done | bytes 28704 | tf_op jit(solution)/shard_map/ppermute | solution.py:328
  61.3 1.4 %collective-permute-done.15 = bf16[2,7168]{1,0:T(2,128)(2,1)S(1)} collective-permute-done((bf16[2,7168]{1,0:T(2,128)(2,1)S(1)}, bf16[2,7168]{1,0:T(2,128)(2,1)S(1)}, u32[]{:S(2)}, u32[]{:S(2)}) %collective-permute-start.15) | collective-permute-done | bytes 28704 | tf_op jit(solution)/shard_map/ppermute | solution.py:328
  62.7 0.8 %collective-permute-done.14 = bf16[2,7168]{1,0:T(2,128)(2,1)S(1)} collective-permute-done((bf16[2,7168]{1,0:T(2,128)(2,1)S(1)}, bf16[2,7168]{1,0:T(2,128)(2,1)S(1)}, u32[]{:S(2)}, u32[]{:S(2)}) %collective-permute-start.14) | collective-permute-done | bytes 28704 | tf_op jit(solution)/shard_map/ppermute | solution.py:328
  63.5 0.7 %fusion.3 = bf16[2,7168]{1,0:T(2,128)(2,1)} fusion(bf16[2,7168]{1,0:T(2,128)(2,1)S(1)} %collective-permute-done.15, bf16[2,7168]{1,0:T(2,128)(2,1)S(1)} %collective-permute-done.14, bf16[2,7168]{1,0:T(2,128)(2,1)S(1)} %collective-permute-done.13, f32[8,7168]{1,0:T(8,128)S(1)} %get-tuple-element.18, bf16[2,7168]{1,0:T(2,128)(2,1)S(1)} %copy-done.2), kind=kLoop, calls=%fused_computation.7 | loop fusion | flops 129024 | bytes 200704 | tf_op jit(solution)/shard_map/convert_element_type | solution.py:368
  (42 shorter events, 0.2 us)
Async XLA Ops:
  0.0 11.6 %copy-start.2 = (bf16[2,7168]{1,0:T(2,128)(2,1)S(1)}, bf16[2,7168]{1,0:T(2,128)(2,1)}, u32[]{:S(2)}) copy-start(bf16[2,7168]{1,0:T(2,128)(2,1)} %refs_1_.4) | copy-start | bytes 86020
  0.0 18.1 %copy-start.1 = (bf16[7168,304]{0,1:T(8,128)(2,1)S(1)}, bf16[7168,304]{0,1:T(8,128)(2,1)}, u32[]{:S(2)}) copy-start(bf16[7168,304]{0,1:T(8,128)(2,1)} %param.13) | copy-start | bytes 13074436
  0.0 18.1 %copy-start = (bf16[7168,304]{0,1:T(8,128)(2,1)S(1)}, bf16[7168,304]{0,1:T(8,128)(2,1)}, u32[]{:S(2)}) copy-start(bf16[7168,304]{0,1:T(8,128)(2,1)} %param.12) | copy-start | bytes 13074436
  0.0 7.9 %collective-permute-start.1 = (bf16[2,7168]{1,0:T(2,128)(2,1)}, bf16[2,7168]{1,0:T(2,128)(2,1)S(1)}, u32[]{:S(2)}, u32[]{:S(2)}) collective-permute-start(bf16[2,7168]{1,0:T(2,128)(2,1)} %refs_1_.4), channel_id=1, source_target_pairs={{0,8},{1,9},{2,10},{3,11},{4,12},{5,13},{6,14},{7,15},{8,0},{9,1},... | collective-permute-start | bytes 86024 | tf_op jit(solution)/shard_map/ppermute | solution.py:328
  4.1 4.1 %collective-permute-start = (bf16[2,7168]{1,0:T(2,128)(2,1)}, bf16[2,7168]{1,0:T(2,128)(2,1)S(1)}, u32[]{:S(2)}, u32[]{:S(2)}) collective-permute-start(bf16[2,7168]{1,0:T(2,128)(2,1)} %refs_1_.4), channel_id=1, source_target_pairs={{0,4},{1,5},{2,6},{3,7},{4,0},{5,1},{6,2},{7,3},{8,12},{9,13},{10,... | collective-permute-start | bytes 86024 | tf_op jit(solution)/shard_map/ppermute | solution.py:328
  5.7 5.9 %collective-permute-start.2 = (bf16[2,7168]{1,0:T(2,128)(2,1)}, bf16[2,7168]{1,0:T(2,128)(2,1)S(1)}, u32[]{:S(2)}, u32[]{:S(2)}) collective-permute-start(bf16[2,7168]{1,0:T(2,128)(2,1)} %refs_1_.4), channel_id=1, source_target_pairs={{0,12},{1,13},{2,14},{3,15},{4,8},{5,9},{6,10},{7,11},{8,4},{9,5},... | collective-permute-start | bytes 86024 | tf_op jit(solution)/shard_map/ppermute | solution.py:328
  11.6 4.9 %collective-permute-start.3 = (bf16[8,7168]{1,0:T(8,128)(2,1)S(1)}, bf16[8,7168]{1,0:T(8,128)(2,1)S(1)}, u32[]{:S(2)}, u32[]{:S(2)}) collective-permute-start(bf16[8,7168]{1,0:T(8,128)(2,1)S(1)} %shard_map.92.refs_1_), channel_id=1, source_target_pairs={{0,2},{1,3},{2,0},{3,1},{4,6},{5,7},{6,4},{7,5},{8,10},{9,11},{10,... | collective-permute-start | bytes 344072 | tf_op jit(solution)/shard_map/ppermute | solution.py:328
  16.5 1.6 %collective-permute-start.4 = (bf16[16,7168]{1,0:T(8,128)(2,1)S(1)}, bf16[16,7168]{1,0:T(8,128)(2,1)S(1)}, u32[]{:S(2)}, u32[]{:S(2)}) collective-permute-start(bf16[16,7168]{1,0:T(8,128)(2,1)S(1)} %shard_map.93.mine_ref), channel_id=1, source_target_pairs={{0,1},{1,0},{2,3},{3,2},{4,5},{5,4},{6,7},{7,6},{8,9},{9,8},{10,11... | collective-permute-start | bytes 688136 | tf_op jit(solution)/shard_map/ppermute | solution.py:328
  18.1 12.2 %slice-start = ((s8[29360128]{0:T(1024)(128)(4,1)}), s8[4194304]{0:T(1024)(128)(4,1)S(1)}, s32[]{:S(2)}) async-start(s8[29360128]{0:T(1024)(128)(4,1)} %bitcast.5), calls=%async_computation | async-start | bytes 8388608
  18.1 12.2 %slice-start.1 = ((s8[29360128]{0:T(1024)(128)(4,1)}), s8[4194304]{0:T(1024)(128)(4,1)S(1)}, s32[]{:S(2)}) async-start(s8[29360128]{0:T(1024)(128)(4,1)} %bitcast.5), calls=%async_computation.1 | async-start | bytes 8388608
  18.1 12.2 %slice-start.2 = ((s8[29360128]{0:T(1024)(128)(4,1)}), s8[4194304]{0:T(1024)(128)(4,1)S(1)}, s32[]{:S(2)}) async-start(s8[29360128]{0:T(1024)(128)(4,1)} %bitcast.5), calls=%async_computation.2 | async-start | bytes 8388608
  18.1 12.2 %slice-start.3 = ((s8[29360128]{0:T(1024)(128)(4,1)}), s8[4194304]{0:T(1024)(128)(4,1)S(1)}, s32[]{:S(2)}) async-start(s8[29360128]{0:T(1024)(128)(4,1)} %bitcast.5), calls=%async_computation.3 | async-start | bytes 8388608
  18.1 12.2 %slice-start.4 = ((s8[29360128]{0:T(1024)(128)(4,1)}), s8[4194304]{0:T(1024)(128)(4,1)S(1)}, s32[]{:S(2)}) async-start(s8[29360128]{0:T(1024)(128)(4,1)} %bitcast.5), calls=%async_computation.4 | async-start | bytes 8388608
  18.1 12.2 %slice-start.5 = ((s8[29360128]{0:T(1024)(128)(4,1)}), s8[4194304]{0:T(1024)(128)(4,1)S(1)}, s32[]{:S(2)}) async-start(s8[29360128]{0:T(1024)(128)(4,1)} %bitcast.5), calls=%async_computation.5 | async-start | bytes 8388608
  18.1 12.2 %slice-start.6 = ((s8[29360128]{0:T(1024)(128)(4,1)}), s8[4194304]{0:T(1024)(128)(4,1)S(1)}, s32[]{:S(2)}) async-start(s8[29360128]{0:T(1024)(128)(4,1)} %bitcast.5), calls=%async_computation.6 | async-start | bytes 8388608
  18.1 12.2 %copy-start.3 = (s32[32,2]{0,1:T(2,128)S(1)}, s32[32,2]{0,1:T(2,128)}, u32[]{:S(2)}) copy-start(s32[32,2]{0,1:T(2,128)} %param.10) | copy-start | bytes 772
  18.1 12.2 %copy-start.4 = (f32[32,2]{0,1:T(2,128)S(1)}, f32[32,2]{0,1:T(2,128)}, u32[]{:S(2)}) copy-start(f32[32,2]{0,1:T(2,128)} %param.11) | copy-start | bytes 772
  18.2 30.1 %slice-start.7 = ((s8[4358144]{0:T(1024)(128)(4,1)}), s8[4194304]{0:T(1024)(128)(4,1)S(1)}, s32[]{:S(2)}) async-start(s8[4358144]{0:T(1024)(128)(4,1)} %bitcast.9), calls=%async_computation.7 | async-start | bytes 8388608
  20.7 3.3 %collective-permute-start.7 = (bf16[1,32,304]{2,1,0:T(8,128)(2,1)S(1)}, bf16[1,32,304]{2,1,0:T(8,128)(2,1)S(1)}, u32[]{:S(2)}, u32[]{:S(2)}) collective-permute-start(bf16[1,32,304]{2,1,0:T(8,128)(2,1)S(1)} %get-tuple-element.14.refs_0_), channel_id=1, source_target_pairs={{0,3},{1,2},{2,1},{3,0},{4,7},{5,6},{6,5},{7,4},{8,11},{9,10},{10,... | collective-permute-start | bytes 58376 | tf_op jit(solution)/shard_map/ppermute | solution.py:328
  22.0 3.8 %collective-permute-start.6 = (bf16[1,32,304]{2,1,0:T(8,128)(2,1)S(1)}, bf16[1,32,304]{2,1,0:T(8,128)(2,1)S(1)}, u32[]{:S(2)}, u32[]{:S(2)}) collective-permute-start(bf16[1,32,304]{2,1,0:T(8,128)(2,1)S(1)} %get-tuple-element.14.refs_0_), channel_id=1, source_target_pairs={{0,2},{1,3},{2,0},{3,1},{4,6},{5,7},{6,4},{7,5},{8,10},{9,11},{10,... | collective-permute-start | bytes 58376 | tf_op jit(solution)/shard_map/ppermute | solution.py:328
  22.5 3.3 %collective-permute-start.5 = (bf16[1,32,304]{2,1,0:T(8,128)(2,1)S(1)}, bf16[1,32,304]{2,1,0:T(8,128)(2,1)S(1)}, u32[]{:S(2)}, u32[]{:S(2)}) collective-permute-start(bf16[1,32,304]{2,1,0:T(8,128)(2,1)S(1)} %get-tuple-element.14.refs_0_), channel_id=1, source_target_pairs={{0,1},{1,0},{2,3},{3,2},{4,5},{5,4},{6,7},{7,6},{8,9},{9,8},{10,11... | collective-permute-start | bytes 58376 | tf_op jit(solution)/shard_map/ppermute | solution.py:328
  25.8 22.3 %collective-permute-start.10 = (bf16[4,32,304]{2,1,0:T(8,128)(2,1)S(1)}, bf16[4,32,304]{2,1,0:T(8,128)(2,1)S(1)}, u32[]{:S(2)}, u32[]{:S(2)}) collective-permute-start(bf16[4,32,304]{2,1,0:T(8,128)(2,1)S(1)} %shard_map.96.b0), channel_id=1, source_target_pairs={{0,12},{1,13},{2,14},{3,15},{4,8},{5,9},{6,10},{7,11},{8,4},{9,5},... | collective-permute-start | bytes 233480 | tf_op jit(solution)/shard_map/ppermute | solution.py:328
  26.2 22.0 %collective-permute-start.9 = (bf16[4,32,304]{2,1,0:T(8,128)(2,1)S(1)}, bf16[4,32,304]{2,1,0:T(8,128)(2,1)S(1)}, u32[]{:S(2)}, u32[]{:S(2)}) collective-permute-start(bf16[4,32,304]{2,1,0:T(8,128)(2,1)S(1)} %shard_map.96.b0), channel_id=1, source_target_pairs={{0,8},{1,9},{2,10},{3,11},{4,12},{5,13},{6,14},{7,15},{8,0},{9,1},... | collective-permute-start | bytes 233480 | tf_op jit(solution)/shard_map/ppermute | solution.py:328
  26.2 22.0 %collective-permute-start.8 = (bf16[4,32,304]{2,1,0:T(8,128)(2,1)S(1)}, bf16[4,32,304]{2,1,0:T(8,128)(2,1)S(1)}, u32[]{:S(2)}, u32[]{:S(2)}) collective-permute-start(bf16[4,32,304]{2,1,0:T(8,128)(2,1)S(1)} %shard_map.96.b0), channel_id=1, source_target_pairs={{0,4},{1,5},{2,6},{3,7},{4,0},{5,1},{6,2},{7,3},{8,12},{9,13},{10,... | collective-permute-start | bytes 233480 | tf_op jit(solution)/shard_map/ppermute | solution.py:328
  30.4 17.9 %slice-start.8 = ((s8[4358144]{0:T(1024)(128)(4,1)}), s8[163840]{0:T(1024)(128)(4,1)S(1)}, s32[]{:S(2)}) async-start(s8[4358144]{0:T(1024)(128)(4,1)} %bitcast.9), calls=%async_computation.8 | async-start | bytes 327680
  49.9 1.6 %collective-permute-start.11 = (bf16[16,7168]{1,0:T(8,128)(2,1)S(1)}, bf16[16,7168]{1,0:T(8,128)(2,1)S(1)}, u32[]{:S(2)}, u32[]{:S(2)}) collective-permute-start(bf16[16,7168]{1,0:T(8,128)(2,1)S(1)} %get-tuple-element.16), channel_id=1, source_target_pairs={{0,1},{1,0},{2,3},{3,2},{4,5},{5,4},{6,7},{7,6},{8,9},{9,8},{10,11... | collective-permute-start | bytes 688136 | tf_op jit(solution)/shard_map/ppermute | solution.py:328
  51.5 5.3 %collective-permute-start.12 = (bf16[8,7168]{1,0:T(8,128)(2,1)S(1)}, bf16[8,7168]{1,0:T(8,128)(2,1)S(1)}, u32[]{:S(2)}, u32[]{:S(2)}) collective-permute-start(bf16[8,7168]{1,0:T(8,128)(2,1)S(1)} %slice.42), channel_id=1, source_target_pairs={{0,2},{1,3},{2,0},{3,1},{4,6},{5,7},{6,4},{7,5},{8,10},{9,11},{10,... | collective-permute-start | bytes 344072 | tf_op jit(solution)/shard_map/ppermute | solution.py:328
  56.9 4.4 %collective-permute-start.13 = (bf16[2,7168]{1,0:T(2,128)(2,1)S(1)}, bf16[2,7168]{1,0:T(2,128)(2,1)S(1)}, u32[]{:S(2)}, u32[]{:S(2)}) collective-permute-start(bf16[2,7168]{1,0:T(2,128)(2,1)S(1)} %get-tuple-element.19), channel_id=1, source_target_pairs={{0,4},{1,5},{2,6},{3,7},{4,0},{5,1},{6,2},{7,3},{8,12},{9,13},{10,... | collective-permute-start | bytes 86024 | tf_op jit(solution)/shard_map/ppermute | solution.py:328
  57.0 5.7 %collective-permute-start.15 = (bf16[2,7168]{1,0:T(2,128)(2,1)S(1)}, bf16[2,7168]{1,0:T(2,128)(2,1)S(1)}, u32[]{:S(2)}, u32[]{:S(2)}) collective-permute-start(bf16[2,7168]{1,0:T(2,128)(2,1)S(1)} %get-tuple-element.20), channel_id=1, source_target_pairs={{0,12},{1,13},{2,14},{3,15},{4,8},{5,9},{6,10},{7,11},{8,4},{9,5},... | collective-permute-start | bytes 86024 | tf_op jit(solution)/shard_map/ppermute | solution.py:328
  58.4 5.1 %collective-permute-start.14 = (bf16[2,7168]{1,0:T(2,128)(2,1)S(1)}, bf16[2,7168]{1,0:T(2,128)(2,1)S(1)}, u32[]{:S(2)}, u32[]{:S(2)}) collective-permute-start(bf16[2,7168]{1,0:T(2,128)(2,1)S(1)} %get-tuple-element.21), channel_id=1, source_target_pairs={{0,8},{1,9},{2,10},{3,11},{4,12},{5,13},{6,14},{7,15},{8,0},{9,1},... | collective-permute-start | bytes 86024 | tf_op jit(solution)/shard_map/ppermute | solution.py:328
